TPU v7x, 32 devices: a whole 2x2x4 slice. The times are simulated.
32 devices in a mesh: dp: 4 (over x, core), fsdp: 8 (over z, y).
Axes of the slice: x: 2, y: 2, z: 4, core: 2. Of those that a mesh axis runs over, the one named last changes fastest.
Arguments:
- tokens: bfloat16 [8192, 2048], P(('dp', 'fsdp')), may hold values from -6 to 6
- out_grad: bfloat16 [8192, 2048], P(('dp', 'fsdp')), may hold values from -6 to 6
- block_first: int32 [128], P(('dp', 'fsdp')), may hold values from 0 to 1, as said below
- block_live: int32 [128], P(('dp', 'fsdp')), may hold values from 0 to 64, as said below
- norm1_gain: bfloat16 [2048], P(('dp', 'fsdp')), may hold values from 0.5 to 1.5
- w_proj: bfloat16 [2048, 12288], P(('dp', 'fsdp')), may hold values from -0.125 to 0.125
- w_decay: bfloat16 [2048, 32], P(('dp', 'fsdp')), may hold values from -0.125 to 0.125
- conv_w: bfloat16 [4, 8192], P(None, ('dp', 'fsdp')), may hold values from -3 to 3
- w_out: bfloat16 [4096, 2048], P(('dp', 'fsdp')), may hold values from -0.1875 to 0.1875
- a_log: float32 [16], replicated, may hold values from 0 to 2.7
- dt_bias: float32 [16], replicated, may hold values from -6.5 to -2
- head_gain: float32 [256], replicated, may hold values from 0.5 to 1.5
- norm2_gain: bfloat16 [2048], P(('dp', 'fsdp')), may hold values from 0.5 to 1.5
- w_gate_up: bfloat16 [2048, 11264], P(('dp', 'fsdp')), may hold values from -0.125 to 0.125
- w_down: bfloat16 [5632, 2048], P(('dp', 'fsdp')), may hold values from -0.15625 to 0.15625
Outputs:
- layer_out: bfloat16 [8192, 2048], P(('dp', 'fsdp'))
- tokens_grad: bfloat16 [8192, 2048], P(('dp', 'fsdp'))
- norm1_gain_grad: float32 [2048], P(('dp', 'fsdp'))
- w_proj_grad: float32 [2048, 12288], P(('dp', 'fsdp'))
- w_decay_grad: float32 [2048, 32], P(('dp', 'fsdp'))
- conv_w_grad: float32 [4, 8192], P(None, ('dp', 'fsdp'))
- w_out_grad: float32 [4096, 2048], P(('dp', 'fsdp'))
- a_log_grad: float32 [16], replicated
- dt_bias_grad: float32 [16], replicated
- head_gain_grad: float32 [256], replicated
- norm2_gain_grad: float32 [2048], P(('dp', 'fsdp'))
- w_gate_up_grad: float32 [2048, 11264], P(('dp', 'fsdp'))
- w_down_grad: float32 [5632, 2048], P(('dp', 'fsdp'))
Inputs may be any that keep to these rules, and one draw needn't show every extreme that they name: `block_first`: every device's first block begins a bucket; a bucket spans a power of two of blocks, at most 4, and begins at a multiple of its span within its device's blocks. `block_live`: A bucket holds one sequence whose length is more than half the bucket's rows; its live rows fill the bucket's blocks from the first one on.
All inputs are finite; a program needn't handle non-finite values.
Results may differ from a plain program's by a relative error of at most 0.012.
Values may be sent and summed in bfloat16 or wider, within the bound.
A program may use at most 640 MiB of HBM per device.

v0:
```python
from functools import partial

import jax
import jax.numpy as jnp
from jax import lax
from jax.sharding import PartitionSpec as P

HEADS = 16
DK = 128
DV = 256
CONV = 4
BLOCK = 64


EPS = 1e-06
HIGH = lax.Precision.HIGHEST


def rms_scale(values_in, gain_vec):
    return (
        values_in
        * lax.rsqrt(jnp.mean(values_in * values_in, axis=-1, keepdims=True) + EPS)
        * gain_vec
    )


def unit_rows(values_in):
    return values_in * lax.rsqrt(jnp.sum(values_in * values_in, axis=-1, keepdims=True) + EPS)


def tall_dot(left, right):
    return lax.dot_general(
        left, right, (((0,), (0,)), ((), ())), preferred_element_type=jnp.float32
    )


def back_dot(left, right):
    return lax.dot_general(
        left, right, (((1,), (1,)), ((), ())), preferred_element_type=jnp.float32
    )


def row_layout(block_first, block_live, row_total):
    block_index = jnp.arange(block_first.shape[0], dtype=jnp.int32)
    bucket_starts = lax.cummax(jnp.where(block_first > 0, block_index * BLOCK, 0), axis=0)
    row_index = jnp.arange(row_total, dtype=jnp.int32)
    position = row_index - jnp.repeat(bucket_starts, BLOCK)
    live_mask = (row_index % BLOCK < jnp.repeat(block_live, BLOCK)).astype(jnp.float32)
    return (position, live_mask)


def short_conv(raw_input, conv_weight, position):
    running = raw_input * conv_weight[CONV - 1]
    for lag_steps in range(1, CONV):
        shifted = jnp.concatenate(
            [jnp.zeros((lag_steps, raw_input.shape[1]), raw_input.dtype), raw_input[:-lag_steps]],
            axis=0,
        )
        keep_rows = (position >= lag_steps).astype(raw_input.dtype)[:, None]
        running = running + shifted * keep_rows * conv_weight[CONV - 1 - lag_steps]
    return jax.nn.silu(running)


def prepare(projected, decay_raw, conv_weight, a_log, dt_bias, position):
    row_total = projected.shape[0]
    key_width = HEADS * DK
    conv_width = 2 * key_width + HEADS * DV
    conv_out = short_conv(projected[:, :conv_width], conv_weight, position)
    query = unit_rows(conv_out[:, :key_width].reshape(row_total, HEADS, DK)) * DK ** (-0.5)
    key_vec = unit_rows(conv_out[:, key_width : 2 * key_width].reshape(row_total, HEADS, DK))
    value_vec = conv_out[:, 2 * key_width :].reshape(row_total, HEADS, DV)
    beta_gate = jax.nn.sigmoid(decay_raw[:, HEADS:])
    log_decay = -jnp.exp(a_log) * jax.nn.softplus(decay_raw[:, :HEADS] + dt_bias)
    return (query, key_vec, value_vec, beta_gate, log_decay, projected[:, conv_width:])


def block_rule(query, key_vec, value_vec, beta_gate, log_decay, fresh_blocks):
    row_total = query.shape[0]
    block_total = row_total // BLOCK

    def to_blocks(array):
        return array.reshape((block_total, BLOCK) + array.shape[1:]).swapaxes(1, 2)

    query_blocks = to_blocks(query)
    key_blocks = to_blocks(key_vec)
    value_blocks = to_blocks(value_vec)
    beta_blocks = to_blocks(beta_gate)
    cum_decay = jnp.cumsum(to_blocks(log_decay), axis=-1)
    row_pos = jnp.arange(BLOCK)
    lower_eq = row_pos[:, None] >= row_pos[None, :]
    lower_strict = row_pos[:, None] > row_pos[None, :]
    decay_gap = cum_decay[..., :, None] - cum_decay[..., None, :]
    decay_pair = jnp.where(lower_eq, jnp.exp(jnp.where(lower_eq, decay_gap, 0.0)), 0.0)
    key_pair = jnp.einsum("nhik,nhjk->nhij", key_blocks, key_blocks, precision=HIGH)
    query_pair = jnp.einsum("nhik,nhjk->nhij", query_blocks, key_blocks, precision=HIGH)
    system = jnp.eye(BLOCK, dtype=query.dtype) + beta_blocks[..., :, None] * jnp.where(
        lower_strict, key_pair * decay_pair, 0.0
    )
    attention = query_pair * decay_pair

    def step_fn(carry_state, inputs):
        (
            query_part,
            key_part,
            value_part,
            beta_part,
            decay_part,
            attend_part,
            system_part,
            fresh_part,
        ) = inputs
        carry_state = carry_state * (1.0 - fresh_part)
        start_decay = jnp.exp(decay_part)[..., None]
        predicted = jnp.einsum("hck,hvk->hcv", key_part, carry_state, precision=HIGH)
        right_side = beta_part[..., None] * (value_part - start_decay * predicted)
        new_values = jax.scipy.linalg.solve_triangular(
            system_part, right_side, lower=True, unit_diagonal=True
        )
        outputs = start_decay * jnp.einsum(
            "hck,hvk->hcv", query_part, carry_state, precision=HIGH
        ) + jnp.einsum("hij,hjv->hiv", attend_part, new_values, precision=HIGH)
        tail_decay = jnp.exp(decay_part[:, -1:] - decay_part)[..., None]
        carry_state = jnp.exp(decay_part[:, -1])[:, None, None] * carry_state + jnp.einsum(
            "hcv,hck->hvk", new_values * tail_decay, key_part, precision=HIGH
        )
        return (carry_state, outputs)

    initial = jnp.zeros((HEADS, DV, DK), query.dtype)
    _, outputs = lax.scan(
        step_fn,
        initial,
        (
            query_blocks,
            key_blocks,
            value_blocks,
            beta_blocks,
            cum_decay,
            attention,
            system,
            fresh_blocks,
        ),
    )
    return outputs.swapaxes(1, 2).reshape(row_total, HEADS, DV)


def mixer_core(projected, decay_raw, conv_weight, a_log, dt_bias, head_gain, position):
    query, key_vec, value_vec, beta_gate, log_decay, gate_raw = prepare(
        projected, decay_raw, conv_weight, a_log, dt_bias, position
    )
    fresh_blocks = (position[::BLOCK] == 0).astype(jnp.float32)
    mix_heads = block_rule(query, key_vec, value_vec, beta_gate, log_decay, fresh_blocks)
    normed = rms_scale(mix_heads, head_gain)
    return normed.reshape(mix_heads.shape[0], HEADS * DV) * jax.nn.silu(gate_raw)


def swiglu_fn(gate_up):
    half_width = gate_up.shape[1] // 2
    return jax.nn.silu(gate_up[:, :half_width]) * gate_up[:, half_width:]


def local(
    tokens,
    out_grad,
    block_first,
    block_live,
    norm1_gain,
    w_proj,
    w_decay,
    conv_w,
    w_out,
    a_log,
    dt_bias,
    head_gain,
    norm2_gain,
    w_gate_up,
    w_down,
):
    position, live_mask = row_layout(block_first, block_live, tokens.shape[0])
    gain_one, proj_full, decay_full, out_full, conv_full = (
        lax.all_gather(norm1_gain, ("dp", "fsdp"), axis=0, tiled=True),
        lax.all_gather(w_proj, ("dp", "fsdp"), axis=0, tiled=True),
        lax.all_gather(w_decay, ("dp", "fsdp"), axis=0, tiled=True),
        lax.all_gather(w_out, ("dp", "fsdp"), axis=0, tiled=True),
        lax.all_gather(conv_w, ("dp", "fsdp"), axis=1, tiled=True),
    )
    tokens_f = tokens.astype(jnp.float32)
    normed_f, norm_one_pull = jax.vjp(rms_scale, tokens_f, gain_one.astype(jnp.float32))
    normed_one = normed_f.astype(jnp.bfloat16)
    projected = jnp.dot(normed_one, proj_full, preferred_element_type=jnp.float32)
    decay_raw = jnp.dot(normed_one, decay_full, preferred_element_type=jnp.float32)
    core_fn = partial(mixer_core, position=position)
    mixed_f, core_pull = jax.vjp(
        core_fn, projected, decay_raw, conv_full.astype(jnp.float32), a_log, dt_bias, head_gain
    )
    mixed = mixed_f.astype(jnp.bfloat16)
    residual = tokens_f + jnp.dot(mixed, out_full, preferred_element_type=jnp.float32)
    gain_two, gate_up_full, down_full = (
        lax.all_gather(norm2_gain, ("dp", "fsdp"), axis=0, tiled=True),
        lax.all_gather(w_gate_up, ("dp", "fsdp"), axis=0, tiled=True),
        lax.all_gather(w_down, ("dp", "fsdp"), axis=0, tiled=True),
    )
    normed_two_f, norm_two_pull = jax.vjp(rms_scale, residual, gain_two.astype(jnp.float32))
    normed_two = normed_two_f.astype(jnp.bfloat16)
    gate_up = jnp.dot(normed_two, gate_up_full, preferred_element_type=jnp.float32)
    hidden_f, swiglu_pull = jax.vjp(swiglu_fn, gate_up)
    hidden = hidden_f.astype(jnp.bfloat16)
    row_mask = live_mask[:, None]
    layer_out = (
        row_mask * (residual + jnp.dot(hidden, down_full, preferred_element_type=jnp.float32))
    ).astype(jnp.bfloat16)
    cotangent = row_mask * out_grad.astype(jnp.float32)
    grad_down = cotangent.astype(jnp.bfloat16)
    gate_up_back, down_back = (
        lax.all_gather(w_gate_up, ("dp", "fsdp"), axis=0, tiled=True),
        lax.all_gather(w_down, ("dp", "fsdp"), axis=0, tiled=True),
    )
    grad_wdown = tall_dot(hidden, grad_down)
    grad_hidden = back_dot(grad_down, down_back)
    (grad_gate_up_f,) = swiglu_pull(grad_hidden)
    grad_gate_up = grad_gate_up_f.astype(jnp.bfloat16)
    grad_wgate_up = tall_dot(normed_two, grad_gate_up)
    grad_normed_two = back_dot(grad_gate_up, gate_up_back)
    grad_from_two, grad_gain_two = norm_two_pull(grad_normed_two)
    grad_residual = cotangent + grad_from_two
    ffn_sums = (
        lax.psum_scatter(grad_gain_two, ("dp", "fsdp"), scatter_dimension=0, tiled=True),
        lax.psum_scatter(grad_wgate_up, ("dp", "fsdp"), scatter_dimension=0, tiled=True),
        lax.psum_scatter(grad_wdown, ("dp", "fsdp"), scatter_dimension=0, tiled=True),
    )
    proj_back, decay_back, out_back = (
        lax.all_gather(w_proj, ("dp", "fsdp"), axis=0, tiled=True),
        lax.all_gather(w_decay, ("dp", "fsdp"), axis=0, tiled=True),
        lax.all_gather(w_out, ("dp", "fsdp"), axis=0, tiled=True),
    )
    grad_mixed_in = grad_residual.astype(jnp.bfloat16)
    grad_wout = tall_dot(mixed, grad_mixed_in)
    grad_mixed = back_dot(grad_mixed_in, out_back)
    grad_proj_f, grad_decay_f, grad_conv, grad_log_rate, grad_step_bias, grad_head_gain = core_pull(
        grad_mixed
    )
    grad_proj = grad_proj_f.astype(jnp.bfloat16)
    grad_decay = grad_decay_f.astype(jnp.bfloat16)
    grad_wproj = tall_dot(normed_one, grad_proj)
    grad_wdecay = tall_dot(normed_one, grad_decay)
    grad_normed_one = back_dot(grad_proj, proj_back) + back_dot(grad_decay, decay_back)
    grad_from_one, grad_gain_one = norm_one_pull(grad_normed_one)
    tokens_grad = (grad_residual + grad_from_one).astype(jnp.bfloat16)
    mixer_sums = (
        lax.psum_scatter(grad_gain_one, ("dp", "fsdp"), scatter_dimension=0, tiled=True),
        lax.psum_scatter(grad_wproj, ("dp", "fsdp"), scatter_dimension=0, tiled=True),
        lax.psum_scatter(grad_wdecay, ("dp", "fsdp"), scatter_dimension=0, tiled=True),
        lax.psum_scatter(grad_wout, ("dp", "fsdp"), scatter_dimension=0, tiled=True),
        lax.psum_scatter(grad_conv, ("dp", "fsdp"), scatter_dimension=1, tiled=True),
    )
    head_sums = lax.psum((grad_log_rate, grad_step_bias, grad_head_gain), ("dp", "fsdp"))
    return (
        layer_out,
        tokens_grad,
        mixer_sums[0],
        mixer_sums[1],
        mixer_sums[2],
        mixer_sums[4],
        mixer_sums[3],
        head_sums[0],
        head_sums[1],
        head_sums[2],
        ffn_sums[0],
        ffn_sums[1],
        ffn_sums[2],
    )


def solution(mesh):
    in_specs = (
        P(("dp", "fsdp"), None),
        P(("dp", "fsdp"), None),
        P(("dp", "fsdp")),
        P(("dp", "fsdp")),
        P(("dp", "fsdp")),
        P(("dp", "fsdp"), None),
        P(("dp", "fsdp"), None),
        P(None, ("dp", "fsdp")),
        P(("dp", "fsdp"), None),
        P(),
        P(),
        P(),
        P(("dp", "fsdp")),
        P(("dp", "fsdp"), None),
        P(("dp", "fsdp"), None),
    )
    out_specs = (
        P(("dp", "fsdp"), None),
        P(("dp", "fsdp"), None),
        P(("dp", "fsdp")),
        P(("dp", "fsdp"), None),
        P(("dp", "fsdp"), None),
        P(None, ("dp", "fsdp")),
        P(("dp", "fsdp"), None),
        P(),
        P(),
        P(),
        P(("dp", "fsdp")),
        P(("dp", "fsdp"), None),
        P(("dp", "fsdp"), None),
    )
    return jax.shard_map(local, mesh=mesh, in_specs=in_specs, out_specs=out_specs, check_vma=False)
```

profile of v0, /device:TPU:0, one launch (start us, length us, event | category | flops | bytes accessed | tf_op | source)
XLA Modules:
  0.0 6335.5 jit_solution(15392647840652341835)
XLA Ops:
  10.8 44.8 all-reduce.26
  55.5 69.6 %all-gather = bf16[32,64,32]{1,2,0:T(8,128)(2,1)S(1)} all-gather(bf16[1,64,32]{1,2,0:T(8,128)(2,1)S(1)} %bitcast.498), channel_id=1, replica_groups=mesh['dp'=4,'fsdp'=8] {'dp','fsdp'}, dimensions={0}, use_global_device_ids=true | all-gather | bytes 135168 | tf_op jit(solution)/shard_map/all_gather | solution.py:182
  130.9 66.1 %all_gather.32 = bf16[4,8192]{1,0:T(4,128)(2,1)S(1)} all-gather(bf16[4,256]{1,0:T(4,128)(2,1)S(1)} %copy-done.103), channel_id=1, replica_groups=mesh['dp'=4,'fsdp'=8] {'dp','fsdp'}, dimensions={1}, use_global_device_ids=true | all-gather | bytes 67584 | tf_op jit(solution)/shard_map/all_gather | solution.py:184
  198.5 93.6 %all-gather.6.cloned.1.call-done = bf16[2048,12288]{1,0:T(8,128)(2,1)} async-done(((bf16[64,12288]{1,0:T(8,128)(2,1)}), bf16[2048,12288]{1,0:T(8,128)(2,1)}) %all-gather.6.cloned.1.call-update) | async-done | bytes 50331664 | tf_op jit(solution)/shard_map/all_gather | solution.py:181
  292.2 25.2 fusion.224
  411.4 450.0 %while.70 = (s32[]{:T(128)}, f32[16,256,128]{2,1,0:T(8,128)S(1)}, f32[4,16,64,256]{3,2,1,0:T(8,128)}, f32[4]{0:T(128)S(1)}, f32[4,16,64]{2,1,0:T(8,128)S(1)}, /*...) while((s32[]{:T(128)}, f32[16,256,128]{2,1,0:T(8,128)S(1)}, ...), condition=%wide.region_6.7_spmd.clone, body=%wide.region_5.6_spmd.clone.sunk | while | flops 1618361344 | bytes 35822040 | solution.py:129
  427.8 80.0 %custom-call.30 = f32[16,1,64,64]{2,3,1,0:T(8,128)} custom-call(f32[16,1,64,64]{3,2,1,0:T(8,128)} %add_bitcast_fusion.7), custom_call_target="InvertDiagBlocksLowerTriangular" | custom-call | tf_op jit(solution)/shard_map/jvp()/while/body/eval_jaxpr/jit(_solve_triangular)/vmap()/triangular_solve | solution.py:116
  540.6 80.0 %custom-call.30 = f32[16,1,64,64]{2,3,1,0:T(8,128)} custom-call(f32[16,1,64,64]{3,2,1,0:T(8,128)} %add_bitcast_fusion.7), custom_call_target="InvertDiagBlocksLowerTriangular" | custom-call | tf_op jit(solution)/shard_map/jvp()/while/body/eval_jaxpr/jit(_solve_triangular)/vmap()/triangular_solve | solution.py:116
  652.9 80.0 %custom-call.30 = f32[16,1,64,64]{2,3,1,0:T(8,128)} custom-call(f32[16,1,64,64]{3,2,1,0:T(8,128)} %add_bitcast_fusion.7), custom_call_target="InvertDiagBlocksLowerTriangular" | custom-call | tf_op jit(solution)/shard_map/jvp()/while/body/eval_jaxpr/jit(_solve_triangular)/vmap()/triangular_solve | solution.py:116
  765.1 80.0 %custom-call.30 = f32[16,1,64,64]{2,3,1,0:T(8,128)} custom-call(f32[16,1,64,64]{3,2,1,0:T(8,128)} %add_bitcast_fusion.7), custom_call_target="InvertDiagBlocksLowerTriangular" | custom-call | tf_op jit(solution)/shard_map/jvp()/while/body/eval_jaxpr/jit(_solve_triangular)/vmap()/triangular_solve | solution.py:116
  917.6 27.5 fusion.188
  1007.5 519.1 %while.71 = (s32[]{:T(128)}, f32[16,256,128]{2,1,0:T(8,128)S(1)}, f32[4,16,64,128]{3,2,1,0:T(8,128)}, f32[4,16,64,128]{3,2,1,0:T(8,128)}, f32[4,16,64,256]{3,2,1...) while((s32[]{:T(128)}, f32[16,256,128]{2,1,0:T(8,128)S(1)}, ...), condition=%wide.region_18.19_spmd.clone, body=%wide.region_11.18_spmd.clone.sunk | while | flops 3282715648 | bytes 70527152 | solution.py:129
  1018.8 80.0 %custom-call.31 = f32[16,1,64,64]{2,3,1,0:T(8,128)} custom-call(f32[16,1,64,64]{3,2,1,0:T(8,128)} %add_bitcast_fusion.8), custom_call_target="InvertDiagBlocksLowerTriangular" | custom-call | tf_op jit(solution)/shard_map/transpose(jvp())/while/body/eval_jaxpr/jit(_solve_triangular)/vmap()/triangular_solve | solution.py:116
  1148.5 80.0 %custom-call.31 = f32[16,1,64,64]{2,3,1,0:T(8,128)} custom-call(f32[16,1,64,64]{3,2,1,0:T(8,128)} %add_bitcast_fusion.8), custom_call_target="InvertDiagBlocksLowerTriangular" | custom-call | tf_op jit(solution)/shard_map/transpose(jvp())/while/body/eval_jaxpr/jit(_solve_triangular)/vmap()/triangular_solve | solution.py:116
  1278.2 80.0 %custom-call.31 = f32[16,1,64,64]{2,3,1,0:T(8,128)} custom-call(f32[16,1,64,64]{3,2,1,0:T(8,128)} %add_bitcast_fusion.8), custom_call_target="InvertDiagBlocksLowerTriangular" | custom-call | tf_op jit(solution)/shard_map/transpose(jvp())/while/body/eval_jaxpr/jit(_solve_triangular)/vmap()/triangular_solve | solution.py:116
  1407.7 80.0 %custom-call.31 = f32[16,1,64,64]{2,3,1,0:T(8,128)} custom-call(f32[16,1,64,64]{3,2,1,0:T(8,128)} %add_bitcast_fusion.8), custom_call_target="InvertDiagBlocksLowerTriangular" | custom-call | tf_op jit(solution)/shard_map/transpose(jvp())/while/body/eval_jaxpr/jit(_solve_triangular)/vmap()/triangular_solve | solution.py:116
  1688.5 37.6 fusion.184
  1727.8 34.6 fusion.186
  1791.8 38.6 all-reduce.25
  1848.5 41.8 reduce-scatter.19.cloned.1.call-done
  1891.8 704.2 %reduce-scatter.13.cloned.1.call-done = f32[128,2048]{1,0:T(8,128)} async-done(((f32[4096,2048]{1,0:T(8,128)}), f32[128,2048]{1,0:T(8,128)}) %reduce-scatter.13.cloned.1.call-update) | async-done | bytes 1048592 | tf_op jit(solution)/shard_map/reduce_scatter | solution.py:252
  2596.0 970.3 %reduce-scatter.17.cloned.1.call-done = f32[176,2048]{1,0:T(8,128)} async-done(((f32[5632,2048]{1,0:T(8,128)}), f32[176,2048]{1,0:T(8,128)}) %reduce-scatter.17.cloned.1.call-update) | async-done | bytes 1441808 | tf_op jit(solution)/shard_map/reduce_scatter | solution.py:228
  3566.3 835.0 %reduce-scatter.11.cloned.1.call-done = f32[64,12288]{1,0:T(8,128)} async-done(((f32[2048,12288]{1,0:T(8,128)}), f32[64,12288]{1,0:T(8,128)}) %reduce-scatter.11.cloned.1.call-update) | async-done | bytes 3145744 | tf_op jit(solution)/shard_map/reduce_scatter | solution.py:250
  4401.3 1927.2 %reduce-scatter.15.cloned.1.call-done = f32[64,11264]{1,0:T(8,128)} async-done(((f32[2048,11264]{1,0:T(8,128)}), f32[64,11264]{1,0:T(8,128)}) %reduce-scatter.15.cloned.1.call-update) | async-done | bytes 2883600 | tf_op jit(solution)/shard_map/reduce_scatter | solution.py:227
  (686 shorter events, 761.7 us)
Async XLA Ops:
  7.2 284.9 %all-gather.6.cloned.1.call-start = ((), (), s32[]{:S(2)}) async-start(), calls=%async_computation.6 | async-start | bytes 51904512 | tf_op jit(solution)/shard_map/all_gather | solution.py:181
  8.0 874.1 %all-gather.8.cloned.1.call-start = ((), (), s32[]{:S(2)}) async-start(), calls=%async_computation.7 | async-start | bytes 17301504 | tf_op jit(solution)/shard_map/all_gather | solution.py:183
  8.7 884.0 %all-gather.10.cloned.1.call-start = ((), (), s32[]{:S(2)}) async-start(), calls=%async_computation.8 | async-start | bytes 47579136 | tf_op jit(solution)/shard_map/all_gather | solution.py:199
  9.5 908.1 %all-gather.12.cloned.1.call-start = ((), (), s32[]{:S(2)}) async-start(), calls=%async_computation.9 | async-start | bytes 23789568 | tf_op jit(solution)/shard_map/all_gather | solution.py:200
  10.0 1836.9 %reduce-scatter.21.cloned.1.call-start = ((), (), s32[]{:S(2)}) async-start(), calls=%async_computation.15 | async-start | bytes 4325376
  55.5 236.6 %copy-start.45 = (f32[2048]{0:T(1024)}, f32[2048]{0:T(1024)S(1)}, u32[]{:S(2)}) copy-start(f32[2048]{0:T(1024)S(1)} %convert_element_type.88) | copy-start | bytes 24580
  127.1 190.2 %copy-start.51 = (f32[256]{0:T(256)}, f32[256]{0:T(256)S(1)}, u32[]{:S(2)}) copy-start(f32[256]{0:T(256)S(1)} %fusion.208) | copy-start | bytes 3076
  197.0 181.6 %copy-start.53 = (pred[64,64]{0,1:T(8,128)(4,1)}, pred[64,64]{0,1:T(8,128)(4,1)S(1)}, u32[]{:S(2)}) copy-start(pred[64,64]{0,1:T(8,128)(4,1)S(1)} %get-tuple-element.1434) | copy-start | bytes 12292
  197.0 181.6 %copy-start.66 = (pred[64,64]{0,1:T(8,128)(4,1)}, pred[64,64]{0,1:T(8,128)(4,1)S(1)}, u32[]{:S(2)}) copy-start(pred[64,64]{0,1:T(8,128)(4,1)S(1)} %get-tuple-element.1435) | copy-start | bytes 12292
  197.7 137.2 %copy-start.82 = (f32[256]{0:T(256)}, f32[256]{0:T(256)S(1)}, u32[]{:S(2)}) copy-start(f32[256]{0:T(256)S(1)} %get-tuple-element.1424) | copy-start | bytes 3076
  197.7 137.2 %copy-start.84 = (f32[256]{0:T(256)}, f32[256]{0:T(256)S(1)}, u32[]{:S(2)}) copy-start(f32[256]{0:T(256)S(1)} %get-tuple-element.1423) | copy-start | bytes 3076
  197.7 137.2 %copy-start.86 = (f32[256]{0:T(256)}, f32[256]{0:T(256)S(1)}, u32[]{:S(2)}) copy-start(f32[256]{0:T(256)S(1)} %get-tuple-element.1422) | copy-start | bytes 3076
  198.5 136.5 %copy-start.58 = (f32[1,8192]{1,0:T(1,128)}, f32[1,8192]{1,0:T(1,128)S(1)}, u32[]{:S(2)}) copy-start(f32[1,8192]{1,0:T(1,128)S(1)} %get-tuple-element.1413) | copy-start | bytes 98308
  198.5 136.5 %copy-start.60 = (f32[1,8192]{1,0:T(1,128)}, f32[1,8192]{1,0:T(1,128)S(1)}, u32[]{:S(2)}) copy-start(f32[1,8192]{1,0:T(1,128)S(1)} %get-tuple-element.1412) | copy-start | bytes 98308
  198.5 136.5 %copy-start.62 = (f32[1,8192]{1,0:T(1,128)}, f32[1,8192]{1,0:T(1,128)S(1)}, u32[]{:S(2)}) copy-start(f32[1,8192]{1,0:T(1,128)S(1)} %get-tuple-element.1411) | copy-start | bytes 98308
  1007.4 519.1 %copy-start.33 = (f32[4,16,64]{2,1,0:T(8,128)S(1)}, f32[4,16,64]{2,1,0:T(8,128)}, u32[]{:S(2)}) copy-start(f32[4,16,64]{2,1,0:T(8,128)} %copy-done.32) | copy-start | bytes 49156
  1007.5 519.1 %copy-start.44 = (f32[4,16,64]{2,1,0:T(8,128)S(1)}, f32[4,16,64]{2,1,0:T(8,128)}, u32[]{:S(2)}) copy-start(f32[4,16,64]{2,1,0:T(8,128)} %copy-done.43) | copy-start | bytes 49156
  1007.5 519.1 %copy-start.54 = (pred[64,64]{0,1:T(8,128)(4,1)S(1)}, pred[64,64]{0,1:T(8,128)(4,1)}, u32[]{:S(2)}) copy-start(pred[64,64]{0,1:T(8,128)(4,1)} %copy-done.53) | copy-start | bytes 12292
  1007.5 519.1 %copy-start.67 = (pred[64,64]{0,1:T(8,128)(4,1)S(1)}, pred[64,64]{0,1:T(8,128)(4,1)}, u32[]{:S(2)}) copy-start(pred[64,64]{0,1:T(8,128)(4,1)} %copy-done.66) | copy-start | bytes 12292
  1613.6 276.7 %reduce-scatter.19.cloned.1.call-start = ((), (), s32[]{:S(2)}) async-start(), calls=%async_computation.14 | async-start | bytes 1081344
  1616.7 979.2 %reduce-scatter.13.cloned.1.call-start = ((), (), s32[]{:S(2)}) async-start(), calls=%async_computation.11 | async-start | bytes 34603008 | tf_op jit(solution)/shard_map/reduce_scatter | solution.py:252
  1631.7 1934.6 %reduce-scatter.17.cloned.1.call-start = ((), (), s32[]{:S(2)}) async-start(), calls=%async_computation.13 | async-start | bytes 47579136 | tf_op jit(solution)/shard_map/reduce_scatter | solution.py:228
  1652.8 2748.5 %reduce-scatter.11.cloned.1.call-start = ((), (), s32[]{:S(2)}) async-start(), calls=%async_computation.10 | async-start | bytes 103809024 | tf_op jit(solution)/shard_map/reduce_scatter | solution.py:250
  1726.2 4602.3 %reduce-scatter.15.cloned.1.call-start = ((), (), s32[]{:S(2)}) async-start(), calls=%async_computation.12 | async-start | bytes 95158272 | tf_op jit(solution)/shard_map/reduce_scatter | solution.py:227
  (125 other events, 2336.9 us)
Sparse Core Ops, SparseCore 0:
  11.0 281.1 all-gather.5
  295.2 113.0 all-gather.7
  411.2 253.8 all-gather.9
  667.8 143.4 all-gather.11
  1613.7 142.1 reduce-scatter.20
  1758.0 132.2 reduce-scatter.18
  1893.3 702.5 reduce-scatter.12
  2598.9 967.3 reduce-scatter.16
  3574.5 826.8 reduce-scatter.10
  4404.2 1924.2 reduce-scatter.14
where the time goes:
time: 6340 us
  waiting for transfers between devices  4570 us (72%)
  other arithmetic  813 us (13%)
  matrix products  558 us (9%)
  blocking collectives  219 us (3%)
  local copies, waits for them, and re-layouts  153 us (2%)
    reduce_scatter x1, waiting for transfers between devices, local(): lax.psum_scatter(grad_wgate_up, ('dp', 'fsdp'), scatter_dimension=0, tile...  1930 us
    reduce_scatter x1, waiting for transfers between devices, local(): lax.psum_scatter(grad_wdown, ('dp', 'fsdp'), scatter_dimension=0, tiled=T...  970 us
    reduce_scatter x1, waiting for transfers between devices, local(): lax.psum_scatter(grad_wproj, ('dp', 'fsdp'), scatter_dimension=0, tiled=T...  835 us
    reduce_scatter x1, waiting for transfers between devices, local(): lax.psum_scatter(grad_wout, ('dp', 'fsdp'), scatter_dimension=0, tiled=True)  704 us
    another operation x36, other arithmetic, step_fn(): jax.scipy.linalg.solve_triangular(system_part, right_side, lower=True, un...  656 us
  transfers between devices with their start and end apart: 10, of which 6 were waited for; matrix products, arithmetic and copies ran while one was open for 13% of the time, Pallas kernels for 0%

commit v1 on v0

v1 whole, which is shorter than its diff:
```python
from functools import partial

import jax
import jax.numpy as jnp
from jax import lax
from jax.experimental import pallas as pl
from jax.experimental.pallas import tpu as pltpu
from jax.sharding import PartitionSpec as P

HEADS = 16
DK = 128
DV = 256
CONV = 4
BLOCK = 64
TP = 4
LH = HEADS // TP
TAIL = 128
EPS = 1e-06
HIGH = lax.Precision.HIGHEST
F32 = jnp.float32
BF16 = jnp.bfloat16


def mm(left, right, dims=((1,), (0,))):
    return lax.dot_general(left, right, (dims, ((), ())), preferred_element_type=F32)


def mmb(left, right, dims=((1,), (0,))):
    return mm(left.astype(BF16), right.astype(BF16), dims)


def mm3(left, right):
    left_hi = left.astype(BF16)
    right_hi = right.astype(BF16)
    left_lo = (left - left_hi.astype(F32)).astype(BF16)
    right_lo = (right - right_hi.astype(F32)).astype(BF16)
    return mm(left_hi, right_hi) + (mm(left_hi, right_lo) + mm(left_lo, right_hi))


def mmx(left, right, dims=((1,), (0,))):
    return lax.dot_general(left, right, (dims, ((), ())), precision=HIGH, preferred_element_type=F32)


def sigmoid(v):
    return 1.0 / (1.0 + jnp.exp(-v))


def conv_rows(raw, taps, pos):
    total = raw * taps[CONV - 1 : CONV]
    for lag in range(1, CONV):
        moved = pltpu.roll(raw, lag, 0)
        total = total + jnp.where(pos >= lag, moved, 0.0) * taps[CONV - 1 - lag : CONV - lag]
    return total


def conv_back(grad, raw, taps, pos):
    rows = raw.shape[0]
    total = grad * taps[CONV - 1 : CONV]
    sums = [jnp.sum(grad * raw, axis=0, keepdims=True)]
    for lag in range(1, CONV):
        kept = jnp.where(pos >= lag, grad, 0.0)
        total = total + pltpu.roll(kept, rows - lag, 0) * taps[CONV - 1 - lag : CONV - lag]
        sums.append(jnp.sum(kept * pltpu.roll(raw, lag, 0), axis=0, keepdims=True))
    return total, sums[::-1]


def unit(v, scale):
    inv = lax.rsqrt(jnp.sum(v * v, axis=-1, keepdims=True) + EPS)
    return v * (inv * scale), inv


def unit_back(grad, v, inv, scale):
    g = grad * scale
    return inv * g - v * (inv * inv * inv * jnp.sum(v * g, axis=-1, keepdims=True))


def silu_back(grad, pre, sig):
    return grad * (sig * (1.0 + pre * (1.0 - sig)))


def group_terms(tail_ref, prm_ref, pos_ref):
    rows = tail_ref.shape[0]
    pos = pos_ref[:, 0:1].astype(jnp.int32)
    row_i = lax.broadcasted_iota(jnp.int32, (rows, rows), 0)
    row_j = lax.broadcasted_iota(jnp.int32, (rows, rows), 1)
    lower = (row_j <= row_i) & (row_j >= row_i - pos)
    raw = tail_ref[...]
    shifted = raw + prm_ref[1:2]
    soft = jnp.maximum(shifted, 0.0) + jnp.log1p(jnp.exp(-jnp.abs(shifted)))
    log_decay = prm_ref[0:1] * soft
    beta = sigmoid(raw)
    lower_f = lower.astype(F32)
    cum = mmx(lower_f, log_decay)
    return pos, row_i, row_j, lower, lower_f, raw, shifted, log_decay, beta, cum, cum.T


def unit_lower_inverse(low, bits):
    rows = low.shape[0]
    eye = (bits == 0).astype(F32)
    inv = eye - jnp.where(bits == 1, low, 0.0)
    step = 1
    while (2 << step) <= rows:
        part = jnp.where((bits >> step) == 1, low, 0.0)
        inv = inv - mm3(inv, mm3(part, inv))
        step += 1
    return inv


def head_slices(head):
    key_width = LH * DK
    return (
        slice(head * DK, (head + 1) * DK),
        slice(key_width + head * DK, key_width + (head + 1) * DK),
        slice(2 * key_width + head * DV, 2 * key_width + (head + 1) * DV),
        slice(2 * key_width + (LH + head) * DV, 2 * key_width + (LH + head + 1) * DV),
    )


def mixer_fwd_kernel(proj_ref, pos_ref, conv_ref, prm_ref, gain_ref, mixed_ref, inv_ref, new_ref):
    width = proj_ref.shape[1]
    tail_ref = proj_ref.at[:, width - TAIL :]
    pos, row_i, row_j, lower, _, _, _, _, beta_all, cum, cum_t = group_terms(tail_ref, prm_ref, pos_ref)
    strict = lower & (row_j < row_i)
    bits = row_i ^ row_j
    for head in range(LH):
        sq, sk, sv, sg = head_slices(head)
        q_pre = conv_rows(proj_ref[:, sq], conv_ref[:, sq], pos)
        k_pre = conv_rows(proj_ref[:, sk], conv_ref[:, sk], pos)
        v_pre = conv_rows(proj_ref[:, sv], conv_ref[:, sv], pos)
        query, _ = unit(q_pre * sigmoid(q_pre), DK**-0.5)
        key, _ = unit(k_pre * sigmoid(k_pre), 1.0)
        value = v_pre * sigmoid(v_pre)
        beta = beta_all[:, LH + head : LH + head + 1]
        gap = cum[:, head : head + 1] - cum_t[head : head + 1, :]
        decay = jnp.where(lower, jnp.exp(gap), 0.0)
        pair = mmb(key, key, ((1,), (1,)))
        attend = mmb(query, key, ((1,), (1,))) * decay
        low = jnp.where(strict, beta * pair * decay, 0.0)
        inv = unit_lower_inverse(low, bits)
        new = mmb(inv, beta * value)
        mix = mmb(attend, new)
        scale = lax.rsqrt(jnp.mean(mix * mix, axis=-1, keepdims=True) + EPS)
        gate = proj_ref[:, sg]
        out = mix * scale * gain_ref[0:1] * (gate * sigmoid(gate))
        mixed_ref[:, head * DV : (head + 1) * DV] = out.astype(BF16)
        inv_ref[head] = inv.astype(BF16)
        new_ref[:, head * DV : (head + 1) * DV] = new.astype(BF16)


def mixer_bwd_kernel(
    proj_ref, pos_ref, conv_ref, prm_ref, gain_ref, inv_ref, new_ref, gmix_ref, gproj_ref, gconv_ref, misc_ref
):
    width = proj_ref.shape[1]
    rows = proj_ref.shape[0]
    tail_ref = proj_ref.at[:, width - TAIL :]
    pos, row_i, row_j, lower, lower_f, raw, shifted, log_decay, beta_all, cum, cum_t = group_terms(
        tail_ref, prm_ref, pos_ref
    )
    strict = lower & (row_j < row_i)
    lane = lax.broadcasted_iota(jnp.int32, (rows, TAIL), 1)
    ones = jnp.ones((rows, TAIL), F32)
    grad_cum = jnp.zeros((rows, TAIL), F32)
    grad_beta_all = jnp.zeros((rows, TAIL), F32)
    gain_sum = jnp.zeros((1, DV), F32)
    gconv_ref[...] = jnp.zeros_like(gconv_ref)
    misc_ref[...] = jnp.zeros_like(misc_ref)
    for head in range(LH):
        sq, sk, sv, sg = head_slices(head)
        q_raw, k_raw, v_raw = proj_ref[:, sq], proj_ref[:, sk], proj_ref[:, sv]
        q_pre = conv_rows(q_raw, conv_ref[:, sq], pos)
        k_pre = conv_rows(k_raw, conv_ref[:, sk], pos)
        v_pre = conv_rows(v_raw, conv_ref[:, sv], pos)
        q_sig, k_sig, v_sig = sigmoid(q_pre), sigmoid(k_pre), sigmoid(v_pre)
        q_act, k_act, value = q_pre * q_sig, k_pre * k_sig, v_pre * v_sig
        query, q_inv = unit(q_act, DK**-0.5)
        key, k_inv = unit(k_act, 1.0)
        query_b, key_b = query.astype(BF16), key.astype(BF16)
        beta = beta_all[:, LH + head : LH + head + 1]
        gap = cum[:, head : head + 1] - cum_t[head : head + 1, :]
        decay = jnp.where(lower, jnp.exp(gap), 0.0)
        pair = mm(key_b, key_b, ((1,), (1,)))
        query_pair = mm(query_b, key_b, ((1,), (1,)))
        attend = (query_pair * decay).astype(BF16)
        inv = inv_ref[head]
        new = new_ref[:, head * DV : (head + 1) * DV]
        mix = mm(attend, new)
        scale = lax.rsqrt(jnp.mean(mix * mix, axis=-1, keepdims=True) + EPS)
        gate = proj_ref[:, sg]
        gate_sig = sigmoid(gate)
        grad_out = gmix_ref[:, head * DV : (head + 1) * DV]
        unscaled = mix * scale
        grad_norm = grad_out * (gate * gate_sig)
        grad_gate = silu_back(grad_out * unscaled * gain_ref[0:1], gate, gate_sig)
        gain_sum = gain_sum + jnp.sum(grad_norm * unscaled, axis=0, keepdims=True)
        weighted = grad_norm * gain_ref[0:1]
        grad_mix = scale * weighted - mix * (
            scale * scale * scale * jnp.mean(mix * weighted, axis=-1, keepdims=True)
        )
        grad_mix_b = grad_mix.astype(BF16)
        grad_new = mm(attend, grad_mix_b, ((0,), (0,)))
        grad_attend = mm(grad_mix_b, new, ((1,), (1,)))
        grad_rhs = mmb(inv, grad_new, ((0,), (0,)))
        grad_low = -mm(grad_rhs.astype(BF16), new, ((1,), (1,)))
        grad_value = beta * grad_rhs
        low_decay = jnp.where(strict, grad_low * decay, 0.0)
        low_pair = low_decay * pair
        grad_beta = jnp.sum(grad_rhs * value, axis=-1, keepdims=True) + jnp.sum(
            low_pair, axis=-1, keepdims=True
        )
        grad_pair = beta * low_decay
        grad_query_pair = grad_attend * decay
        both = beta * low_pair + grad_query_pair * query_pair
        column = jnp.sum(both, axis=-1, keepdims=True) - mmx(both, ones, ((0,), (0,)))
        grad_cum = jnp.where(lane == head, column, grad_cum)
        grad_beta_all = jnp.where(lane == LH + head, grad_beta, grad_beta_all)
        grad_pair_b = grad_pair.astype(BF16)
        grad_qp_b = grad_query_pair.astype(BF16)
        grad_query = mm(grad_qp_b, key_b)
        grad_key = (
            mm(grad_qp_b, query_b, ((0,), (0,))) + mm(grad_pair_b, key_b) + mm(grad_pair_b, key_b, ((0,), (0,)))
        )
        grad_q = silu_back(unit_back(grad_query, q_act, q_inv, DK**-0.5), q_pre, q_sig)
        grad_k = silu_back(unit_back(grad_key, k_act, k_inv, 1.0), k_pre, k_sig)
        grad_v = silu_back(grad_value, v_pre, v_sig)
        for grad, part, where in ((grad_q, q_raw, sq), (grad_k, k_raw, sk), (grad_v, v_raw, sv)):
            moved, sums = conv_back(grad, part, conv_ref[:, where], pos)
            gproj_ref[:, where] = moved.astype(BF16)
            for tap in range(CONV):
                gconv_ref[0, tap : tap + 1, where] = sums[tap]
        gproj_ref[:, sg] = grad_gate.astype(BF16)
    grad_log = mmx(lower_f, grad_cum, ((0,), (0,)))
    grad_step = grad_log * prm_ref[0:1] * sigmoid(shifted)
    grad_tail = grad_step + grad_beta_all * beta_all * (1.0 - beta_all)
    gproj_ref[:, width - TAIL :] = grad_tail.astype(BF16)
    misc_ref[0, 0:1, :] = gain_sum
    misc_ref[0, 1:2, 0:TAIL] = jnp.sum(grad_log * log_decay, axis=0, keepdims=True)
    misc_ref[0, 2:3, 0:TAIL] = jnp.sum(grad_step, axis=0, keepdims=True)


VMEM_LIMIT = 56 * 1024 * 1024


def mixer_fwd(proj, pos, conv, prm, gain):
    total, width = proj.shape
    rows = total // TP
    return pl.pallas_call(
        mixer_fwd_kernel,
        grid=(TP,),
        in_specs=[
            pl.BlockSpec((rows, width), lambda g: (g, 0)),
            pl.BlockSpec((rows, TAIL), lambda g: (g, 0)),
            pl.BlockSpec(conv.shape, lambda g: (0, 0)),
            pl.BlockSpec(prm.shape, lambda g: (0, 0)),
            pl.BlockSpec(gain.shape, lambda g: (0, 0)),
        ],
        out_specs=[
            pl.BlockSpec((rows, LH * DV), lambda g: (g, 0)),
            pl.BlockSpec((LH, rows, rows), lambda g: (g, 0, 0)),
            pl.BlockSpec((rows, LH * DV), lambda g: (g, 0)),
        ],
        out_shape=[
            jax.ShapeDtypeStruct((total, LH * DV), BF16),
            jax.ShapeDtypeStruct((TP * LH, rows, rows), BF16),
            jax.ShapeDtypeStruct((total, LH * DV), BF16),
        ],
        compiler_params=pltpu.CompilerParams(vmem_limit_bytes=VMEM_LIMIT),
        cost_estimate=pl.CostEstimate(flops=30_000_000_000, bytes_accessed=30_000_000, transcendentals=5_000_000),
        name="mixer_fwd",
    )(proj, pos, conv, prm, gain)


def mixer_bwd(proj, pos, conv, prm, gain, inv, new, gmix):
    total, width = proj.shape
    rows = total // TP
    return pl.pallas_call(
        mixer_bwd_kernel,
        grid=(TP,),
        in_specs=[
            pl.BlockSpec((rows, width), lambda g: (g, 0)),
            pl.BlockSpec((rows, TAIL), lambda g: (g, 0)),
            pl.BlockSpec(conv.shape, lambda g: (0, 0)),
            pl.BlockSpec(prm.shape, lambda g: (0, 0)),
            pl.BlockSpec(gain.shape, lambda g: (0, 0)),
            pl.BlockSpec((LH, rows, rows), lambda g: (g, 0, 0)),
            pl.BlockSpec((rows, LH * DV), lambda g: (g, 0)),
            pl.BlockSpec((rows, LH * DV), lambda g: (g, 0)),
        ],
        out_specs=[
            pl.BlockSpec((rows, width), lambda g: (g, 0)),
            pl.BlockSpec((1, 8, conv.shape[1]), lambda g: (g, 0, 0)),
            pl.BlockSpec((1, 8, DV), lambda g: (g, 0, 0)),
        ],
        out_shape=[
            jax.ShapeDtypeStruct((total, width), BF16),
            jax.ShapeDtypeStruct((TP, 8, conv.shape[1]), F32),
            jax.ShapeDtypeStruct((TP, 8, DV), F32),
        ],
        compiler_params=pltpu.CompilerParams(vmem_limit_bytes=VMEM_LIMIT),
        cost_estimate=pl.CostEstimate(flops=50_000_000_000, bytes_accessed=40_000_000, transcendentals=5_000_000),
        name="mixer_bwd",
    )(proj, pos, conv, prm, gain, inv, new, gmix)


def after(value, *earlier):
    return lax.optimization_barrier((value,) + earlier)[0]


class Moves:
    def __init__(self, fsdp_size):
        self.nf = fsdp_size
        self.nz = fsdp_size // 2
        self.f = lax.axis_index("fsdp")
        self.z = self.f // 2
        self.y = self.f % 2
        self.d = lax.axis_index("dp")

    def dp_swap(self, value, mask):
        return lax.ppermute(value, "dp", [(i, i ^ mask) for i in range(TP)])

    def y_swap(self, value):
        return lax.ppermute(value, "fsdp", [(i, i ^ 1) for i in range(self.nf)])

    def z_turn(self, value, step):
        pairs = [(i, ((i // 2 + step) % self.nz) * 2 + i % 2) for i in range(self.nf)]
        return lax.ppermute(value, "fsdp", pairs)

    def dp_gather(self, value):
        far = self.dp_swap(value, 2)
        near = self.dp_swap(value, 1)
        return jnp.stack([value, near, far, self.dp_swap(far, 1)])

    def dp_reduce(self, parts):
        got = self.dp_swap(jnp.stack([parts[1], parts[3]]), 1)
        mine = parts[0].astype(F32) + got[0].astype(F32)
        far = (parts[2].astype(F32) + got[1].astype(F32)).astype(BF16)
        return mine + self.dp_swap(far, 2).astype(F32)

    def gather(self, value, before=()):
        value = after(value, *before)
        turned = [value] + [self.z_turn(value, k) for k in range(1, self.nz)]
        full = jnp.zeros((self.nz, 2) + value.shape, value.dtype)
        for k, part in enumerate(turned):
            other = self.y_swap(part)
            where = (self.z - k) % self.nz
            zero = (0,) * value.ndim
            full = lax.dynamic_update_slice(full, part[None, None], (where, self.y) + zero)
            full = lax.dynamic_update_slice(full, other[None, None], (where, 1 - self.y) + zero)
        return full.reshape((self.nf,) + value.shape), tuple(turned[1:])

    def reduce(self, send, keep):
        total = keep + self.y_swap(send).astype(F32)
        rounded = total.astype(BF16)
        mine = lax.dynamic_index_in_dim(total, self.z, 0, keepdims=False)
        for k in range(1, self.nz):
            part = lax.dynamic_index_in_dim(rounded, (self.z + k) % self.nz, 0, keepdims=False)
            mine = mine + self.z_turn(part, k).astype(F32)
        return mine

    def halves(self, value, axis):
        shape = value.shape
        split = value.reshape(shape[:axis] + (self.nz, 2, shape[axis] // self.nf) + shape[axis + 1 :])
        return tuple(
            lax.dynamic_index_in_dim(split, which, axis + 1, keepdims=False).reshape(
                shape[:axis] + (shape[axis] // 2,) + shape[axis + 1 :]
            )
            for which in (1 - self.y, self.y)
        )


def local(
    tokens,
    out_grad,
    block_first,
    block_live,
    norm1_gain,
    w_proj,
    w_decay,
    conv_w,
    w_out,
    a_log,
    dt_bias,
    head_gain,
    norm2_gain,
    w_gate_up,
    w_down,
    *,
    fsdp_size,
):
    mv = Moves(fsdp_size)
    nf, nz = mv.nf, mv.nz
    rows, width = tokens.shape
    own = w_proj.shape[0]
    key_width = HEADS * DK
    value_width = HEADS * DV
    ff = w_down.shape[0] * nf

    def to_perm(value):
        return value.reshape(rows, TP, nf, own).swapaxes(1, 2).reshape(rows, width)

    def from_perm(value):
        return value.reshape(rows, nf, TP, own).swapaxes(1, 2).reshape(rows, width)

    block_index = jnp.arange(block_first.shape[0], dtype=jnp.int32)
    earlier = (block_index[:, None] >= block_index[None]) & (block_first[None] > 0)
    bucket_starts = jnp.max(jnp.where(earlier, block_index[None] * BLOCK, 0), axis=1)
    row_index = jnp.arange(rows, dtype=jnp.int32)
    position = row_index - jnp.repeat(bucket_starts, BLOCK)
    live = (row_index % BLOCK < jnp.repeat(block_live, BLOCK)).astype(F32)[:, None]

    def by_target(value):
        return value.reshape(own, TP, -1).swapaxes(0, 1)

    taps = conv_w.reshape(own, -1)
    tail = jnp.concatenate(
        [
            by_target(w_decay[:, :HEADS]),
            by_target(w_decay[:, HEADS:]),
            jnp.broadcast_to(
                jnp.concatenate([norm1_gain[:, None], norm2_gain[:, None], taps], axis=1)[None],
                (TP, own, 2 + taps.shape[1]),
            ),
        ],
        axis=2,
    )
    tail = jnp.pad(tail, ((0, 0), (0, 0), (0, TAIL - tail.shape[2])))
    pack_one = jnp.concatenate(
        [
            by_target(w_proj[:, :key_width]),
            by_target(w_proj[:, key_width : 2 * key_width]),
            by_target(w_proj[:, 2 * key_width : 2 * key_width + value_width]),
            by_target(w_proj[:, 2 * key_width + value_width :]),
            tail,
        ],
        axis=2,
    )
    pack_two = jnp.concatenate([by_target(w_gate_up[:, :ff * TP]), by_target(w_gate_up[:, ff * TP :])], axis=2)

    out_blocks, out_done = mv.gather(w_out)
    pack_one = lax.all_to_all(pack_one, "dp", 0, 0, tiled=True)
    pack_two = lax.all_to_all(pack_two, "dp", 0, 0, tiled=True)
    one_blocks, one_done = mv.gather(pack_one, out_done)
    two_blocks, two_done = mv.gather(pack_two, one_done)
    down_blocks, _ = mv.gather(w_down, two_done)
    out_full = out_blocks.reshape(-1, width)
    proj_full = one_blocks.reshape(width, -1)
    gate_up_full = two_blocks.reshape(width, -1)
    down_full = down_blocks.reshape(-1, width)

    tokens_perm = to_perm(tokens)
    extra = jnp.broadcast_to(position.astype(BF16)[:, None], (rows, TAIL))
    group = mv.dp_gather(jnp.concatenate([tokens_perm, extra], axis=1)).reshape(TP * rows, width + TAIL)
    group_pos = group[:, width:].astype(F32)
    group_tokens = group[:, :width].astype(F32)
    cotangent = live * out_grad.astype(F32)
    grad_down = mv.dp_gather(cotangent.astype(BF16)).reshape(TP * rows, width)

    tail_full = proj_full[:, -TAIL:]
    gain_one = tail_full[:, 2 * LH].astype(F32)
    gain_two = tail_full[:, 2 * LH + 1].astype(F32)
    taps_full = tail_full[:, 2 * LH + 2 : 2 * LH + 2 + taps.shape[1]]
    taps_full = (
        taps_full.reshape(nf, TP, CONV, -1).transpose(2, 1, 0, 3).reshape(CONV, 2 * key_width + value_width).astype(F32)
    )

    def my_columns(value):
        k, v = LH * DK, LH * DV
        return jnp.concatenate(
            [
                lax.dynamic_slice_in_dim(value, mv.d * k, k, 1),
                lax.dynamic_slice_in_dim(value, key_width + mv.d * k, k, 1),
                lax.dynamic_slice_in_dim(value, 2 * key_width + mv.d * v, v, 1),
            ],
            axis=1,
        )

    conv_mine = jnp.pad(my_columns(taps_full), ((0, 8 - CONV), (0, 0)))
    rate = -jnp.exp(lax.dynamic_slice_in_dim(a_log, mv.d * LH, LH))
    bias = lax.dynamic_slice_in_dim(dt_bias, mv.d * LH, LH)
    prm = jnp.pad(jnp.stack([rate, bias]), ((0, 6), (0, TAIL - LH)))
    gain_head = jnp.broadcast_to(head_gain[None], (8, DV))

    scale_one = lax.rsqrt(jnp.mean(group_tokens * group_tokens, axis=-1, keepdims=True) + EPS)
    normed_one = (group_tokens * scale_one * gain_one).astype(BF16)
    proj = mm(normed_one, proj_full)
    mixed, inv, new = mixer_fwd(proj, group_pos, conv_mine, prm, gain_head)
    mixed_out = mm(mixed, out_full).astype(BF16).reshape(TP, rows, width)
    residual = tokens.astype(F32) + mv.dp_reduce(mixed_out)
    residual_perm = to_perm(residual)
    scale_two = lax.rsqrt(jnp.mean(residual * residual, axis=-1, keepdims=True) + EPS)
    normed_two = mv.dp_gather((residual_perm * scale_two * gain_two).astype(BF16)).reshape(TP * rows, width)
    gate_up = mm(normed_two, gate_up_full)
    gate, up = gate_up[:, :ff], gate_up[:, ff:]
    gate_sig = jax.nn.sigmoid(gate)
    gate_act = gate * gate_sig
    hidden = (gate_act * up).astype(BF16)
    down_out = mm(hidden, down_full).astype(BF16).reshape(TP, rows, width)
    layer_out = (live * (residual + mv.dp_reduce(down_out))).astype(BF16)

    grad_wdown = mm(hidden, grad_down, ((0,), (0,)))
    down_send, down_keep = mv.halves(grad_wdown, 0)
    wdown_grad = mv.reduce(down_send.astype(BF16).reshape(nz, -1, width), down_keep.reshape(nz, -1, width))
    grad_hidden = mm(grad_down, down_full, ((1,), (1,)))
    grad_gate = (grad_hidden * up * gate_sig * (1.0 + gate * (1.0 - gate_sig))).astype(BF16)
    grad_up = (grad_hidden * gate_act).astype(BF16)
    grad_gate_up = jnp.concatenate([grad_gate, grad_up], axis=1)
    two_other, two_mine = mv.halves(normed_two, 1)
    two_shape = (nz, TP * own, 2 * ff)
    two_grad = mv.reduce(
        mm(two_other, grad_gate_up, ((0,), (0,))).astype(BF16).reshape(two_shape),
        mm(two_mine, grad_gate_up, ((0,), (0,))).reshape(two_shape),
    )
    grad_two = mv.dp_reduce(
        mm(grad_gate_up, gate_up_full, ((1,), (1,))).astype(BF16).reshape(TP, rows, width)
    )
    weighted = grad_two * gain_two
    gain_two_part = jnp.sum(grad_two * residual_perm * scale_two, axis=0)
    grad_residual = (
        to_perm(cotangent)
        + scale_two * weighted
        - residual_perm * (scale_two**3 * jnp.mean(residual_perm * weighted, axis=-1, keepdims=True))
    )

    grad_mixed_in = mv.dp_gather(from_perm(grad_residual).astype(BF16)).reshape(TP * rows, width)
    mixed_other, mixed_mine = mv.halves(mixed, 1)
    out_shape = (nz, -1, width)
    wout_grad = mv.reduce(
        mm(mixed_other, grad_mixed_in, ((0,), (0,))).astype(BF16).reshape(out_shape),
        mm(mixed_mine, grad_mixed_in, ((0,), (0,))).reshape(out_shape),
    )
    grad_mixed = mm(grad_mixed_in, out_full, ((1,), (1,)))
    grad_proj, grad_taps, misc = mixer_bwd(
        proj, group_pos, conv_mine, prm, gain_head, inv, new, grad_mixed
    )
    grad_one_part = mm(grad_proj, proj_full, ((1,), (1,)))
    gain_one_part = jnp.sum(grad_one_part * group_tokens * scale_one, axis=0)
    grad_one = mv.dp_reduce(grad_one_part.astype(BF16).reshape(TP, rows, width))

    grad_taps = jnp.sum(grad_taps[:, :CONV], axis=0)
    k, v = LH * DK, LH * DV
    taps_all = jnp.zeros((CONV, 2 * key_width + value_width), F32)
    taps_all = lax.dynamic_update_slice(taps_all, grad_taps[:, :k], (0, mv.d * k))
    taps_all = lax.dynamic_update_slice(taps_all, grad_taps[:, k : 2 * k], (0, key_width + mv.d * k))
    taps_all = lax.dynamic_update_slice(taps_all, grad_taps[:, 2 * k :], (0, 2 * key_width + mv.d * v))
    taps_all = (
        taps_all.reshape(CONV, TP, nf, -1).transpose(2, 1, 0, 3).reshape(width, taps.shape[1])
    )
    small = jnp.concatenate([gain_one_part[:, None], gain_two_part[:, None], taps_all], axis=1)
    small = small.reshape(nz, 2, TP * own, small.shape[1])
    columns = proj.shape[1]
    pads = ((0, 0), (0, 0), (columns - TAIL + 2 * LH, TAIL - 2 * LH - small.shape[3]))

    def small_of(which):
        return jnp.pad(lax.dynamic_index_in_dim(small, which, 1, keepdims=False), pads)

    one_other, one_mine = mv.halves(normed_one, 1)
    one_shape = (nz, TP * own, columns)
    one_grad = mv.reduce(
        (mm(one_other, grad_proj, ((0,), (0,))).reshape(one_shape) + small_of(1 - mv.y)).astype(BF16),
        mm(one_mine, grad_proj, ((0,), (0,))).reshape(one_shape) + small_of(mv.y),
    )

    def to_owner(value):
        return lax.all_to_all(
            value.astype(BF16).reshape(TP, own, value.shape[-1]), "dp", 0, 0, tiled=True
        ).astype(F32)

    def columns_of(value):
        return value.swapaxes(0, 1).reshape(own, -1)

    two_own = to_owner(two_grad)
    w_gate_up_grad = jnp.concatenate([columns_of(two_own[:, :, :ff]), columns_of(two_own[:, :, ff:])], axis=1)
    one_own = to_owner(one_grad)
    w_proj_grad = jnp.concatenate(
        [
            columns_of(one_own[:, :, :k]),
            columns_of(one_own[:, :, k : 2 * k]),
            columns_of(one_own[:, :, 2 * k : 2 * k + v]),
            columns_of(one_own[:, :, 2 * k + v : 2 * k + 2 * v]),
        ],
        axis=1,
    )
    own_tail = one_own[:, :, columns - TAIL :]
    w_decay_grad = jnp.concatenate(
        [columns_of(own_tail[:, :, :LH]), columns_of(own_tail[:, :, LH : 2 * LH])], axis=1
    )
    own_small = jnp.sum(own_tail[:, :, 2 * LH : 2 * LH + 2 + taps.shape[1]], axis=0)
    norm1_gain_grad = own_small[:, 0]
    norm2_gain_grad = own_small[:, 1]
    conv_grad = own_small[:, 2:].reshape(CONV, -1)

    tokens_perm_f = tokens_perm.astype(F32)
    scale_own = scale_one[:rows]
    weighted_one = grad_one * gain_one
    from_one = scale_own * weighted_one - tokens_perm_f * (
        scale_own**3 * jnp.mean(tokens_perm_f * weighted_one, axis=-1, keepdims=True)
    )
    tokens_grad = from_perm((grad_residual + from_one).astype(BF16))

    misc = jnp.sum(misc, axis=0)
    heads_zero = jnp.zeros((HEADS,), F32)
    head_vec = jnp.concatenate(
        [
            lax.dynamic_update_slice(heads_zero, misc[1, :LH], (mv.d * LH,)),
            lax.dynamic_update_slice(heads_zero, misc[2, :LH], (mv.d * LH,)),
            misc[0],
        ]
    )
    head_vec = lax.psum(head_vec, ("dp", "fsdp"))
    return (
        layer_out,
        tokens_grad,
        norm1_gain_grad,
        w_proj_grad,
        w_decay_grad,
        conv_grad,
        wout_grad.reshape(w_out.shape),
        head_vec[:HEADS],
        head_vec[HEADS : 2 * HEADS],
        head_vec[2 * HEADS :],
        norm2_gain_grad,
        w_gate_up_grad,
        wdown_grad.reshape(w_down.shape),
    )


def solution(mesh):
    rows = P(("dp", "fsdp"), None)
    flat = P(("dp", "fsdp"))
    in_specs = (rows, rows, flat, flat, flat, rows, rows, P(None, ("dp", "fsdp")), rows, P(), P(), P(), flat, rows, rows)
    out_specs = (rows, rows, flat, rows, rows, P(None, ("dp", "fsdp")), rows, P(), P(), P(), flat, rows, rows)
    return jax.shard_map(
        partial(local, fsdp_size=mesh.shape["fsdp"]),
        mesh=mesh,
        in_specs=in_specs,
        out_specs=out_specs,
        check_vma=False,
    )
```

time: 6340 us -> 1530 us (0.24)
  waiting for transfers between devices: 4570 us -> 506 us
  other arithmetic: 813 us -> 89.1 us
  matrix products: 558 us -> 185 us
  starting transfers between devices: 0.4 us -> 169 us
  Pallas kernels: 0 us -> 137 us
  local copies, waits for them, and re-layouts: 153 us -> 254 us
    reduce_scatter x4 -> x0, waiting for transfers between devices: 4440 us -> none  [the longest x1 1930 us: local(): lax.psum_scatter(grad_wgate_up, ('dp', 'fsdp'), scatter_dimension=0, tile...]
    another operation x44 -> x11, other arithmetic: 659 us -> 20 us  [the longest x5 14.4 us: dp_gather(): return jnp.stack([value, near, far, self.dp_swap(far, 1)])]
    ppermute x0 -> x64, waiting for transfers between devices: none -> 495 us  [the longest x24 367 us: z_turn(): return lax.ppermute(value, 'fsdp', pairs)]
    dot_general x72 -> x15, matrix products: 525 us -> 185 us  [mm(): lax.dot_general(left, right, (dims, ((), ())), preferred_element_type=F32)]
    psum x0 -> x1, blocking collectives: none -> 169 us  [local(): head_vec = lax.psum(head_vec, ('dp', 'fsdp'))]
    ppermute x0 -> x64, starting transfers between devices: none -> 153 us  [the longest x24 124 us: z_turn(): return lax.ppermute(value, 'fsdp', pairs)]
    pallas_call x0 -> x2, Pallas kernels: none -> 137 us  [the longest x1 96.1 us: mixer_fwd(): pl.pallas_call(mixer_fwd_kernel, grid=(TP,), in_specs=[pl.BlockSpec((rows...]
    all_gather x2 -> x0, blocking collectives: 136 us -> none  [the longest x1 69.6 us: local(): lax.all_gather(w_decay, ('dp', 'fsdp'), axis=0, tiled=True)]
  transfers between devices with their start and end apart: 10 -> 68, of which waited for: 6 -> 20; matrix products, arithmetic and copies ran while one was open for 13% -> 29% of each run, Pallas kernels for 0% -> 9%
where the time goes in v1:
time: 1530 us; the launch traced here: 1510 us
  waiting for transfers between devices  506 us (33%)
  local copies, waits for them, and re-layouts  254 us (17%)
  matrix products  185 us (12%)
  starting transfers between devices  169 us (11%)
  blocking collectives  169 us (11%)
  Pallas kernels  137 us (9%)
  other arithmetic  89.1 us (6%)
    ppermute x24, waiting for transfers between devices, z_turn(): return lax.ppermute(value, 'fsdp', pairs)  367 us
    dot_general x15, matrix products, mm(): lax.dot_general(left, right, (dims, ((), ())), preferred_element_type=F32)  185 us
    psum x1, blocking collectives, local(): head_vec = lax.psum(head_vec, ('dp', 'fsdp'))  169 us
    ppermute x24, starting transfers between devices, z_turn(): return lax.ppermute(value, 'fsdp', pairs)  124 us
    ppermute x20, waiting for transfers between devices, y_swap(): return lax.ppermute(value, 'fsdp', [(i, i ^ 1) for i in range(self.nf)])  112 us
    pallas_call x1, Pallas kernels, mixer_fwd(): pl.pallas_call(mixer_fwd_kernel, grid=(TP,), in_specs=[pl.BlockSpec((rows...  96.1 us
    unnamed x129, local copies, waits for them, and re-layouts  71.4 us
    pallas_call x1, Pallas kernels, mixer_bwd(): pl.pallas_call(mixer_bwd_kernel, grid=(TP,), in_specs=[pl.BlockSpec((rows...  41.2 us
  transfers between devices with their start and end apart: 68, of which 20 were waited for; matrix products, arithmetic and copies ran while one was open for 29% of the time, Pallas kernels for 9%

profile of v1, /device:TPU:0, one launch (start us, length us, event | category | flops | bytes accessed | tf_op | source)
XLA Modules:
  0.0 1512.5 jit_solution(7701362991472195800)
XLA Ops:
  70.8 16.4 %collective-permute-done.39 = bf16[256,2048]{1,0:T(8,128)(2,1)S(1)} collective-permute-done((bf16[256,2048]{1,0:T(8,128)(2,1)S(1)}, bf16[256,2048]{1,0:T(8,128)(2,1)S(1)}, u32[]{:S(2)}, u32[]{:S(2)}) %collective-permute-start.39) | collective-permute-done | bytes 1048608 | tf_op jit(solution)/shard_map/ppermute | solution.py:318
  127.9 17.7 %collective-permute-done.7 = bf16[4,64,3200]{2,1,0:T(8,128)(2,1)} collective-permute-done((bf16[4,64,3200]{2,1,0:T(8,128)(2,1)}, bf16[4,64,3200]{2,1,0:T(8,128)(2,1)}, u32[]{:S(2)}, u32[]{:S(2)}) %collective-permute-start.7) | collective-permute-done | bytes 1638432 | tf_op jit(solution)/shard_map/ppermute | solution.py:325
  145.6 69.4 %collective-permute-done.9 = bf16[4,64,3200]{2,1,0:T(8,128)(2,1)} collective-permute-done((bf16[4,64,3200]{2,1,0:T(8,128)(2,1)}, bf16[4,64,3200]{2,1,0:T(8,128)(2,1)}, u32[]{:S(2)}, u32[]{:S(2)}) %collective-permute-start.9) | collective-permute-done | bytes 1638432 | tf_op jit(solution)/shard_map/ppermute | solution.py:325
  216.6 35.3 %collective-permute-start.23 = (bf16[4,64,2816]{2,1,0:T(8,128)(2,1)S(1)}, bf16[4,64,2816]{2,1,0:T(8,128)(2,1)}, u32[]{:S(2)}, u32[]{:S(2)}) collective-permute-start(bf16[4,64,2816]{2,1,0:T(8,128)(2,1)S(1)} %all-to-all-done.1), channel_id=1, source_target_pairs={{0,2},{1,3},{2,4},{3,5},{4,6},{5,7},{6,0},{7,1},{8,10},{9,11},{10,... | collective-permute-start | bytes 4325384 | tf_op jit(solution)/shard_map/ppermute | solution.py:325
  267.0 16.9 %collective-permute-done.23 = bf16[4,64,2816]{2,1,0:T(8,128)(2,1)} collective-permute-done((bf16[4,64,2816]{2,1,0:T(8,128)(2,1)S(1)}, bf16[4,64,2816]{2,1,0:T(8,128)(2,1)}, u32[]{:S(2)}, u32[]{:S(2)}) %collective-permute-start.23) | collective-permute-done | bytes 1441824 | tf_op jit(solution)/shard_map/ppermute | solution.py:325
  284.4 59.6 %collective-permute-done.25 = bf16[4,64,2816]{2,1,0:T(8,128)(2,1)S(1)} collective-permute-done((bf16[4,64,2816]{2,1,0:T(8,128)(2,1)S(1)}, bf16[4,64,2816]{2,1,0:T(8,128)(2,1)S(1)}, u32[]{:S(2)}, u32[]{:S(2)}) %collective-permute-start.25) | collective-permute-done | bytes 1441824 | tf_op jit(solution)/shard_map/ppermute | solution.py:325
  348.0 31.0 %collective-permute-start.30 = (bf16[176,2048]{1,0:T(8,128)(2,1)}, bf16[176,2048]{1,0:T(8,128)(2,1)}, u32[]{:S(2)}, u32[]{:S(2)}) collective-permute-start(bf16[176,2048]{1,0:T(8,128)(2,1)} %param.29), channel_id=1, source_target_pairs={{0,2},{1,3},{2,4},{3,5},{4,6},{5,7},{6,0},{7,1},{8,10},{9,11},{10,... | collective-permute-start | bytes 2162696 | tf_op jit(solution)/shard_map/ppermute | solution.py:325
  403.9 21.1 %fusion.74.proj_ref = f32[1024,3200]{1,0:T(8,128)} fusion(bf16[1024,2048]{1,0:T(8,128)(2,1)S(1)} %fusion.2, bf16[2048,3200]{1,0:T(8,128)(2,1)} %bitcast.406), kind=kOutput, calls=%fused_computation.244 | convolution fusion | flops 13421772800 | bytes 30408704 | tf_op jit(solution)/shard_map/dot_general | solution.py:25
  426.9 96.1 %mixer_fwd.1 = (bf16[1024,1024]{1,0:T(8,128)(2,1)}, bf16[16,256,256]{2,1,0:T(8,128)(2,1)}, bf16[1024,1024]{1,0:T(8,128)(2,1)}) custom-call(f32[1024,3200]{1,0:T(8,128)} %fusion.74.proj_ref, f32[1024,128]{1,0:T(8,128)} %slice_convert_fusion.1.pos_ref, f32[8,2048]{1,0:T(8,128)} %select_maximum_fusion.conv_ref, f32[8,128]{1,0:T(8,128)} %select_maximum_fusion.2.prm_ref, ...), custom_call_target="tpu_custom_call" | custom-call | flops 30000001024 | bytes 30000000 | tf_op jit(solution)/shard_map/mixer_fwd/pallas_call | solution.py:246
  550.4 22.6 %collective-permute-done.26 = bf16[4,64,2816]{2,1,0:T(8,128)(2,1)S(1)} collective-permute-done((bf16[4,64,2816]{2,1,0:T(8,128)(2,1)S(1)}, bf16[4,64,2816]{2,1,0:T(8,128)(2,1)S(1)}, u32[]{:S(2)}, u32[]{:S(2)}) %collective-permute-start.26) | collective-permute-done | bytes 1441824 | tf_op jit(solution)/shard_map/ppermute | solution.py:321
  579.1 24.8 %collective-permute-done.28 = bf16[4,64,2816]{2,1,0:T(8,128)(2,1)S(1)} collective-permute-done((bf16[4,64,2816]{2,1,0:T(8,128)(2,1)S(1)}, bf16[4,64,2816]{2,1,0:T(8,128)(2,1)S(1)}, u32[]{:S(2)}, u32[]{:S(2)}) %collective-permute-start.28) | collective-permute-done | bytes 1441824 | tf_op jit(solution)/shard_map/ppermute | solution.py:321
  656.8 19.0 %fusion.75 = f32[1024,2816]{1,0:T(8,128)} fusion(bf16[1024,2048]{1,0:T(8,128)(2,1)S(1)} %bitcast.403, bf16[2048,2816]{1,0:T(8,128)(2,1)} %bitcast.408), kind=kOutput, calls=%fused_computation.245 | convolution fusion | flops 11811160064 | bytes 27262976 | tf_op jit(solution)/shard_map/dot_general | solution.py:25
  675.9 15.3 %multiply_convert_fusion.1 = (bf16[1024,1408]{1,0:T(8,128)(2,1)}, bf16[1024,1408]{1,0:T(8,128)(2,1)}, bf16[1024,1408]{1,0:T(8,128)(2,1)}) fusion(f32[1024,2816]{1,0:T(8,128)} %fusion.75, bf16[1024,2048]{1,0:T(8,128)(2,1)} %bitcast.422, bf16[1408,2048]{1,0:T(8,128)(2,1)S(1)} %bitcast.418), kind=kOutput, calls=%fused_computation.19 | convolution fusion | flops 5927206912 | bytes 30146560 | tf_op jit(solution)/shard_map/dot_general | solution.py:25
  703.1 15.8 %convolution_convert_fusion.1 = bf16[1024,2048]{1,0:T(8,128)(2,1)S(1)} fusion(bf16[2048,2816]{1,0:T(8,128)(2,1)} %bitcast.409, bf16[1024,1408]{1,0:T(8,128)(2,1)} %get-tuple-element.122, bf16[1024,1408]{1,0:T(8,128)(2,1)S(1)} %copy-done.50), kind=kOutput, calls=%fused_computation.29 | convolution fusion | flops 11824791552 | bytes 21495808 | tf_op jit(solution)/shard_map/dot_general | solution.py:25
  777.4 21.0 %constant_dynamic-slice_fusion.1 = (bf16[1024,4,1,256]{3,2,1,0:T(2,128)(2,1)}, bf16[1024,4,1,256]{3,2,1,0:T(2,128)(2,1)}, bf16[1024,4,1,256]{3,2,1,0:T(2,128)(2,1)}, bf16[1024,4,1,256]{3,2,1,0:T(2,128)(2,1)}) fusion(bf16[1024,4,2,256]{3,2,1,0:T(2,128)(2,1)} %reshape_reshape.19, s32[]{:T(128)S(6)} %select_n.241, s32[]{:T(128)S(6)} %select_n.242, ...), kind=kLoop, calls=%fused_computation.192 | loop fusion | bytes 16777224 | tf_op jit(solution)/shard_map/jit(dynamic_index_in_dim)/dynamic_slice | solution.py:363
  825.0 18.8 %collective-permute-start.63 = (bf16[176,2048]{1,0:T(8,128)(2,1)}, bf16[176,2048]{1,0:T(8,128)(2,1)}, u32[]{:S(2)}, u32[]{:S(2)}) collective-permute-start(bf16[176,2048]{1,0:T(8,128)(2,1)} %get-tuple-element.151), channel_id=1, source_target_pairs={{0,6},{1,7},{2,0},{3,1},{4,2},{5,3},{6,4},{7,5},{8,14},{9,15},{10,... | collective-permute-start | bytes 2162696 | tf_op jit(solution)/shard_map/ppermute | solution.py:325
  927.9 41.2 %mixer_bwd.1 = (bf16[1024,3200]{1,0:T(8,128)(2,1)}, f32[4,8,2048]{2,1,0:T(8,128)}, f32[4,8,256]{2,1,0:T(8,128)}) custom-call(f32[1024,3200]{1,0:T(8,128)} %fusion.74.proj_ref, f32[1024,128]{1,0:T(8,128)} %slice_convert_fusion.1.pos_ref, f32[8,2048]{1,0:T(8,128)} %select_maximum_fusion.conv_ref, f32[8,128]{1,0:T(8,128)} %select_maximum_fusion.2.prm_ref, ...), custom_call_target="tpu_custom_call" | custom-call | flops 49999998976 | bytes 40000000 | tf_op jit(solution)/shard_map/mixer_bwd/pallas_call | solution.py:275
  971.0 21.6 %fusion.4 = (f32[2048]{0:T(1024)S(1)}, bf16[1024,2048]{1,0:T(8,128)(2,1)}) fusion(f32[1024]{0:T(1024)S(1)} %copy-done.38, bf16[1024,2176]{1,0:T(8,128)(2,1)} %bitcast.397, bf16[1024,3200]{1,0:T(8,128)(2,1)} %get-tuple-element.28, bf16[2048,3200]{1,0:T(8,128)(2,1)} %bitcast.407), kind=kOutput, calls=%fused_computation.10 | convolution fusion | flops 13432256512 | bytes 28061696 | tf_op jit(solution)/shard_map/dot_general | solution.py:25
  1005.8 20.9 %collective-permute-done.56 = bf16[4,256,2816]{2,1,0:T(8,128)(2,1)} collective-permute-done((bf16[4,256,2816]{2,1,0:T(8,128)(2,1)}, bf16[4,256,2816]{2,1,0:T(8,128)(2,1)}, u32[]{:S(2)}, u32[]{:S(2)}) %collective-permute-start.56) | collective-permute-done | bytes 5767200 | tf_op jit(solution)/shard_map/ppermute | solution.py:321
  1062.0 21.5 %collective-permute-done.59 = bf16[256,2816]{1,0:T(8,128)(2,1)} collective-permute-done((bf16[256,2816]{1,0:T(8,128)(2,1)S(1)}, bf16[256,2816]{1,0:T(8,128)(2,1)}, u32[]{:S(2)}, u32[]{:S(2)}) %collective-permute-start.59) | collective-permute-done | bytes 1441824 | tf_op jit(solution)/shard_map/ppermute | solution.py:325
  1083.6 169.0 %psum.7 = f32[288]{0:T(512)S(1)} all-reduce(f32[288]{0:T(512)S(1)} %pad_maximum_fusion.19), channel_id=1, replica_groups=mesh['dp'=4,'fsdp'=8] {'dp','fsdp'}, use_global_device_ids=true, to_apply=%region_10.11 | all-reduce | flops 288 | bytes 2304 | tf_op jit(solution)/shard_map/psum | solution.py:608
  1282.8 32.5 %collective-permute-done.54 = bf16[128,2048]{1,0:T(8,128)(2,1)S(1)} collective-permute-done((bf16[128,2048]{1,0:T(8,128)(2,1)S(1)}, bf16[128,2048]{1,0:T(8,128)(2,1)S(1)}, u32[]{:S(2)}, u32[]{:S(2)}) %collective-permute-start.54) | collective-permute-done | bytes 524320 | tf_op jit(solution)/shard_map/ppermute | solution.py:325
  1339.5 31.0 %collective-permute-done.51 = bf16[256,3200]{1,0:T(8,128)(2,1)S(1)} collective-permute-done((bf16[256,3200]{1,0:T(8,128)(2,1)S(1)}, bf16[256,3200]{1,0:T(8,128)(2,1)S(1)}, u32[]{:S(2)}, u32[]{:S(2)}) %collective-permute-start.51) | collective-permute-done | bytes 1638432 | tf_op jit(solution)/shard_map/ppermute | solution.py:325
  1370.5 105.5 %collective-permute-done.50 = bf16[256,3200]{1,0:T(8,128)(2,1)S(1)} collective-permute-done((bf16[256,3200]{1,0:T(8,128)(2,1)S(1)}, bf16[256,3200]{1,0:T(8,128)(2,1)S(1)}, u32[]{:S(2)}, u32[]{:S(2)}) %collective-permute-start.50) | collective-permute-done | bytes 1638432 | tf_op jit(solution)/shard_map/ppermute | solution.py:325
  (448 shorter events, 566.2 us)
Async XLA Ops:
  94.9 159.4 %collective-permute-start.6 = (bf16[4,64,3200]{2,1,0:T(8,128)(2,1)}, bf16[4,64,3200]{2,1,0:T(8,128)(2,1)}, u32[]{:S(2)}, u32[]{:S(2)}) collective-permute-start(bf16[4,64,3200]{2,1,0:T(8,128)(2,1)} %all-to-all-done), channel_id=1, source_target_pairs={{0,1},{1,0},{2,3},{3,2},{4,5},{5,4},{6,7},{7,6},{8,9},{9,8},{10,11... | collective-permute-start | bytes 4915208 | tf_op jit(solution)/shard_map/ppermute | solution.py:321
  105.3 109.7 %collective-permute-start.9 = (bf16[4,64,3200]{2,1,0:T(8,128)(2,1)}, bf16[4,64,3200]{2,1,0:T(8,128)(2,1)}, u32[]{:S(2)}, u32[]{:S(2)}) collective-permute-start(bf16[4,64,3200]{2,1,0:T(8,128)(2,1)} %all-to-all-done), channel_id=1, source_target_pairs={{0,4},{1,5},{2,6},{3,7},{4,0},{5,1},{6,2},{7,3},{8,12},{9,13},{10,... | collective-permute-start | bytes 4915208 | tf_op jit(solution)/shard_map/ppermute | solution.py:325
  105.7 109.3 %collective-permute-start.11 = (bf16[4,64,3200]{2,1,0:T(8,128)(2,1)}, bf16[4,64,3200]{2,1,0:T(8,128)(2,1)}, u32[]{:S(2)}, u32[]{:S(2)}) collective-permute-start(bf16[4,64,3200]{2,1,0:T(8,128)(2,1)} %all-to-all-done), channel_id=1, source_target_pairs={{0,6},{1,7},{2,0},{3,1},{4,2},{5,3},{6,4},{7,5},{8,14},{9,15},{10,... | collective-permute-start | bytes 4915208 | tf_op jit(solution)/shard_map/ppermute | solution.py:325
  215.0 133.0 %collective-permute-start.22 = (bf16[4,64,2816]{2,1,0:T(8,128)(2,1)S(1)}, bf16[4,64,2816]{2,1,0:T(8,128)(2,1)S(1)}, u32[]{:S(2)}, u32[]{:S(2)}) collective-permute-start(bf16[4,64,2816]{2,1,0:T(8,128)(2,1)S(1)} %all-to-all-done.1), channel_id=1, source_target_pairs={{0,1},{1,0},{2,3},{3,2},{4,5},{5,4},{6,7},{7,6},{8,9},{9,8},{10,11... | collective-permute-start | bytes 4325384 | tf_op jit(solution)/shard_map/ppermute | solution.py:321
  251.8 92.2 %collective-permute-start.25 = (bf16[4,64,2816]{2,1,0:T(8,128)(2,1)S(1)}, bf16[4,64,2816]{2,1,0:T(8,128)(2,1)S(1)}, u32[]{:S(2)}, u32[]{:S(2)}) collective-permute-start(bf16[4,64,2816]{2,1,0:T(8,128)(2,1)S(1)} %all-to-all-done.1), channel_id=1, source_target_pairs={{0,4},{1,5},{2,6},{3,7},{4,0},{5,1},{6,2},{7,3},{8,12},{9,13},{10,... | collective-permute-start | bytes 4325384 | tf_op jit(solution)/shard_map/ppermute | solution.py:325
  251.8 92.8 %collective-permute-start.27 = (bf16[4,64,2816]{2,1,0:T(8,128)(2,1)S(1)}, bf16[4,64,2816]{2,1,0:T(8,128)(2,1)S(1)}, u32[]{:S(2)}, u32[]{:S(2)}) collective-permute-start(bf16[4,64,2816]{2,1,0:T(8,128)(2,1)S(1)} %all-to-all-done.1), channel_id=1, source_target_pairs={{0,6},{1,7},{2,0},{3,1},{4,2},{5,3},{6,4},{7,5},{8,14},{9,15},{10,... | collective-permute-start | bytes 4325384 | tf_op jit(solution)/shard_map/ppermute | solution.py:325
  254.3 128.6 %collective-permute-start.8 = (bf16[4,64,3200]{2,1,0:T(8,128)(2,1)}, bf16[4,64,3200]{2,1,0:T(8,128)(2,1)S(1)}, u32[]{:S(2)}, u32[]{:S(2)}) collective-permute-start(bf16[4,64,3200]{2,1,0:T(8,128)(2,1)} %collective-permute-done.7), channel_id=1, source_target_pairs={{0,1},{1,0},{2,3},{3,2},{4,5},{5,4},{6,7},{7,6},{8,9},{9,8},{10,11... | collective-permute-start | bytes 4915208 | tf_op jit(solution)/shard_map/ppermute | solution.py:321
  284.0 106.3 %collective-permute-start.10 = (bf16[4,64,3200]{2,1,0:T(8,128)(2,1)}, bf16[4,64,3200]{2,1,0:T(8,128)(2,1)S(1)}, u32[]{:S(2)}, u32[]{:S(2)}) collective-permute-start(bf16[4,64,3200]{2,1,0:T(8,128)(2,1)} %collective-permute-done.9), channel_id=1, source_target_pairs={{0,1},{1,0},{2,3},{3,2},{4,5},{5,4},{6,7},{7,6},{8,9},{9,8},{10,11... | collective-permute-start | bytes 4915208 | tf_op jit(solution)/shard_map/ppermute | solution.py:321
  344.7 192.6 %collective-permute-start.29 = (bf16[176,2048]{1,0:T(8,128)(2,1)}, bf16[176,2048]{1,0:T(8,128)(2,1)}, u32[]{:S(2)}, u32[]{:S(2)}) collective-permute-start(bf16[176,2048]{1,0:T(8,128)(2,1)} %param.29), channel_id=1, source_target_pairs={{0,1},{1,0},{2,3},{3,2},{4,5},{5,4},{6,7},{7,6},{8,9},{9,8},{10,11... | collective-permute-start | bytes 2162696 | tf_op jit(solution)/shard_map/ppermute | solution.py:321
  348.0 194.0 %collective-permute-start.30 = (bf16[176,2048]{1,0:T(8,128)(2,1)}, bf16[176,2048]{1,0:T(8,128)(2,1)}, u32[]{:S(2)}, u32[]{:S(2)}) collective-permute-start(bf16[176,2048]{1,0:T(8,128)(2,1)} %param.29), channel_id=1, source_target_pairs={{0,2},{1,3},{2,4},{3,5},{4,6},{5,7},{6,0},{7,1},{8,10},{9,11},{10,... | collective-permute-start | bytes 2162696 | tf_op jit(solution)/shard_map/ppermute | solution.py:325
  382.9 165.5 %collective-permute-start.32 = (bf16[176,2048]{1,0:T(8,128)(2,1)}, bf16[176,2048]{1,0:T(8,128)(2,1)}, u32[]{:S(2)}, u32[]{:S(2)}) collective-permute-start(bf16[176,2048]{1,0:T(8,128)(2,1)} %param.29), channel_id=1, source_target_pairs={{0,4},{1,5},{2,6},{3,7},{4,0},{5,1},{6,2},{7,3},{8,12},{9,13},{10,... | collective-permute-start | bytes 2162696 | tf_op jit(solution)/shard_map/ppermute | solution.py:325
  390.3 159.6 %collective-permute-start.34 = (bf16[176,2048]{1,0:T(8,128)(2,1)}, bf16[176,2048]{1,0:T(8,128)(2,1)}, u32[]{:S(2)}, u32[]{:S(2)}) collective-permute-start(bf16[176,2048]{1,0:T(8,128)(2,1)} %param.29), channel_id=1, source_target_pairs={{0,6},{1,7},{2,0},{3,1},{4,2},{5,3},{6,4},{7,5},{8,14},{9,15},{10,... | collective-permute-start | bytes 2162696 | tf_op jit(solution)/shard_map/ppermute | solution.py:325
  395.4 149.2 %collective-permute-start.24 = (bf16[4,64,2816]{2,1,0:T(8,128)(2,1)}, bf16[4,64,2816]{2,1,0:T(8,128)(2,1)}, u32[]{:S(2)}, u32[]{:S(2)}) collective-permute-start(bf16[4,64,2816]{2,1,0:T(8,128)(2,1)} %collective-permute-done.23), channel_id=1, source_target_pairs={{0,1},{1,0},{2,3},{3,2},{4,5},{5,4},{6,7},{7,6},{8,9},{9,8},{10,11... | collective-permute-start | bytes 4325384 | tf_op jit(solution)/shard_map/ppermute | solution.py:321
  549.9 85.0 %collective-permute-start.33 = (bf16[176,2048]{1,0:T(8,128)(2,1)}, bf16[176,2048]{1,0:T(8,128)(2,1)}, u32[]{:S(2)}, u32[]{:S(2)}) collective-permute-start(bf16[176,2048]{1,0:T(8,128)(2,1)} %collective-permute-done.32), channel_id=1, source_target_pairs={{0,1},{1,0},{2,3},{3,2},{4,5},{5,4},{6,7},{7,6},{8,9},{9,8},{10,11... | collective-permute-start | bytes 2162696 | tf_op jit(solution)/shard_map/ppermute | solution.py:321
  721.5 87.6 %collective-permute-start.41 = (bf16[2,256,2048]{2,1,0:T(8,128)(2,1)}, bf16[2,256,2048]{2,1,0:T(8,128)(2,1)}, u32[]{:S(2)}, u32[]{:S(2)}) collective-permute-start(bf16[2,256,2048]{2,1,0:T(8,128)(2,1)} %pad_maximum_fusion.9), channel_id=1, source_target_pairs={{0,8},{8,0},{16,24},{24,16},{1,9},{9,1},{17,25},{25,17},{2,10},{10... | collective-permute-start | bytes 6291464 | tf_op jit(solution)/shard_map/ppermute | solution.py:318
  899.2 127.5 %collective-permute-start.56 = (bf16[4,256,2816]{2,1,0:T(8,128)(2,1)}, bf16[4,256,2816]{2,1,0:T(8,128)(2,1)}, u32[]{:S(2)}, u32[]{:S(2)}) collective-permute-start(bf16[4,256,2816]{2,1,0:T(8,128)(2,1)} %bitcast.468), channel_id=1, source_target_pairs={{0,1},{1,0},{2,3},{3,2},{4,5},{5,4},{6,7},{7,6},{8,9},{9,8},{10,11... | collective-permute-start | bytes 17301512 | tf_op jit(solution)/shard_map/ppermute | solution.py:321
  1005.1 311.8 %collective-permute-start.48 = (bf16[4,256,3200]{2,1,0:T(8,128)(2,1)}, bf16[4,256,3200]{2,1,0:T(8,128)(2,1)}, u32[]{:S(2)}, u32[]{:S(2)}) collective-permute-start(bf16[4,256,3200]{2,1,0:T(8,128)(2,1)} %add_convert_fusion), channel_id=1, source_target_pairs={{0,1},{1,0},{2,3},{3,2},{4,5},{5,4},{6,7},{7,6},{8,9},{9,8},{10,11... | collective-permute-start | bytes 19660808 | tf_op jit(solution)/shard_map/ppermute | solution.py:321
  1056.1 206.1 %collective-permute-start.52 = (bf16[4,128,2048]{2,1,0:T(8,128)(2,1)}, bf16[4,128,2048]{2,1,0:T(8,128)(2,1)}, u32[]{:S(2)}, u32[]{:S(2)}) collective-permute-start(bf16[4,128,2048]{2,1,0:T(8,128)(2,1)} %bitcast.469), channel_id=1, source_target_pairs={{0,1},{1,0},{2,3},{3,2},{4,5},{5,4},{6,7},{7,6},{8,9},{9,8},{10,11... | collective-permute-start | bytes 6291464 | tf_op jit(solution)/shard_map/ppermute | solution.py:321
  1056.7 197.2 %collective-permute-start.58 = (bf16[256,2816]{1,0:T(8,128)(2,1)}, bf16[256,2816]{1,0:T(8,128)(2,1)}, u32[]{:S(2)}, u32[]{:S(2)}) collective-permute-start(bf16[256,2816]{1,0:T(8,128)(2,1)} %get-tuple-element.131), channel_id=1, source_target_pairs={{0,4},{1,5},{2,6},{3,7},{4,0},{5,1},{6,2},{7,3},{8,12},{9,13},{10,... | collective-permute-start | bytes 4325384 | tf_op jit(solution)/shard_map/ppermute | solution.py:325
  1056.7 197.1 %collective-permute-start.57 = (bf16[256,2816]{1,0:T(8,128)(2,1)S(1)}, bf16[256,2816]{1,0:T(8,128)(2,1)}, u32[]{:S(2)}, u32[]{:S(2)}) collective-permute-start(bf16[256,2816]{1,0:T(8,128)(2,1)S(1)} %get-tuple-element.129), channel_id=1, source_target_pairs={{0,2},{1,3},{2,4},{3,5},{4,6},{5,7},{6,0},{7,1},{8,10},{9,11},{10,... | collective-permute-start | bytes 4325384 | tf_op jit(solution)/shard_map/ppermute | solution.py:325
  1083.6 186.6 %collective-permute-start.46 = (bf16[2,256,2048]{2,1,0:T(8,128)(2,1)}, bf16[2,256,2048]{2,1,0:T(8,128)(2,1)S(1)}, u32[]{:S(2)}, u32[]{:S(2)}) collective-permute-start(bf16[2,256,2048]{2,1,0:T(8,128)(2,1)} %pad_maximum_fusion.10), channel_id=1, source_target_pairs={{0,8},{8,0},{16,24},{24,16},{1,9},{9,1},{17,25},{25,17},{2,10},{10... | collective-permute-start | bytes 6291464 | tf_op jit(solution)/shard_map/ppermute | solution.py:318
  1273.5 211.1 %collective-permute-start.47 = (bf16[256,2048]{1,0:T(8,128)(2,1)}, bf16[256,2048]{1,0:T(8,128)(2,1)}, u32[]{:S(2)}, u32[]{:S(2)}) collective-permute-start(bf16[256,2048]{1,0:T(8,128)(2,1)} %fusion.26), channel_id=1, source_target_pairs={{0,16},{8,24},{16,0},{24,8},{1,17},{9,25},{17,1},{25,9},{2,18},{10... | collective-permute-start | bytes 3145736 | tf_op jit(solution)/shard_map/ppermute | solution.py:318
  1332.7 143.3 %collective-permute-start.50 = (bf16[256,3200]{1,0:T(8,128)(2,1)S(1)}, bf16[256,3200]{1,0:T(8,128)(2,1)S(1)}, u32[]{:S(2)}, u32[]{:S(2)}) collective-permute-start(bf16[256,3200]{1,0:T(8,128)(2,1)S(1)} %get-tuple-element.128), channel_id=1, source_target_pairs={{0,4},{1,5},{2,6},{3,7},{4,0},{5,1},{6,2},{7,3},{8,12},{9,13},{10,... | collective-permute-start | bytes 4915208 | tf_op jit(solution)/shard_map/ppermute | solution.py:325
  1335.1 140.9 %collective-permute-start.49 = (bf16[256,3200]{1,0:T(8,128)(2,1)S(1)}, bf16[256,3200]{1,0:T(8,128)(2,1)S(1)}, u32[]{:S(2)}, u32[]{:S(2)}) collective-permute-start(bf16[256,3200]{1,0:T(8,128)(2,1)S(1)} %get-tuple-element.126), channel_id=1, source_target_pairs={{0,2},{1,3},{2,4},{3,5},{4,6},{5,7},{6,0},{7,1},{8,10},{9,11},{10,... | collective-permute-start | bytes 4915208 | tf_op jit(solution)/shard_map/ppermute | solution.py:325
  (100 other events, 2830.5 us)

commit v2 on v1

v2 whole, which is shorter than its diff:
```python
from functools import partial

import jax
import jax.numpy as jnp
from jax import lax
from jax.experimental import pallas as pl
from jax.experimental.pallas import tpu as pltpu
from jax.sharding import PartitionSpec as P

HEADS = 16
DK = 128
DV = 256
CONV = 4
BLOCK = 64
TP = 4
LH = HEADS // TP
TAIL = 128
EPS = 1e-06
HIGH = lax.Precision.HIGHEST
F32 = jnp.float32
BF16 = jnp.bfloat16


def mm(left, right, dims=((1,), (0,))):
    return lax.dot_general(left, right, (dims, ((), ())), preferred_element_type=F32)


def mmb(left, right, dims=((1,), (0,))):
    return mm(left.astype(BF16), right.astype(BF16), dims)


def mm3(left, right, dims=((1,), (0,))):
    left_hi = left.astype(BF16)
    right_hi = right.astype(BF16)
    left_lo = (left - left_hi.astype(F32)).astype(BF16)
    right_lo = (right - right_hi.astype(F32)).astype(BF16)
    return mm(left_hi, right_hi, dims) + (mm(left_hi, right_lo, dims) + mm(left_lo, right_hi, dims))


def mmx(left, right, dims=((1,), (0,))):
    return lax.dot_general(left, right, (dims, ((), ())), precision=HIGH, preferred_element_type=F32)


def sigmoid(v):
    return 1.0 / (1.0 + jnp.exp(-v))


def conv_rows(raw, taps, pos):
    total = raw * taps[CONV - 1 : CONV]
    for lag in range(1, CONV):
        moved = pltpu.roll(raw, lag, 0)
        total = total + jnp.where(pos >= lag, moved, 0.0) * taps[CONV - 1 - lag : CONV - lag]
    return total


def conv_back(grad, raw, taps, pos):
    rows = raw.shape[0]
    total = grad * taps[CONV - 1 : CONV]
    sums = [jnp.sum(grad * raw, axis=0, keepdims=True)]
    for lag in range(1, CONV):
        kept = jnp.where(pos >= lag, grad, 0.0)
        total = total + pltpu.roll(kept, rows - lag, 0) * taps[CONV - 1 - lag : CONV - lag]
        sums.append(jnp.sum(kept * pltpu.roll(raw, lag, 0), axis=0, keepdims=True))
    return total, sums[::-1]


def unit(v, scale):
    inv = lax.rsqrt(jnp.sum(v * v, axis=-1, keepdims=True) + EPS)
    return v * (inv * scale), inv


def unit_back(grad, v, inv, scale):
    g = grad * scale
    return inv * g - v * (inv * inv * inv * jnp.sum(v * g, axis=-1, keepdims=True))


def silu_back(grad, pre, sig):
    return grad * (sig * (1.0 + pre * (1.0 - sig)))


def group_terms(tail_ref, prm_ref, pos_ref):
    rows = tail_ref.shape[0]
    pos = pos_ref[:, 0:1].astype(jnp.int32)
    row_i = lax.broadcasted_iota(jnp.int32, (rows, rows), 0)
    row_j = lax.broadcasted_iota(jnp.int32, (rows, rows), 1)
    lower = (row_j <= row_i) & (row_j >= row_i - pos)
    raw = tail_ref[...]
    shifted = raw + prm_ref[1:2]
    soft = jnp.maximum(shifted, 0.0) + jnp.log1p(jnp.exp(-jnp.abs(shifted)))
    log_decay = prm_ref[0:1] * soft
    beta = sigmoid(raw)
    lower_f = lower.astype(F32)
    cum = mmx(lower_f, log_decay)
    return pos, row_i, row_j, lower, lower_f, raw, shifted, log_decay, beta, cum, cum.T


def head_slices(head):
    key_width = LH * DK
    return (
        slice(head * DK, (head + 1) * DK),
        slice(key_width + head * DK, key_width + (head + 1) * DK),
        slice(2 * key_width + head * DV, 2 * key_width + (head + 1) * DV),
        slice(2 * key_width + (LH + head) * DV, 2 * key_width + (LH + head + 1) * DV),
    )


def mixer_fwd_kernel(proj_ref, pos_ref, conv_ref, prm_ref, gain_ref, mixed_ref, inv_ref, new_ref):
    width = proj_ref.shape[1]
    tail_ref = proj_ref.at[:, width - TAIL :]
    pos, row_i, row_j, lower, _, _, _, _, beta_all, cum, cum_t = group_terms(tail_ref, prm_ref, pos_ref)
    strict = lower & (row_j < row_i)
    bits = row_i ^ row_j
    eye = (bits == 0).astype(F32)
    lows, attends, values = [], [], []
    for head in range(LH):
        sq, sk, sv, _ = head_slices(head)
        q_pre = conv_rows(proj_ref[:, sq], conv_ref[:, sq], pos)
        k_pre = conv_rows(proj_ref[:, sk], conv_ref[:, sk], pos)
        v_pre = conv_rows(proj_ref[:, sv], conv_ref[:, sv], pos)
        query, _ = unit(q_pre * sigmoid(q_pre), DK**-0.5)
        key, _ = unit(k_pre * sigmoid(k_pre), 1.0)
        beta = beta_all[:, LH + head : LH + head + 1]
        values.append(beta * (v_pre * sigmoid(v_pre)))
        gap = cum[:, head : head + 1] - cum_t[head : head + 1, :]
        decay = jnp.where(lower, jnp.exp(gap), 0.0)
        attends.append(mm3(query, key, ((1,), (1,))) * decay)
        lows.append(jnp.where(strict, beta * mm3(key, key, ((1,), (1,))) * decay, 0.0))
    invs = [eye - jnp.where(bits == 1, low, 0.0) for low in lows]
    step = 1
    while (2 << step) <= proj_ref.shape[0]:
        keep = (bits >> step) == 1
        parts = [mm3(jnp.where(keep, low, 0.0), inv) for low, inv in zip(lows, invs)]
        invs = [inv - mm3(inv, part) for inv, part in zip(invs, parts)]
        step += 1
    news = [mm3(inv, value) for inv, value in zip(invs, values)]
    mixes = [mm3(attend, new) for attend, new in zip(attends, news)]
    for head in range(LH):
        mix = mixes[head]
        scale = lax.rsqrt(jnp.mean(mix * mix, axis=-1, keepdims=True) + EPS)
        gate = proj_ref[:, head_slices(head)[3]]
        out = mix * scale * gain_ref[0:1] * (gate * sigmoid(gate))
        mixed_ref[:, head * DV : (head + 1) * DV] = out.astype(BF16)
        inv_ref[head] = invs[head]
        new_ref[:, head * DV : (head + 1) * DV] = news[head]


def mixer_bwd_kernel(
    proj_ref, pos_ref, conv_ref, prm_ref, gain_ref, inv_ref, new_ref, gmix_ref, gproj_ref, gconv_ref, misc_ref
):
    width = proj_ref.shape[1]
    rows = proj_ref.shape[0]
    tail_ref = proj_ref.at[:, width - TAIL :]
    pos, row_i, row_j, lower, lower_f, raw, shifted, log_decay, beta_all, cum, cum_t = group_terms(
        tail_ref, prm_ref, pos_ref
    )
    strict = lower & (row_j < row_i)
    lane = lax.broadcasted_iota(jnp.int32, (rows, TAIL), 1)
    ones = jnp.ones((rows, TAIL), F32)
    grad_cum = jnp.zeros((rows, TAIL), F32)
    grad_beta_all = jnp.zeros((rows, TAIL), F32)
    gain_sum = jnp.zeros((1, DV), F32)
    gconv_ref[...] = jnp.zeros_like(gconv_ref)
    misc_ref[...] = jnp.zeros_like(misc_ref)
    for head in range(LH):
        sq, sk, sv, sg = head_slices(head)
        q_raw, k_raw, v_raw = proj_ref[:, sq], proj_ref[:, sk], proj_ref[:, sv]
        q_pre = conv_rows(q_raw, conv_ref[:, sq], pos)
        k_pre = conv_rows(k_raw, conv_ref[:, sk], pos)
        v_pre = conv_rows(v_raw, conv_ref[:, sv], pos)
        q_sig, k_sig, v_sig = sigmoid(q_pre), sigmoid(k_pre), sigmoid(v_pre)
        q_act, k_act, value = q_pre * q_sig, k_pre * k_sig, v_pre * v_sig
        query, q_inv = unit(q_act, DK**-0.5)
        key, k_inv = unit(k_act, 1.0)
        query_b, key_b = query, key
        beta = beta_all[:, LH + head : LH + head + 1]
        gap = cum[:, head : head + 1] - cum_t[head : head + 1, :]
        decay = jnp.where(lower, jnp.exp(gap), 0.0)
        pair = mm3(key_b, key_b, ((1,), (1,)))
        query_pair = mm3(query_b, key_b, ((1,), (1,)))
        attend = query_pair * decay
        inv = inv_ref[head]
        new = new_ref[:, head * DV : (head + 1) * DV]
        mix = mm3(attend, new)
        scale = lax.rsqrt(jnp.mean(mix * mix, axis=-1, keepdims=True) + EPS)
        gate = proj_ref[:, sg]
        gate_sig = sigmoid(gate)
        grad_out = gmix_ref[:, head * DV : (head + 1) * DV]
        unscaled = mix * scale
        grad_norm = grad_out * (gate * gate_sig)
        grad_gate = silu_back(grad_out * unscaled * gain_ref[0:1], gate, gate_sig)
        gain_sum = gain_sum + jnp.sum(grad_norm * unscaled, axis=0, keepdims=True)
        weighted = grad_norm * gain_ref[0:1]
        grad_mix = scale * weighted - mix * (
            scale * scale * scale * jnp.mean(mix * weighted, axis=-1, keepdims=True)
        )
        grad_mix_b = grad_mix
        grad_new = mm3(attend, grad_mix_b, ((0,), (0,)))
        grad_attend = mm3(grad_mix_b, new, ((1,), (1,)))
        grad_rhs = mm3(inv, grad_new, ((0,), (0,)))
        grad_low = -mm3(grad_rhs, new, ((1,), (1,)))
        grad_value = beta * grad_rhs
        low_decay = jnp.where(strict, grad_low * decay, 0.0)
        low_pair = low_decay * pair
        grad_beta = jnp.sum(grad_rhs * value, axis=-1, keepdims=True) + jnp.sum(
            low_pair, axis=-1, keepdims=True
        )
        grad_pair = beta * low_decay
        grad_query_pair = grad_attend * decay
        both = beta * low_pair + grad_query_pair * query_pair
        column = jnp.sum(both, axis=-1, keepdims=True) - mmx(both, ones, ((0,), (0,)))
        grad_cum = jnp.where(lane == head, column, grad_cum)
        grad_beta_all = jnp.where(lane == LH + head, grad_beta, grad_beta_all)
        grad_pair_b = grad_pair
        grad_qp_b = grad_query_pair
        grad_query = mm3(grad_qp_b, key_b)
        grad_key = (
            mm3(grad_qp_b, query_b, ((0,), (0,))) + mm3(grad_pair_b, key_b) + mm3(grad_pair_b, key_b, ((0,), (0,)))
        )
        grad_q = silu_back(unit_back(grad_query, q_act, q_inv, DK**-0.5), q_pre, q_sig)
        grad_k = silu_back(unit_back(grad_key, k_act, k_inv, 1.0), k_pre, k_sig)
        grad_v = silu_back(grad_value, v_pre, v_sig)
        for grad, part, where in ((grad_q, q_raw, sq), (grad_k, k_raw, sk), (grad_v, v_raw, sv)):
            moved, sums = conv_back(grad, part, conv_ref[:, where], pos)
            gproj_ref[:, where] = moved.astype(BF16)
            for tap in range(CONV):
                gconv_ref[0, tap : tap + 1, where] = sums[tap]
        gproj_ref[:, sg] = grad_gate.astype(BF16)
    grad_log = mmx(lower_f, grad_cum, ((0,), (0,)))
    grad_step = grad_log * prm_ref[0:1] * sigmoid(shifted)
    grad_tail = grad_step + grad_beta_all * beta_all * (1.0 - beta_all)
    gproj_ref[:, width - TAIL :] = grad_tail.astype(BF16)
    misc_ref[0, 0:1, :] = gain_sum
    misc_ref[0, 1:2, 0:TAIL] = jnp.sum(grad_log * log_decay, axis=0, keepdims=True)
    misc_ref[0, 2:3, 0:TAIL] = jnp.sum(grad_step, axis=0, keepdims=True)


VMEM_LIMIT = 56 * 1024 * 1024


def mixer_fwd(proj, pos, conv, prm, gain):
    total, width = proj.shape
    rows = total // TP
    return pl.pallas_call(
        mixer_fwd_kernel,
        grid=(TP,),
        in_specs=[
            pl.BlockSpec((rows, width), lambda g: (g, 0)),
            pl.BlockSpec((rows, TAIL), lambda g: (g, 0)),
            pl.BlockSpec(conv.shape, lambda g: (0, 0)),
            pl.BlockSpec(prm.shape, lambda g: (0, 0)),
            pl.BlockSpec(gain.shape, lambda g: (0, 0)),
        ],
        out_specs=[
            pl.BlockSpec((rows, LH * DV), lambda g: (g, 0)),
            pl.BlockSpec((LH, rows, rows), lambda g: (g, 0, 0)),
            pl.BlockSpec((rows, LH * DV), lambda g: (g, 0)),
        ],
        out_shape=[
            jax.ShapeDtypeStruct((total, LH * DV), BF16),
            jax.ShapeDtypeStruct((TP * LH, rows, rows), F32),
            jax.ShapeDtypeStruct((total, LH * DV), F32),
        ],
        compiler_params=pltpu.CompilerParams(vmem_limit_bytes=VMEM_LIMIT),
        cost_estimate=pl.CostEstimate(flops=30_000_000_000, bytes_accessed=30_000_000, transcendentals=5_000_000),
        name="mixer_fwd",
    )(proj, pos, conv, prm, gain)


def mixer_bwd(proj, pos, conv, prm, gain, inv, new, gmix):
    total, width = proj.shape
    rows = total // TP
    return pl.pallas_call(
        mixer_bwd_kernel,
        grid=(TP,),
        in_specs=[
            pl.BlockSpec((rows, width), lambda g: (g, 0)),
            pl.BlockSpec((rows, TAIL), lambda g: (g, 0)),
            pl.BlockSpec(conv.shape, lambda g: (0, 0)),
            pl.BlockSpec(prm.shape, lambda g: (0, 0)),
            pl.BlockSpec(gain.shape, lambda g: (0, 0)),
            pl.BlockSpec((LH, rows, rows), lambda g: (g, 0, 0)),
            pl.BlockSpec((rows, LH * DV), lambda g: (g, 0)),
            pl.BlockSpec((rows, LH * DV), lambda g: (g, 0)),
        ],
        out_specs=[
            pl.BlockSpec((rows, width), lambda g: (g, 0)),
            pl.BlockSpec((1, 8, conv.shape[1]), lambda g: (g, 0, 0)),
            pl.BlockSpec((1, 8, DV), lambda g: (g, 0, 0)),
        ],
        out_shape=[
            jax.ShapeDtypeStruct((total, width), BF16),
            jax.ShapeDtypeStruct((TP, 8, conv.shape[1]), F32),
            jax.ShapeDtypeStruct((TP, 8, DV), F32),
        ],
        compiler_params=pltpu.CompilerParams(vmem_limit_bytes=VMEM_LIMIT),
        cost_estimate=pl.CostEstimate(flops=50_000_000_000, bytes_accessed=40_000_000, transcendentals=5_000_000),
        name="mixer_bwd",
    )(proj, pos, conv, prm, gain, inv, new, gmix)


MESH = pl.DeviceIdType.MESH
AHEAD = 3


class Place:
    def __init__(self, nf):
        self.nf, self.nz = nf, nf // 2
        self.d = lax.axis_index("dp")
        self.f = lax.axis_index("fsdp")
        self.z, self.y = self.f // 2, self.f % 2
        self.over = self.z < self.nz - 1
        self.under = self.z > 0

    def flip(self, value, mask):
        return value + mask * (1 - 2 * ((value // mask) % 2))

    def dp(self, mask):
        if mask == 3:
            return (self.flip(self.flip(self.d, 1), 2), self.f)
        return (self.flip(self.d, mask), self.f)

    def at_z(self, z):
        return (self.d, z * 2 + self.y)

    def beside(self):
        return (self.d, self.flip(self.f, 1))

    def greet(self):
        barrier = pltpu.get_barrier_semaphore()
        for mask in (1, 2, 3):
            pl.semaphore_signal(barrier, inc=1, device_id=self.dp(mask), device_id_type=MESH)
        pl.semaphore_signal(barrier, inc=1, device_id=self.beside(), device_id_type=MESH)

        @pl.when(self.over)
        def _():
            pl.semaphore_signal(barrier, inc=1, device_id=self.at_z(self.z + 1), device_id_type=MESH)

        @pl.when(self.under)
        def _():
            pl.semaphore_signal(barrier, inc=1, device_id=self.at_z(self.z - 1), device_id_type=MESH)

        pl.semaphore_wait(barrier, 4 + self.over.astype(jnp.int32) + self.under.astype(jnp.int32))


def send(src, dst, send_sem, recv_sem, device):
    return pltpu.make_async_remote_copy(
        src_ref=src, dst_ref=dst, send_sem=send_sem, recv_sem=recv_sem, device_id=device, device_id_type=MESH
    )


class Gather:
    def __init__(self, place, views, ready, up_send, down_send, z_recv, y_send, y_recv, pair_send, pair_recv):
        self.p, self.views, self.ready = place, views, ready
        self.up_send, self.down_send, self.z_recv = up_send, down_send, z_recv
        self.y_send, self.y_recv, self.pair_send, self.pair_recv = y_send, y_recv, pair_send, pair_recv
        self.ticks = len(views) + place.nz - 1

    @staticmethod
    def scratch(units, nz):
        return [
            pltpu.SemaphoreType.DMA((units, nz)),
            pltpu.SemaphoreType.DMA((units, nz)),
            pltpu.SemaphoreType.DMA((units, nz)),
            pltpu.SemaphoreType.DMA((units, nz)),
            pltpu.SemaphoreType.DMA((units, nz)),
            pltpu.SemaphoreType.DMA((units,)),
            pltpu.SemaphoreType.DMA((units,)),
        ]

    def block(self, u, z, y):
        return self.views[u](z * 2 + y)

    def up(self, u, r):
        ref = self.block(u, self.p.z - (r - 1), self.p.y)
        return send(ref, ref, self.up_send.at[u, r], self.z_recv.at[u, r], self.p.at_z(self.p.z + 1))

    def down(self, u, r):
        ref = self.block(u, self.p.z + (r - 1), self.p.y)
        nz = self.p.nz
        return send(ref, ref, self.down_send.at[u, r], self.z_recv.at[u, nz - r], self.p.at_z(self.p.z - 1))

    def over_y(self, u, r):
        ref = self.block(u, lax.rem(self.p.z - r + self.p.nz, self.p.nz), self.p.y)
        return send(ref, ref, self.y_send.at[u, r], self.y_recv.at[u, r], self.p.beside())

    def pair(self, u):
        ref = self.block(u, self.p.z, 1 - self.p.y)
        return send(ref, ref, self.pair_send.at[u], self.pair_recv.at[u], self.p.at_z(self.p.flip(self.p.z, 1)))

    def wait_z(self, u, r):
        ref = self.block(u, lax.rem(self.p.z - r + self.p.nz, self.p.nz), self.p.y)
        send(ref, ref, self.up_send.at[u, 1], self.z_recv.at[u, r], self.p.beside()).wait_recv()

    def wait_y(self, u, r):
        ref = self.block(u, lax.rem(self.p.z - r + self.p.nz, self.p.nz), 1 - self.p.y)
        send(ref, ref, self.y_send.at[u, r], self.y_recv.at[u, r], self.p.beside()).wait_recv()

    def wait_pair(self, u):
        other = self.p.flip(self.p.z, 1)
        ref = self.block(u, other, 1 - self.p.y)
        send(ref, ref, self.pair_send.at[u], self.pair_recv.at[u], self.p.at_z(other)).wait_recv()

    def odd(self, u):
        return u % 2 == 1

    def skips(self, u, r):
        if not self.odd(u) or r not in (1, self.p.nz - 1):
            return None
        odd = self.p.z % 2 == 1
        if self.p.nz == 2:
            return odd | ~odd
        return odd if r == 1 else ~odd

    def unless_skipped(self, u, r, action):
        skip = self.skips(u, r)
        if skip is None:
            action()
        else:
            pl.when(~skip)(action)

    def own(self, t):
        p = self.p
        self.ready[t]()

        @pl.when(p.over)
        def _():
            self.up(t, 1).start()

        @pl.when(p.under)
        def _():
            self.down(t, 1).start()

        self.over_y(t, 0).start()

    def tick(self, t):
        p, nz = self.p, self.p.nz
        for u in range(AHEAD + 1) if t == 0 else (t + AHEAD,):
            if u < len(self.views):
                self.own(u)
        for s in range(1, nz):
            u = t - s
            if not 0 <= u < len(self.views):
                continue

            @pl.when(p.z >= s)
            def _():
                self.wait_z(u, s)

                @pl.when(p.over)
                def _():
                    self.up(u, s + 1).start()

                self.unless_skipped(u, s, self.over_y(u, s).start)

            @pl.when(p.z <= nz - 1 - s)
            def _():
                self.wait_z(u, nz - s)

                @pl.when(p.under)
                def _():
                    self.down(u, s + 1).start()

                self.unless_skipped(u, nz - s, self.over_y(u, nz - s).start)

            if s == min(AHEAD, nz - 1) and self.odd(u):
                self.wait_y(u, 0)
                self.pair(u).start()

    def finish(self):
        p, nz = self.p, self.p.nz
        for u in range(len(self.views)):
            if not self.odd(u):
                self.wait_y(u, 0)
            else:
                self.wait_pair(u)
                self.pair(u).wait_send()
            self.over_y(u, 0).wait_send()
            for r in range(1, nz):

                def both():
                    self.wait_y(u, r)
                    self.over_y(u, r).wait_send()

                self.unless_skipped(u, r, both)
            for r in range(1, nz):

                @pl.when(p.over & (p.z >= r - 1))
                def _():
                    self.up(u, r).wait_send()

                @pl.when(p.under & (p.z <= nz - r))
                def _():
                    self.down(u, r).wait_send()


def gather_kernel(nf, packs, shards, groups, *refs):
    count = len(packs) + len(shards) + groups
    ins, outs = refs[:count], refs[count : 2 * count]
    to_send, to_recv, near_send, near_recv, local_sem = refs[2 * count : 2 * count + 5]
    p = Place(nf)
    pack_in, shard_in, group_in = ins[: len(packs)], ins[len(packs) : len(packs) + len(shards)], ins[count - groups :]
    pack_out, shard_out, group_out = (
        outs[: len(packs)],
        outs[len(packs) : len(packs) + len(shards)],
        outs[count - groups :],
    )

    def own_pack(i, d):
        return pack_out[i].at[d, p.f] if packs[i] else pack_out[i].at[d]

    def exchange(i, m):
        target = p.dp(m)
        return send(pack_in[i].at[target[0]], own_pack(i, p.d), to_send.at[i, m], to_recv.at[i, m], target)

    def wait_exchange(i, m):
        source = p.dp(m)
        ref = own_pack(i, source[0])
        send(ref, ref, to_send.at[i, m], to_recv.at[i, m], source).wait_recv()

    def near(j, k):
        src, dst, mask = ((group_in[j], 2, 2), (group_in[j], 1, 1), (group_out[j].at[2], 3, 1))[k]
        return send(src, group_out[j].at[dst], near_send.at[j, k], near_recv.at[j, k], p.dp(mask))

    def wait_near(j, k):
        ref = group_out[j].at[(2, 1, 3)[k]]
        send(ref, ref, near_send.at[j, k], near_recv.at[j, k], p.dp(1)).wait_recv()

    def local(n):
        if n < len(packs):
            return pltpu.make_async_copy(pack_in[n].at[p.d], own_pack(n, p.d), local_sem.at[n])
        if n < len(packs) + len(shards):
            i = n - len(packs)
            return pltpu.make_async_copy(shard_in[i], shard_out[i].at[p.f], local_sem.at[n])
        j = n - len(packs) - len(shards)
        return pltpu.make_async_copy(group_in[j], group_out[j].at[0], local_sem.at[n])

    p.greet()
    views, ready = [], []
    for i, whole in enumerate(packs):
        for m in range(TP if whole else 0):
            source = p.dp(m)[0] if m else p.d
            views.append(lambda f, i=i, d=source: pack_out[i].at[d, f])
            ready.append(partial(wait_exchange, i, m) if m else local(i).wait)
    for i in range(len(shards)):
        views.append(lambda f, i=i: shard_out[i].at[f])
        ready.append(local(len(packs) + i).wait)
    gather = Gather(p, views, ready, *refs[2 * count + 5 :])
    for n in range(count):
        local(n).start()
    for m in (1, 2, 3):
        exchange(0, m).start()
    for j in range(groups):
        near(j, 0).start()
        near(j, 1).start()
    for i in range(1, len(packs)):
        for m in (2, 3, 1):
            exchange(i, m).start()
    for t in range(gather.ticks):
        gather.tick(t)
        if t == 2:
            for j in range(groups):
                wait_near(j, 0)
                near(j, 2).start()
    gather.finish()
    for i, whole in enumerate(packs):
        for m in (1, 2, 3):
            exchange(i, m).wait_send()
            if not whole:
                wait_exchange(i, m)
        if not whole:
            local(i).wait()
    for j in range(groups):
        wait_near(j, 1)
        wait_near(j, 2)
        for k in range(3):
            near(j, k).wait_send()
        local(len(packs) + len(shards) + j).wait()


def gather_all(nf, collective_id, packs, shards, groups):
    marks = tuple(whole for _, whole in packs)
    ins = [array for array, _ in packs] + list(shards) + list(groups)
    outs = (
        [
            jax.ShapeDtypeStruct(array.shape[:1] + ((nf,) if whole else ()) + array.shape[1:], array.dtype)
            for array, whole in packs
        ]
        + [jax.ShapeDtypeStruct((nf,) + array.shape, array.dtype) for array in shards]
        + [jax.ShapeDtypeStruct((TP,) + array.shape, array.dtype) for array in groups]
    )
    units = TP * sum(marks) + len(shards)
    sent = sum(out.size * 2 for out in outs)
    any_space = pl.BlockSpec(memory_space=pl.ANY)
    return pl.pallas_call(
        partial(gather_kernel, nf, marks, (True,) * len(shards), len(groups)),
        in_specs=[any_space] * len(ins),
        out_specs=[any_space] * len(outs),
        out_shape=outs,
        scratch_shapes=[
            pltpu.SemaphoreType.DMA((len(packs), TP)),
            pltpu.SemaphoreType.DMA((len(packs), TP)),
            pltpu.SemaphoreType.DMA((max(len(groups), 1), 3)),
            pltpu.SemaphoreType.DMA((max(len(groups), 1), 3)),
            pltpu.SemaphoreType.DMA((len(ins),)),
        ]
        + Gather.scratch(units, nf // 2),
        compiler_params=pltpu.CompilerParams(
            collective_id=collective_id, has_side_effects=True, vmem_limit_bytes=1024 * 1024
        ),
        cost_estimate=pl.CostEstimate(flops=0, bytes_accessed=2 * sent, transcendentals=0),
        name="gather_" + str(collective_id),
    )(*ins)


def add_into(dst, srcs):
    rows = dst.shape[-2]
    size = 16 if rows % 16 == 0 else rows
    lead = dst.shape[0] if len(dst.shape) == 3 else 1

    def body(i, _):
        at = pl.ds(pl.multiple_of((i % (rows // size)) * size, size), size)
        where = (i // (rows // size), at) if len(dst.shape) == 3 else (at,)
        total = srcs[0][where].astype(F32)
        for src in srcs[1:]:
            total = total + src[where].astype(F32)
        dst[where] = total.astype(dst.dtype)
        return 0

    lax.fori_loop(0, lead * (rows // size), body, 0)


class Reduce:
    def __init__(self, place, part, done, y_in, z_in, pair_in, sems):
        self.p, self.part, self.done = place, part, done
        self.y_in, self.z_in, self.pair_in = y_in, z_in, pair_in
        self.y_send, self.y_recv, self.z_send, self.z_recv, self.pair_send, self.pair_recv = sems
        self.count = len(y_in)
        self.ticks = self.count + place.nz

    @staticmethod
    def scratch(blocks, nz):
        units = len(blocks)
        return (
            [pltpu.VMEM((nz,) + block, BF16) for block in blocks]
            + [pltpu.VMEM((nz + 1,) + block, BF16) for block in blocks]
            + [pltpu.VMEM(block, BF16) for block in blocks]
            + [pltpu.SemaphoreType.DMA((units, nz))] * 3
            + [pltpu.SemaphoreType.DMA((units, nz + 1))]
            + [pltpu.SemaphoreType.DMA((units,))] * 2
        )

    def odd(self, u):
        return u % 2 == 1

    def copy_y(self, u, z0):
        src = self.part(u, z0 * 2 + 1 - self.p.y)
        return send(src, self.y_in[u].at[z0], self.y_send.at[u, z0], self.y_recv.at[u, z0], self.p.beside())

    def copy_late(self, u):
        z = self.p.z
        return send(self.pair_in[u], self.y_in[u].at[z], self.y_send.at[u, z], self.y_recv.at[u, z], self.p.beside())

    def copy_pair(self, u):
        other = self.p.flip(self.p.z, 1)
        src = self.part(u, other * 2 + 1 - self.p.y)
        return send(src, self.pair_in[u], self.pair_send.at[u], self.pair_recv.at[u], self.p.at_z(other))

    def copy_z(self, u, z0, slot, z):
        return send(self.y_in[u].at[z0], self.z_in[u].at[slot], self.z_send.at[u, z0], self.z_recv.at[u, slot], self.p.at_z(z))

    def wait_z(self, u, slot):
        ref = self.z_in[u].at[slot]
        send(ref, ref, self.z_send.at[u, 0], self.z_recv.at[u, slot], self.p.beside()).wait_recv()

    def pass_on(self, u, z0, arrived, slot, z):
        own = self.part(u, z0 * 2 + self.p.y)
        here = self.y_in[u].at[z0]
        if self.odd(u):
            other = self.p.flip(self.p.z, 1)

            @pl.when(other != z0)
            def _():
                add_into(here, [own, here] + arrived)

            @pl.when(other == z0)
            def _():
                add_into(here, [own] + arrived)
        else:
            add_into(here, [own, here] + arrived)
        self.copy_z(u, z0, slot, z).start()

    def tick(self, t):
        p, nz = self.p, self.p.nz
        if t < self.count:
            if self.odd(t):
                self.copy_pair(t).start()
                other = p.flip(p.z, 1)
                for z0 in range(nz):

                    @pl.when((z0 != p.z) & (z0 != other))
                    def _():
                        self.copy_y(t, z0).start()
            else:
                for z0 in range(nz):
                    self.copy_y(t, z0).start()
        u = t - 1
        if 0 <= u < self.count:
            if self.odd(u):
                self.copy_pair(u).wait_recv()
                add_into(self.pair_in[u], [self.pair_in[u], self.part(u, p.z * 2 + 1 - p.y)])
                self.copy_late(u).start()
            other = p.flip(p.z, 1)
            for z0 in range(nz):
                needed = (z0 != p.z) & (z0 != other) if self.odd(u) else z0 != p.z

                @pl.when(needed)
                def _():
                    self.copy_y(u, z0).wait_recv()

            @pl.when(p.z == nz - 1)
            def _():
                for z0 in range(nz - 1):
                    self.pass_on(u, z0, [], z0, p.z - 1)

            @pl.when(p.z == 0)
            def _():
                for z0 in range(nz - 1, 0, -1):
                    self.pass_on(u, z0, [], nz if z0 == 1 else z0, p.z + 1)

        for hop in range(1, nz):
            u = t - 1 - hop
            if not 0 <= u < self.count:
                continue

            @pl.when(p.z == nz - 1 - hop)
            def _():
                for z0 in range(nz - hop):
                    self.wait_z(u, z0)
                    if z0 < nz - 1 - hop:
                        self.pass_on(u, z0, [self.z_in[u].at[z0]], z0, p.z - 1)

            @pl.when(p.z == hop)
            def _():
                for z0 in range(nz - 1, hop - 1, -1):
                    slot = nz if z0 == hop else z0
                    self.wait_z(u, slot)
                    if z0 > hop:
                        self.pass_on(u, z0, [self.z_in[u].at[z0]], nz if z0 == hop + 1 else z0, p.z + 1)

        u = t - nz
        if 0 <= u < self.count:
            self.copy_y(u, p.z).wait_recv()
            own = [self.part(u, p.f), self.y_in[u].at[p.z]]
            above, below = self.z_in[u].at[p.z], self.z_in[u].at[nz]

            @pl.when(p.z == 0)
            def _():
                self.done(u, own + [above])

            @pl.when(p.z == nz - 1)
            def _():
                self.done(u, own + [below])

            @pl.when(p.over & p.under)
            def _():
                self.done(u, own + [above, below])

    def finish(self):
        p, nz = self.p, self.p.nz
        other = p.flip(p.z, 1)
        for u in range(self.count):
            if self.odd(u):
                self.copy_pair(u).wait_send()
                self.copy_late(u).wait_send()
            for z0 in range(nz):
                needed = (z0 != p.z) & (z0 != other) if self.odd(u) else None
                if needed is None:
                    self.copy_y(u, z0).wait_send()
                else:

                    @pl.when(needed)
                    def _():
                        self.copy_y(u, z0).wait_send()

                @pl.when(z0 != p.z)
                def _():
                    self.copy_z(u, z0, z0, p.z).wait_send()


def reduce_kernel(nf, kinds, units, groups, vecs, *refs):
    arrays = len(kinds)
    count = arrays + groups + vecs
    ins, outs, rest = refs[:count], refs[count : 2 * count], refs[2 * count :]
    p = Place(nf)
    nz = p.nz
    n = len(units)
    y_in, z_in, pair_in, rest = rest[:n], rest[n : 2 * n], rest[2 * n : 3 * n], rest[3 * n :]
    sems, rest = rest[:6], rest[6:]
    packs = [u for u, (i, _, _) in enumerate(units) if kinds[i]]
    final = dict(zip(packs, rest[: len(packs)]))
    rest = rest[len(packs) :]
    to_send, to_recv, to_local, rest = rest[0], rest[1], rest[2], rest[3:]
    if groups:
        group_in, group_sems, rest = rest[0], rest[1:3], rest[3:]
    if vecs:
        vec_in, vec_own, vec_sems = rest[0], rest[1], rest[2:4]

    def part(u, f):
        i, start, size = units[u]
        columns = pl.ds(start, size)
        return ins[i].at[:, f, :, columns] if kinds[i] else ins[i].at[f, :, columns]

    def owner_copy(u, m):
        i, start, size = units[u]
        target = p.dp(m)
        return send(
            final[u].at[target[0]],
            outs[i].at[p.d, :, pl.ds(start, size)],
            to_send.at[u, m],
            to_recv.at[u, m],
            target,
        )

    def owner_local(u):
        i, start, size = units[u]
        return pltpu.make_async_copy(final[u].at[p.d], outs[i].at[p.d, :, pl.ds(start, size)], to_local.at[u])

    def done(u, sources):
        i, start, size = units[u]
        if kinds[i]:
            add_into(final[u], sources)
        else:
            add_into(outs[i].at[:, pl.ds(start, size)], sources)

    def wait_owner(u, m):
        i, start, size = units[u]
        source = p.dp(m)
        ref = outs[i].at[source[0], :, pl.ds(start, size)]
        send(ref, ref, to_send.at[u, m], to_recv.at[u, m], source).wait_recv()

    def group_copy(j, k):
        src, mask = ((ins[arrays + j].at[1], 1), (ins[arrays + j].at[3], 1), (group_in.at[j, 1], 2))[k]
        return send(src, group_in.at[j, (0, 1, 2)[k]], group_sems[0].at[j, k], group_sems[1].at[j, k], p.dp(mask))

    def vec_copy(k):
        device = (p.dp(1), p.dp(2), p.beside())[k]
        return send(vec_own.at[k], vec_in.at[k], vec_sems[0].at[k], vec_sems[1].at[k], device)

    def vec_z(k):
        z = lax.rem(p.z + k, nz)
        return send(vec_own.at[3], vec_in.at[3 + p.z], vec_sems[0].at[2 + k], vec_sems[1].at[2 + k], p.at_z(z))

    def vec_step(k):
        if k:
            vec_copy(k - 1).wait()
            vec_own[k] = vec_own[k - 1] + vec_in[k - 1]
        else:
            vec_own[0] = ins[arrays + groups][...]
        if k < 3:
            vec_copy(k).start()

    p.greet()
    red = Reduce(p, part, done, y_in, z_in, pair_in, sems)
    for j in range(groups):
        group_copy(j, 0).start()
        group_copy(j, 1).start()
    for t in range(red.ticks):
        red.tick(t)
        u = t - nz
        if u in final:
            for m in (2, 3, 1):
                owner_copy(u, m).start()
            owner_local(u).start()
        if t == 0:
            for j in range(groups):
                group_copy(j, 0).wait_recv()
                group_copy(j, 1).wait_recv()
                add_into(group_in.at[j, 1], [ins[arrays + j].at[2], group_in.at[j, 1]])
                group_copy(j, 2).start()
        if vecs and t < 4:
            vec_step(t)
    for j in range(groups):
        group_copy(j, 2).wait_recv()
        add_into(outs[arrays + j], [ins[arrays + j].at[0], group_in.at[j, 0], group_in.at[j, 2]])
        for k in range(3):
            group_copy(j, k).wait_send()
    if vecs:
        vec_in[3 + p.z] = vec_own[3]
        for k in range(1, nz):
            vec_z(k).start()
        for k in range(1, nz):
            source = lax.rem(p.z - k + nz, nz)
            ref = vec_in.at[3 + source]
            send(ref, ref, vec_sems[0].at[2 + k], vec_sems[1].at[2 + k], p.at_z(source)).wait_recv()
        total = vec_in[3]
        for k in range(1, nz):
            total = total + vec_in[3 + k]
        outs[arrays + groups][...] = total
        for k in range(1, nz):
            vec_z(k).wait_send()
    red.finish()
    for u in packs:
        owner_local(u).wait()
        for m in (1, 2, 3):
            owner_copy(u, m).wait_send()
            wait_owner(u, m)


def reduce_all(nf, collective_id, arrays, widths, groups=(), vec=None):
    nz = nf // 2
    kinds = tuple(array.ndim == 4 for array in arrays)
    units, blocks = [], []
    for i, (array, width) in enumerate(zip(arrays, widths)):
        for start in range(0, array.shape[-1], width):
            size = min(width, array.shape[-1] - start)
            units.append((i, start, size))
            blocks.append(((TP,) if kinds[i] else ()) + (array.shape[-2], size))
    final = [pltpu.VMEM(block, BF16) for block, unit in zip(blocks, units) if kinds[unit[0]]]
    scratch = Reduce.scratch(blocks, nz) + final
    scratch += [
        pltpu.SemaphoreType.DMA((len(units), TP)),
        pltpu.SemaphoreType.DMA((len(units), TP)),
        pltpu.SemaphoreType.DMA((len(units),)),
    ]
    if groups:
        scratch += [pltpu.VMEM((len(groups), 3) + groups[0].shape[1:], BF16)]
        scratch += [pltpu.SemaphoreType.DMA((len(groups), 3))] * 2
    if vec is not None:
        scratch += [pltpu.VMEM((3 + nz, 8, TAIL), F32), pltpu.VMEM((4, 8, TAIL), F32)]
        scratch += [pltpu.SemaphoreType.DMA((2 + nz,))] * 2
    vmem, any_space = pl.BlockSpec(memory_space=pltpu.VMEM), pl.BlockSpec(memory_space=pl.ANY)
    outs, out_specs = [], []
    for array, kind in zip(arrays, kinds):
        if kind:
            outs.append(jax.ShapeDtypeStruct((TP,) + array.shape[2:], BF16))
            out_specs.append(any_space)
        else:
            outs.append(jax.ShapeDtypeStruct(array.shape[1:], F32))
            out_specs.append(vmem)
    for array in groups:
        outs.append(jax.ShapeDtypeStruct(array.shape[1:], F32))
        out_specs.append(vmem)
    vecs = []
    if vec is not None:
        vecs = [vec]
        outs.append(jax.ShapeDtypeStruct(vec.shape, F32))
        out_specs.append(vmem)
    ins = list(arrays) + list(groups) + vecs
    return pl.pallas_call(
        partial(reduce_kernel, nf, kinds, tuple(units), len(groups), len(vecs)),
        in_specs=[vmem] * len(ins),
        out_specs=out_specs,
        out_shape=outs,
        scratch_shapes=scratch,
        compiler_params=pltpu.CompilerParams(
            collective_id=collective_id, has_side_effects=True, vmem_limit_bytes=VMEM_LIMIT
        ),
        cost_estimate=pl.CostEstimate(
            flops=0, bytes_accessed=sum(2 * a.size * a.dtype.itemsize for a in ins), transcendentals=0
        ),
        name="reduce_" + str(collective_id),
    )(*ins)


def dp_swap(value, mask):
    return lax.ppermute(value, "dp", [(i, i ^ mask) for i in range(TP)])


def dp_gather(value):
    far = dp_swap(value, 2)
    near = dp_swap(value, 1)
    return jnp.stack([value, near, far, dp_swap(far, 1)])


def dp_reduce(parts):
    got = dp_swap(jnp.stack([parts[1], parts[3]]), 1)
    mine = parts[0].astype(F32) + got[0].astype(F32)
    far = (parts[2].astype(F32) + got[1].astype(F32)).astype(BF16)
    return mine + dp_swap(far, 2).astype(F32)


def local(
    tokens,
    out_grad,
    block_first,
    block_live,
    norm1_gain,
    w_proj,
    w_decay,
    conv_w,
    w_out,
    a_log,
    dt_bias,
    head_gain,
    norm2_gain,
    w_gate_up,
    w_down,
    *,
    fsdp_size,
):
    nf = fsdp_size
    me = lax.axis_index("dp")
    rows, width = tokens.shape
    own = w_proj.shape[0]
    key_width = HEADS * DK
    value_width = HEADS * DV
    ff = w_down.shape[0] * nf

    block_index = jnp.arange(block_first.shape[0], dtype=jnp.int32)
    earlier = (block_index[:, None] >= block_index[None]) & (block_first[None] > 0)
    bucket_starts = jnp.max(jnp.where(earlier, block_index[None] * BLOCK, 0), axis=1)
    row_index = jnp.arange(rows, dtype=jnp.int32)
    position = row_index - jnp.repeat(bucket_starts, BLOCK)
    live = (row_index % BLOCK < jnp.repeat(block_live, BLOCK)).astype(F32)[:, None]

    def by_target(value):
        return value.reshape(own, TP, -1).swapaxes(0, 1)

    taps = conv_w.reshape(own, -1)
    tail = jnp.concatenate(
        [
            by_target(w_decay[:, :HEADS]),
            by_target(w_decay[:, HEADS:]),
            jnp.broadcast_to(
                jnp.concatenate([norm1_gain[:, None], norm2_gain[:, None], taps], axis=1)[None],
                (TP, own, 2 + taps.shape[1]),
            ),
        ],
        axis=2,
    )
    tail = jnp.pad(tail, ((0, 0), (0, 0), (0, TAIL - tail.shape[2])))
    pack_one = jnp.concatenate(
        [
            by_target(w_proj[:, :key_width]),
            by_target(w_proj[:, key_width : 2 * key_width]),
            by_target(w_proj[:, 2 * key_width : 2 * key_width + value_width]),
            by_target(w_proj[:, 2 * key_width + value_width :]),
            tail,
        ],
        axis=2,
    )
    pack_gate = by_target(w_gate_up[:, : ff * TP])
    pack_up = by_target(w_gate_up[:, ff * TP :])
    extra = jnp.broadcast_to(position.astype(BF16)[:, None], (rows, TAIL))
    cotangent = live * out_grad.astype(F32)
    proj_full, gate_full, up_full, out_full, down_full, group, grad_down = gather_all(
        nf,
        1,
        ((pack_one, True), (pack_gate, True), (pack_up, True)),
        (w_out, w_down),
        (jnp.concatenate([tokens, extra], axis=1), cotangent.astype(BF16)),
    )
    proj_full = proj_full.reshape(width, -1)
    gate_full = gate_full.reshape(width, ff)
    up_full = up_full.reshape(width, ff)
    out_full = out_full.reshape(-1, width)
    down_full = down_full.reshape(ff, width)
    group = group.reshape(TP * rows, width + TAIL)
    grad_down = grad_down.reshape(TP * rows, width)
    group_pos = group[:, width:].astype(F32)
    group_tokens = group[:, :width].astype(F32)

    tail_full = proj_full[:, -TAIL:]
    gain_one = tail_full[:, 2 * LH].astype(F32)
    gain_two = tail_full[:, 2 * LH + 1].astype(F32)
    taps_full = tail_full[:, 2 * LH + 2 : 2 * LH + 2 + taps.shape[1]]
    taps_full = (
        taps_full.reshape(TP * nf, CONV, -1).swapaxes(0, 1).reshape(CONV, 2 * key_width + value_width).astype(F32)
    )

    def my_columns(value):
        k, v = LH * DK, LH * DV
        return jnp.concatenate(
            [
                lax.dynamic_slice_in_dim(value, me * k, k, 1),
                lax.dynamic_slice_in_dim(value, key_width + me * k, k, 1),
                lax.dynamic_slice_in_dim(value, 2 * key_width + me * v, v, 1),
            ],
            axis=1,
        )

    conv_mine = jnp.pad(my_columns(taps_full), ((0, 8 - CONV), (0, 0)))
    rate = -jnp.exp(lax.dynamic_slice_in_dim(a_log, me * LH, LH))
    bias = lax.dynamic_slice_in_dim(dt_bias, me * LH, LH)
    prm = jnp.pad(jnp.stack([rate, bias]), ((0, 6), (0, TAIL - LH)))
    gain_head = jnp.broadcast_to(head_gain[None], (8, DV))

    scale_one = lax.rsqrt(jnp.mean(group_tokens * group_tokens, axis=-1, keepdims=True) + EPS)
    normed_one = (group_tokens * scale_one * gain_one).astype(BF16)
    proj = mm(normed_one, proj_full)
    mixed, inv, new = mixer_fwd(proj, group_pos, conv_mine, prm, gain_head)
    mixed_out = mm(mixed, out_full).astype(BF16).reshape(TP, rows, width)
    residual = tokens.astype(F32) + dp_reduce(mixed_out)
    scale_two = lax.rsqrt(jnp.mean(residual * residual, axis=-1, keepdims=True) + EPS)
    normed_two = dp_gather((residual * scale_two * gain_two).astype(BF16)).reshape(TP * rows, width)
    gate = mm(normed_two, gate_full)
    up = mm(normed_two, up_full)
    gate_sig = jax.nn.sigmoid(gate)
    gate_act = gate * gate_sig
    hidden = (gate_act * up).astype(BF16)
    down_out = mm(hidden, down_full).astype(BF16).reshape(TP, rows, width)
    layer_out = (live * (residual + dp_reduce(down_out))).astype(BF16)

    grad_wdown = mm(hidden, grad_down, ((0,), (0,))).astype(BF16).reshape(nf, -1, width)
    grad_hidden = mm(grad_down, down_full, ((1,), (1,)))
    grad_gate = (grad_hidden * up * gate_sig * (1.0 + gate * (1.0 - gate_sig))).astype(BF16)
    grad_up = (grad_hidden * gate_act).astype(BF16)
    gate_grad, up_grad = (
        mm(normed_two, grad, ((0,), (0,))).astype(BF16).reshape(TP, nf, own, ff) for grad in (grad_gate, grad_up)
    )
    gate_grad, up_grad, wdown_grad = reduce_all(nf, 2, (gate_grad, up_grad, grad_wdown), (768, 768, 1024))
    grad_two = mm(grad_gate, gate_full, ((1,), (1,))) + mm(grad_up, up_full, ((1,), (1,)))
    grad_two = dp_reduce(grad_two.astype(BF16).reshape(TP, rows, width))
    weighted = grad_two * gain_two
    gain_two_part = jnp.sum(grad_two * residual * scale_two, axis=0)
    grad_residual = (
        cotangent
        + scale_two * weighted
        - residual * (scale_two**3 * jnp.mean(residual * weighted, axis=-1, keepdims=True))
    )

    grad_mixed_in = dp_gather(grad_residual.astype(BF16)).reshape(TP * rows, width)
    wout_grad = mm(mixed, grad_mixed_in, ((0,), (0,))).astype(BF16).reshape(nf, -1, width)
    grad_mixed = mm(grad_mixed_in, out_full, ((1,), (1,)))
    grad_proj, grad_taps, misc = mixer_bwd(
        proj, group_pos, conv_mine, prm, gain_head, inv, new, grad_mixed
    )
    grad_one_part = mm(grad_proj, proj_full, ((1,), (1,)))
    gain_one_part = jnp.sum(grad_one_part * group_tokens * scale_one, axis=0)

    grad_taps = jnp.sum(grad_taps[:, :CONV], axis=0)
    k, v = LH * DK, LH * DV
    taps_all = jnp.zeros((CONV, 2 * key_width + value_width), F32)
    taps_all = lax.dynamic_update_slice(taps_all, grad_taps[:, :k], (0, me * k))
    taps_all = lax.dynamic_update_slice(taps_all, grad_taps[:, k : 2 * k], (0, key_width + me * k))
    taps_all = lax.dynamic_update_slice(taps_all, grad_taps[:, 2 * k :], (0, 2 * key_width + me * v))
    taps_all = taps_all.reshape(CONV, TP * nf, -1).swapaxes(0, 1).reshape(width, taps.shape[1])
    small = jnp.concatenate([gain_one_part[:, None], gain_two_part[:, None], taps_all], axis=1)
    columns = proj.shape[1]
    small = jnp.pad(small, ((0, 0), (columns - TAIL + 2 * LH, TAIL - 2 * LH - small.shape[1])))
    one_grad = (mm(normed_one, grad_proj, ((0,), (0,))) + small).astype(BF16).reshape(TP, nf, own, columns)

    misc = jnp.sum(misc, axis=0)
    heads_zero = jnp.zeros((HEADS,), F32)
    head_vec = jnp.concatenate(
        [
            lax.dynamic_update_slice(heads_zero, misc[1, :LH], (me * LH,)),
            lax.dynamic_update_slice(heads_zero, misc[2, :LH], (me * LH,)),
            misc[0],
        ]
    )
    head_vec = jnp.pad(head_vec, (0, 8 * TAIL - head_vec.shape[0])).reshape(8, TAIL)
    one_own, wout_grad, grad_one, head_vec = reduce_all(
        nf,
        3,
        (one_grad, wout_grad),
        (640, 2048),
        (grad_one_part.astype(BF16).reshape(TP, rows, width),),
        head_vec,
    )
    head_vec = head_vec.reshape(-1)
    one_own = one_own.astype(F32)

    def columns_of(value):
        return value.swapaxes(0, 1).reshape(own, -1)

    w_gate_up_grad = jnp.concatenate(
        [columns_of(gate_grad.astype(F32)), columns_of(up_grad.astype(F32))], axis=1
    )
    w_proj_grad = jnp.concatenate(
        [
            columns_of(one_own[:, :, :k]),
            columns_of(one_own[:, :, k : 2 * k]),
            columns_of(one_own[:, :, 2 * k : 2 * k + v]),
            columns_of(one_own[:, :, 2 * k + v : 2 * k + 2 * v]),
        ],
        axis=1,
    )
    own_tail = one_own[:, :, columns - TAIL :]
    w_decay_grad = jnp.concatenate(
        [columns_of(own_tail[:, :, :LH]), columns_of(own_tail[:, :, LH : 2 * LH])], axis=1
    )
    own_small = jnp.sum(own_tail[:, :, 2 * LH : 2 * LH + 2 + taps.shape[1]], axis=0)
    norm1_gain_grad = own_small[:, 0]
    norm2_gain_grad = own_small[:, 1]
    conv_grad = own_small[:, 2:].reshape(CONV, -1)

    tokens_f = tokens.astype(F32)
    scale_own = scale_one[:rows]
    weighted_one = grad_one * gain_one
    from_one = scale_own * weighted_one - tokens_f * (
        scale_own**3 * jnp.mean(tokens_f * weighted_one, axis=-1, keepdims=True)
    )
    tokens_grad = (grad_residual + from_one).astype(BF16)
    return (
        layer_out,
        tokens_grad,
        norm1_gain_grad,
        w_proj_grad,
        w_decay_grad,
        conv_grad,
        wout_grad.reshape(w_out.shape),
        head_vec[:HEADS],
        head_vec[HEADS : 2 * HEADS],
        head_vec[2 * HEADS : 2 * HEADS + DV],
        norm2_gain_grad,
        w_gate_up_grad,
        wdown_grad.reshape(w_down.shape),
    )


def solution(mesh):
    rows = P(("dp", "fsdp"), None)
    flat = P(("dp", "fsdp"))
    in_specs = (rows, rows, flat, flat, flat, rows, rows, P(None, ("dp", "fsdp")), rows, P(), P(), P(), flat, rows, rows)
    out_specs = (rows, rows, flat, rows, rows, P(None, ("dp", "fsdp")), rows, P(), P(), P(), flat, rows, rows)
    return jax.shard_map(
        partial(local, fsdp_size=mesh.shape["fsdp"]),
        mesh=mesh,
        in_specs=in_specs,
        out_specs=out_specs,
        check_vma=False,
    )
```

time: 1530 us -> 1250 us (0.82)
  Pallas kernels: 137 us -> 880 us
  waiting for transfers between devices: 506 us -> 84.1 us
  local copies, waits for them, and re-layouts: 254 us -> 59.8 us
  blocking collectives: 169 us -> 0 us
  starting transfers between devices: 169 us -> 8.54 us
  other arithmetic: 89.1 us -> 36.9 us
  matrix products: 185 us -> 169 us
    pallas_call x0 -> x3, Pallas kernels: none -> 780 us  [the longest x2 440 us: reduce_all(): pl.pallas_call(partial(reduce_kernel, nf, kinds, tuple(units), len(groups...]
    ppermute x44 -> x0, waiting for transfers between devices: 478 us -> none  [the longest x24 367 us: z_turn(): return lax.ppermute(value, 'fsdp', pairs)]
    psum x1 -> x0, blocking collectives: 169 us -> none  [local(): head_vec = lax.psum(head_vec, ('dp', 'fsdp'))]
    ppermute x44 -> x0, starting transfers between devices: 140 us -> none  [the longest x24 124 us: z_turn(): return lax.ppermute(value, 'fsdp', pairs)]
    ppermute x20 -> x12, waiting for transfers between devices: 16.4 us -> 84.1 us  [dp_swap(): return lax.ppermute(value, 'dp', [(i, i ^ mask) for i in range(TP)])]
    dynamic_update_slice x35 -> x3, local copies, waits for them, and re-layouts: 57.2 us -> 0.2 us  [the longest x1 0.1 us: local(): lax.dynamic_update_slice(heads_zero, misc[2, :LH], (me * LH,))]
    pallas_call x1, Pallas kernels: 96.1 us -> 43.5 us  [mixer_fwd(): pl.pallas_call(mixer_fwd_kernel, grid=(TP,), in_specs=[pl.BlockSpec((rows...]
    unnamed x129 -> x121, local copies, waits for them, and re-layouts: 71.4 us -> 30.2 us
  transfers between devices with their start and end apart: 68 -> 12, of which waited for: 20 -> 7; matrix products, arithmetic and copies ran while one was open for 29% -> 4% of each run, Pallas kernels for 9% -> 17%
where the time goes in v2:
time: 1250 us; the launch traced here: 1240 us
  Pallas kernels  880 us (70%)
  matrix products  169 us (14%)
  waiting for transfers between devices  84.1 us (7%)
  local copies, waits for them, and re-layouts  59.8 us (5%)
  other arithmetic  36.9 us (3%)
    pallas_call x2, Pallas kernels, reduce_all(): pl.pallas_call(partial(reduce_kernel, nf, kinds, tuple(units), len(groups...  440 us
    pallas_call x1, Pallas kernels, gather_all(): pl.pallas_call(partial(gather_kernel, nf, marks, (True,) * len(shards), l...  341 us
    dot_general x15, matrix products, mm(): lax.dot_general(left, right, (dims, ((), ())), preferred_element_type=F32)  169 us
    ppermute x12, waiting for transfers between devices, dp_swap(): return lax.ppermute(value, 'dp', [(i, i ^ mask) for i in range(TP)])  84.1 us
    pallas_call x1, Pallas kernels, mixer_bwd(): pl.pallas_call(mixer_bwd_kernel, grid=(TP,), in_specs=[pl.BlockSpec((rows...  56 us
    pallas_call x1, Pallas kernels, mixer_fwd(): pl.pallas_call(mixer_fwd_kernel, grid=(TP,), in_specs=[pl.BlockSpec((rows...  43.5 us
    unnamed x121, local copies, waits for them, and re-layouts  30.2 us
  transfers between devices with their start and end apart: 12, of which 7 were waited for; matrix products, arithmetic and copies ran while one was open for 4% of the time, Pallas kernels for 17%

profile of v2, /device:TPU:0, one launch (start us, length us, event | category | flops | bytes accessed | tf_op | source)
XLA Modules:
  0.0 1240.3 jit_solution(13036694470909713460)
XLA Ops:
  25.4 340.5 %gather_1.1 = (bf16[4,8,64,3200]{3,2,1,0:T(8,128)(2,1)S(1)}, bf16[4,8,64,1408]{3,2,1,0:T(8,128)(2,1)S(1)}, bf16[4,8,64,1408]{3,2,1,0:T(8,128)(2,1)S(1)}, bf16[8,...) custom-call(bf16[4,64,3200]{2,1,0:T(8,128)(2,1)S(1)} %fusion.35.refs, ...), custom_call_target="tpu_custom_call" | custom-call | bytes 86507520 | tf_op jit(solution)/shard_map/gather_1/pallas_call | solution.py:594
  387.1 22.9 %fusion.24.proj_ref = f32[1024,3200]{1,0:T(8,128)} fusion(bf16[2048,3200]{1,0:T(8,128)(2,1)} %bitcast.217, f32[2048]{0:T(1024)S(1)} %convert_reduce_fusion, f32[1024]{0:T(1024)S(1)} %add_rsqrt_fusion, bf16[1024,2176]{1,0:T(8,128)(2,1)} %bitcast.212), kind=kOutput, calls=%fused_computation.81 | convolution fusion | flops 13430161408 | bytes 30420992 | tf_op jit(solution)/shard_map/dot_general | solution.py:25
  411.9 43.5 %mixer_fwd.1 = (bf16[1024,1024]{1,0:T(8,128)(2,1)}, f32[16,256,256]{2,1,0:T(8,128)}, f32[1024,1024]{1,0:T(8,128)}) custom-call(f32[1024,3200]{1,0:T(8,128)} %fusion.24.proj_ref, f32[1024,128]{1,0:T(8,128)} %slice_convert_fusion.2.pos_ref, f32[8,2048]{1,0:T(8,128)} %select_maximum_fusion.2.conv_ref, f32[8,128]{1,0:T(8,128)} %select_maximum_fusion.6.prm_ref, ...), custom_call_target="tpu_custom_call" | custom-call | flops 30000001024 | bytes 30000000 | tf_op jit(solution)/shard_map/mixer_fwd/pallas_call | solution.py:243
  455.4 6.7 convolution_convert_fusion.5
  473.8 20.1 %collective-permute-done.1 = bf16[256,2048]{1,0:T(8,128)(2,1)} collective-permute-done((bf16[256,2048]{1,0:T(8,128)(2,1)}, bf16[256,2048]{1,0:T(8,128)(2,1)}, u32[]{:S(2)}, u32[]{:S(2)}) %collective-permute-start.1) | collective-permute-done | bytes 1048608 | tf_op jit(solution)/shard_map/ppermute | solution.py:966
  498.3 22.8 %collective-permute-done.3 = bf16[256,2048]{1,0:T(8,128)(2,1)S(1)} collective-permute-done((bf16[256,2048]{1,0:T(8,128)(2,1)S(1)}, bf16[256,2048]{1,0:T(8,128)(2,1)S(1)}, u32[]{:S(2)}, u32[]{:S(2)}) %collective-permute-start.3) | collective-permute-done | bytes 1048608 | tf_op jit(solution)/shard_map/ppermute | solution.py:966
  521.2 8.7 fusion.50
  534.8 8.5 fusion.49
  543.3 15.0 %multiply_convert_fusion = (bf16[1024,1408]{1,0:T(8,128)(2,1)}, bf16[1024,1408]{1,0:T(8,128)(2,1)}, bf16[1024,1408]{1,0:T(8,128)(2,1)}) fusion(f32[1024,1408]{1,0:T(8,128)} %fusion.50, f32[1024,1408]{1,0:T(8,128)} %fusion.49, bf16[1024,2048]{1,0:T(8,128)(2,1)} %bitcast.241, bf16[2048,1408]{1,0:T(8,128)(2,1)S(1)} %bitcast.230), kind=kOutput, calls=%fused_computation.19 | convolution fusion | flops 5927206912 | bytes 30146560 | tf_op jit(solution)/shard_map/dot_general | solution.py:25
  558.3 10.6 fusion.51
  568.9 9.1 add_convert_fusion
  579.9 6.9 convolution_convert_fusion.3
  589.9 8.6 convolution_convert_fusion.2
  601.5 9.1 convolution_convert_fusion.1
  610.6 14.3 %collective-permute-done.8 = bf16[256,2048]{1,0:T(8,128)(2,1)S(1)} collective-permute-done((bf16[256,2048]{1,0:T(8,128)(2,1)S(1)}, bf16[256,2048]{1,0:T(8,128)(2,1)S(1)}, u32[]{:S(2)}, u32[]{:S(2)}) %collective-permute-start.8) | collective-permute-done | bytes 1048608 | tf_op jit(solution)/shard_map/ppermute | solution.py:966
  626.0 21.1 %collective-permute-done.6 = bf16[256,2048]{1,0:T(8,128)(2,1)S(1)} collective-permute-done((bf16[256,2048]{1,0:T(8,128)(2,1)S(1)}, bf16[256,2048]{1,0:T(8,128)(2,1)S(1)}, u32[]{:S(2)}, u32[]{:S(2)}) %collective-permute-start.6) | collective-permute-done | bytes 1048608 | tf_op jit(solution)/shard_map/ppermute | solution.py:966
  651.8 8.1 convolution_convert_fusion
  659.8 212.9 %reduce_2.1 = (bf16[4,64,1408]{2,1,0:T(8,128)(2,1)}, bf16[4,64,1408]{2,1,0:T(8,128)(2,1)}, f32[176,2048]{1,0:T(8,128)}) custom-call(bf16[4,8,64,1408]{3,2,1,0:T(8,128)(2,1)} %bitcast.237, bf16[4,8,64,1408]{3,2,1,0:T(8,128)(2,1)} %bitcast.238, bf16[8,176,2048]{2,1,0:T(8,128)(2,1)} %bitcast.239), custom_call_target="tpu_custom_call" | custom-call | bytes 34603008 | tf_op jit(solution)/shard_map/reduce_2/pallas_call | solution.py:949
  882.3 6.1 fusion.52.gmix_ref
  888.4 6.2 convolution_convert_fusion.4
  894.7 56.0 %mixer_bwd.1 = (bf16[1024,3200]{1,0:T(8,128)(2,1)}, f32[4,8,2048]{2,1,0:T(8,128)}, f32[4,8,256]{2,1,0:T(8,128)}) custom-call(f32[1024,3200]{1,0:T(8,128)} %fusion.24.proj_ref, f32[1024,128]{1,0:T(8,128)} %slice_convert_fusion.2.pos_ref, f32[8,2048]{1,0:T(8,128)} %select_maximum_fusion.2.conv_ref, f32[8,128]{1,0:T(8,128)} %select_maximum_fusion.6.prm_ref, ...), custom_call_target="tpu_custom_call" | custom-call | flops 49999998976 | bytes 40000000 | tf_op jit(solution)/shard_map/mixer_bwd/pallas_call | solution.py:272
  952.1 21.3 %fusion.43 = (bf16[1024,2048]{1,0:T(8,128)(2,1)}, f32[2048]{0:T(1024)S(1)}) fusion(f32[1024]{0:T(1024)S(1)} %copy-done.39, bf16[1024,2176]{1,0:T(8,128)(2,1)} %bitcast.213, bf16[1024,3200]{1,0:T(8,128)(2,1)} %get-tuple-element.43, bf16[2048,3200]{1,0:T(8,128)(2,1)} %bitcast.219), kind=kOutput, calls=%fused_computation.148 | convolution fusion | flops 13432256512 | bytes 28061696 | tf_op jit(solution)/shard_map/dot_general | solution.py:25
  974.1 21.3 %fusion.1 = bf16[2048,3200]{1,0:T(8,128)(2,1)} fusion(f32[2048,16]{1,0:T(8,128)S(1)} %reshape.305, f32[2048,1]{1,0:T(8,128)S(1)} %copy.128, f32[2048,1]{1,0:T(8,128)S(1)} %copy.127, bf16[1024,3200]{1,0:T(8,128)(2,1)} %get-tuple-element.43, f32[2048]{0:T(1024)S(1)} %copy-done.31, f32[1024]{0:T(1024)S(1)} %copy-done.39, bf16[1024,2176]{1,0:T(8,128)(2,1)} %bitcast.214), kind=kOutput, calls=%fused_computation.4 | convolution fusion | flops 13495697408 | bytes 24014848 | tf_op jit(solution)/shard_map/dot_general | solution.py:25
  996.0 226.8 %reduce_3.1 = (bf16[4,64,3200]{2,1,0:T(8,128)(2,1)}, f32[128,2048]{1,0:T(8,128)}, f32[256,2048]{1,0:T(8,128)}, f32[8,128]{1,0:T(8,128)}) custom-call(bf16[4,8,64,3200]{3,2,1,0:T(8,128)(2,1)} %bitcast.236, bf16[8,128,2048]{2,1,0:T(8,128)(2,1)} %bitcast.248, bf16[4,256,2048]{2,1,0:T(8,128)(2,1)} %bitcast.249, f32[8,128]{1,0:T(8,128)} %fusion.36.refs_3_), custom_call_target="tpu_custom_call" | custom-call | bytes 42999808 | tf_op jit(solution)/shard_map/reduce_3/pallas_call | solution.py:949
  (239 shorter events, 111.1 us)
Async XLA Ops:
  385.3 24.7 %copy-start.30 = (f32[2048]{0:T(1024)}, f32[2048]{0:T(1024)S(1)}, u32[]{:S(2)}) copy-start(f32[2048]{0:T(1024)S(1)} %convert_reduce_fusion) | copy-start | bytes 24580
  386.5 143.4 %copy-start.38 = (f32[1024]{0:T(1024)}, f32[1024]{0:T(1024)S(1)}, u32[]{:S(2)}) copy-start(f32[1024]{0:T(1024)S(1)} %add_rsqrt_fusion) | copy-start | bytes 12292
  387.0 24.2 %copy-start.40 = (f32[256]{0:T(256)S(1)}, f32[256]{0:T(256)}, u32[]{:S(2)}) copy-start(f32[256]{0:T(256)} %param.26) | copy-start | bytes 3076
  411.9 43.5 %copy-start.8 = (bf16[8,128,2048]{2,1,0:T(8,128)(2,1)S(1)}, bf16[8,128,2048]{2,1,0:T(8,128)(2,1)}, u32[]{:S(2)}) copy-start(bf16[8,128,2048]{2,1,0:T(8,128)(2,1)} %copy-done.7) | copy-start | bytes 12582916
  462.5 4.2 collective-permute-start
  468.4 25.5 %collective-permute-start.1 = (bf16[256,2048]{1,0:T(8,128)(2,1)}, bf16[256,2048]{1,0:T(8,128)(2,1)}, u32[]{:S(2)}, u32[]{:S(2)}) collective-permute-start(bf16[256,2048]{1,0:T(8,128)(2,1)} %fusion.20), channel_id=1, source_target_pairs={{0,16},{8,24},{16,0},{24,8},{1,17},{9,25},{17,1},{25,9},{2,18},{10... | collective-permute-start | bytes 3145736 | tf_op jit(solution)/shard_map/ppermute | solution.py:966
  472.2 49.0 %slice-start = ((s8[5767168]{0:T(1024)(128)(4,1)}), s8[1572864]{0:T(1024)(128)(4,1)S(1)}, s32[]{:S(2)}) async-start(s8[5767168]{0:T(1024)(128)(4,1)} %bitcast.220), calls=%async_computation | async-start | bytes 3145728
  473.8 47.4 %slice-start.1 = ((s8[5767168]{0:T(1024)(128)(4,1)}), s8[4194304]{0:T(1024)(128)(4,1)S(1)}, s32[]{:S(2)}) async-start(s8[5767168]{0:T(1024)(128)(4,1)} %bitcast.220), calls=%async_computation.1 | async-start | bytes 8388608
  473.8 47.4 %copy-start.11 = (bf16[4,256,2048]{2,1,0:T(8,128)(2,1)S(1)}, bf16[4,256,2048]{2,1,0:T(8,128)(2,1)}, u32[]{:S(2)}) copy-start(bf16[4,256,2048]{2,1,0:T(8,128)(2,1)} %copy-done.10) | copy-start | bytes 12582916
  496.5 34.0 %copy-start.13 = (f32[256,2048]{1,0:T(8,128)}, f32[256,2048]{1,0:T(8,128)S(1)}, u32[]{:S(2)}) copy-start(f32[256,2048]{1,0:T(8,128)S(1)} %get-tuple-element.60) | copy-start | bytes 6291460
  496.8 24.4 %collective-permute-start.3 = (bf16[256,2048]{1,0:T(8,128)(2,1)S(1)}, bf16[256,2048]{1,0:T(8,128)(2,1)S(1)}, u32[]{:S(2)}, u32[]{:S(2)}) collective-permute-start(bf16[256,2048]{1,0:T(8,128)(2,1)S(1)} %multiply_convert_fusion.3), channel_id=1, source_target_pairs={{0,16},{8,24},{16,0},{24,8},{1,17},{9,25},{17,1},{25,9},{2,18},{10... | collective-permute-start | bytes 3145736 | tf_op jit(solution)/shard_map/ppermute | solution.py:966
  498.3 32.4 %collective-permute-start.2 = (bf16[256,2048]{1,0:T(8,128)(2,1)S(1)}, bf16[256,2048]{1,0:T(8,128)(2,1)S(1)}, u32[]{:S(2)}, u32[]{:S(2)}) collective-permute-start(bf16[256,2048]{1,0:T(8,128)(2,1)S(1)} %multiply_convert_fusion.3), channel_id=1, source_target_pairs={{0,8},{8,0},{16,24},{24,16},{1,9},{9,1},{17,25},{25,17},{2,10},{10... | collective-permute-start | bytes 3145736 | tf_op jit(solution)/shard_map/ppermute | solution.py:966
  521.2 9.6 collective-permute-start.4
  578.5 20.0 %collective-permute-start.7 = (bf16[2,256,2048]{2,1,0:T(8,128)(2,1)S(1)}, bf16[2,256,2048]{2,1,0:T(8,128)(2,1)S(1)}, u32[]{:S(2)}, u32[]{:S(2)}) collective-permute-start(bf16[2,256,2048]{2,1,0:T(8,128)(2,1)S(1)} %pad_maximum_fusion.5), channel_id=1, source_target_pairs={{0,8},{8,0},{16,24},{24,16},{1,9},{9,1},{17,25},{25,17},{2,10},{10... | collective-permute-start | bytes 6291464 | tf_op jit(solution)/shard_map/ppermute | solution.py:966
  587.3 13.3 %collective-permute-start.5 = (bf16[2,256,2048]{2,1,0:T(8,128)(2,1)S(1)}, bf16[2,256,2048]{2,1,0:T(8,128)(2,1)S(1)}, u32[]{:S(2)}, u32[]{:S(2)}) collective-permute-start(bf16[2,256,2048]{2,1,0:T(8,128)(2,1)S(1)} %pad_maximum_fusion.4), channel_id=1, source_target_pairs={{0,8},{8,0},{16,24},{24,16},{1,9},{9,1},{17,25},{25,17},{2,10},{10... | collective-permute-start | bytes 6291464 | tf_op jit(solution)/shard_map/ppermute | solution.py:966
  598.9 26.0 %collective-permute-start.8 = (bf16[256,2048]{1,0:T(8,128)(2,1)S(1)}, bf16[256,2048]{1,0:T(8,128)(2,1)S(1)}, u32[]{:S(2)}, u32[]{:S(2)}) collective-permute-start(bf16[256,2048]{1,0:T(8,128)(2,1)S(1)} %fusion.13), channel_id=1, source_target_pairs={{0,16},{8,24},{16,0},{24,8},{1,17},{9,25},{17,1},{25,9},{2,18},{10... | collective-permute-start | bytes 3145736 | tf_op jit(solution)/shard_map/ppermute | solution.py:966
  600.9 46.1 %collective-permute-start.6 = (bf16[256,2048]{1,0:T(8,128)(2,1)S(1)}, bf16[256,2048]{1,0:T(8,128)(2,1)S(1)}, u32[]{:S(2)}, u32[]{:S(2)}) collective-permute-start(bf16[256,2048]{1,0:T(8,128)(2,1)S(1)} %fusion.15), channel_id=1, source_target_pairs={{0,16},{8,24},{16,0},{24,8},{1,17},{9,25},{17,1},{25,9},{2,18},{10... | collective-permute-start | bytes 3145736 | tf_op jit(solution)/shard_map/ppermute | solution.py:966
  610.6 36.4 %copy-start.24 = (bf16[256,2048]{1,0:T(8,128)(2,1)S(1)}, bf16[256,2048]{1,0:T(8,128)(2,1)}, u32[]{:S(2)}) copy-start(bf16[256,2048]{1,0:T(8,128)(2,1)} %param.16) | copy-start | bytes 3145732
  610.6 36.4 %copy-start.37 = (f32[256]{0:T(256)S(1)}, f32[256]{0:T(256)}, u32[]{:S(2)}) copy-start(f32[256]{0:T(256)} %copy-done.36) | copy-start | bytes 3076
  626.0 25.8 %copy-start.12 = (bf16[4,256,2048]{2,1,0:T(8,128)(2,1)S(1)}, bf16[4,256,2048]{2,1,0:T(8,128)(2,1)}, u32[]{:S(2)}) copy-start(bf16[4,256,2048]{2,1,0:T(8,128)(2,1)} %copy-done.10) | copy-start | bytes 12582916
  650.2 225.0 %collective-permute-start.10 = (bf16[256,2048]{1,0:T(8,128)(2,1)S(1)}, bf16[256,2048]{1,0:T(8,128)(2,1)S(1)}, u32[]{:S(2)}, u32[]{:S(2)}) collective-permute-start(bf16[256,2048]{1,0:T(8,128)(2,1)S(1)} %get-tuple-element.57), channel_id=1, source_target_pairs={{0,16},{8,24},{16,0},{24,8},{1,17},{9,25},{17,1},{25,9},{2,18},{10... | collective-permute-start | bytes 3145736 | tf_op jit(solution)/shard_map/ppermute | solution.py:966
  875.1 2.9 collective-permute-start.9
  875.2 4.3 collective-permute-start.11
  894.7 57.4 %copy-start.39 = (f32[1024]{0:T(1024)S(1)}, f32[1024]{0:T(1024)}, u32[]{:S(2)}) copy-start(f32[1024]{0:T(1024)} %copy-done.38) | copy-start | bytes 12292
  (44 other events, 286.3 us)

commit v3 on v2

--- a/solution.py
+++ b/solution.py
@@ -104,7 +104,7 @@
     )
 
 
-def mixer_fwd_kernel(proj_ref, pos_ref, conv_ref, prm_ref, gain_ref, mixed_ref, inv_ref, new_ref):
+def mixer_forward(proj_ref, pos_ref, conv_ref, prm_ref, gain_ref, mixed_ref, inv_ref, new_ref):
     width = proj_ref.shape[1]
     tail_ref = proj_ref.at[:, width - TAIL :]
     pos, row_i, row_j, lower, _, _, _, _, beta_all, cum, cum_t = group_terms(tail_ref, prm_ref, pos_ref)
@@ -144,7 +144,7 @@
         new_ref[:, head * DV : (head + 1) * DV] = news[head]
 
 
-def mixer_bwd_kernel(
+def mixer_back(
     proj_ref, pos_ref, conv_ref, prm_ref, gain_ref, inv_ref, new_ref, gmix_ref, gproj_ref, gconv_ref, misc_ref
 ):
     width = proj_ref.shape[1]
@@ -159,8 +159,6 @@
     grad_cum = jnp.zeros((rows, TAIL), F32)
     grad_beta_all = jnp.zeros((rows, TAIL), F32)
     gain_sum = jnp.zeros((1, DV), F32)
-    gconv_ref[...] = jnp.zeros_like(gconv_ref)
-    misc_ref[...] = jnp.zeros_like(misc_ref)
     for head in range(LH):
         sq, sk, sv, sg = head_slices(head)
         q_raw, k_raw, v_raw = proj_ref[:, sq], proj_ref[:, sk], proj_ref[:, sv]
@@ -223,83 +221,21 @@
             moved, sums = conv_back(grad, part, conv_ref[:, where], pos)
             gproj_ref[:, where] = moved.astype(BF16)
             for tap in range(CONV):
-                gconv_ref[0, tap : tap + 1, where] = sums[tap]
+                gconv_ref[tap : tap + 1, where] += sums[tap]
         gproj_ref[:, sg] = grad_gate.astype(BF16)
     grad_log = mmx(lower_f, grad_cum, ((0,), (0,)))
     grad_step = grad_log * prm_ref[0:1] * sigmoid(shifted)
     grad_tail = grad_step + grad_beta_all * beta_all * (1.0 - beta_all)
     gproj_ref[:, width - TAIL :] = grad_tail.astype(BF16)
-    misc_ref[0, 0:1, :] = gain_sum
-    misc_ref[0, 1:2, 0:TAIL] = jnp.sum(grad_log * log_decay, axis=0, keepdims=True)
-    misc_ref[0, 2:3, 0:TAIL] = jnp.sum(grad_step, axis=0, keepdims=True)
-
-
-VMEM_LIMIT = 56 * 1024 * 1024
-
-
-def mixer_fwd(proj, pos, conv, prm, gain):
-    total, width = proj.shape
-    rows = total // TP
-    return pl.pallas_call(
-        mixer_fwd_kernel,
-        grid=(TP,),
-        in_specs=[
-            pl.BlockSpec((rows, width), lambda g: (g, 0)),
-            pl.BlockSpec((rows, TAIL), lambda g: (g, 0)),
-            pl.BlockSpec(conv.shape, lambda g: (0, 0)),
-            pl.BlockSpec(prm.shape, lambda g: (0, 0)),
-            pl.BlockSpec(gain.shape, lambda g: (0, 0)),
-        ],
-        out_specs=[
-            pl.BlockSpec((rows, LH * DV), lambda g: (g, 0)),
-            pl.BlockSpec((LH, rows, rows), lambda g: (g, 0, 0)),
-            pl.BlockSpec((rows, LH * DV), lambda g: (g, 0)),
-        ],
-        out_shape=[
-            jax.ShapeDtypeStruct((total, LH * DV), BF16),
-            jax.ShapeDtypeStruct((TP * LH, rows, rows), F32),
-            jax.ShapeDtypeStruct((total, LH * DV), F32),
-        ],
-        compiler_params=pltpu.CompilerParams(vmem_limit_bytes=VMEM_LIMIT),
-        cost_estimate=pl.CostEstimate(flops=30_000_000_000, bytes_accessed=30_000_000, transcendentals=5_000_000),
-        name="mixer_fwd",
-    )(proj, pos, conv, prm, gain)
-
-
-def mixer_bwd(proj, pos, conv, prm, gain, inv, new, gmix):
-    total, width = proj.shape
-    rows = total // TP
-    return pl.pallas_call(
-        mixer_bwd_kernel,
-        grid=(TP,),
-        in_specs=[
-            pl.BlockSpec((rows, width), lambda g: (g, 0)),
-            pl.BlockSpec((rows, TAIL), lambda g: (g, 0)),
-            pl.BlockSpec(conv.shape, lambda g: (0, 0)),
-            pl.BlockSpec(prm.shape, lambda g: (0, 0)),
-            pl.BlockSpec(gain.shape, lambda g: (0, 0)),
-            pl.BlockSpec((LH, rows, rows), lambda g: (g, 0, 0)),
-            pl.BlockSpec((rows, LH * DV), lambda g: (g, 0)),
-            pl.BlockSpec((rows, LH * DV), lambda g: (g, 0)),
-        ],
-        out_specs=[
-            pl.BlockSpec((rows, width), lambda g: (g, 0)),
-            pl.BlockSpec((1, 8, conv.shape[1]), lambda g: (g, 0, 0)),
-            pl.BlockSpec((1, 8, DV), lambda g: (g, 0, 0)),
-        ],
-        out_shape=[
-            jax.ShapeDtypeStruct((total, width), BF16),
-            jax.ShapeDtypeStruct((TP, 8, conv.shape[1]), F32),
-            jax.ShapeDtypeStruct((TP, 8, DV), F32),
-        ],
-        compiler_params=pltpu.CompilerParams(vmem_limit_bytes=VMEM_LIMIT),
-        cost_estimate=pl.CostEstimate(flops=50_000_000_000, bytes_accessed=40_000_000, transcendentals=5_000_000),
-        name="mixer_bwd",
-    )(proj, pos, conv, prm, gain, inv, new, gmix)
+    misc_ref[0:1, :] += gain_sum
+    misc_ref[1:2, 0:TAIL] += jnp.sum(grad_log * log_decay, axis=0, keepdims=True)
+    misc_ref[2:3, 0:TAIL] += jnp.sum(grad_step, axis=0, keepdims=True)
+
+
+VMEM_LIMIT = 60 * 1024 * 1024
 
 
 MESH = pl.DeviceIdType.MESH
-AHEAD = 3
 
 
 class Place:
@@ -348,12 +284,23 @@
     )
 
 
+def pieces(columns, count):
+    tiles = columns // 128
+    edges = [128 * (tiles * c // count) for c in range(count + 1)]
+    return [(edge, after - edge) for edge, after in zip(edges, edges[1:])]
+
+
+def nothing():
+    return None
+
+
 class Gather:
-    def __init__(self, place, views, ready, up_send, down_send, z_recv, y_send, y_recv, pair_send, pair_recv):
-        self.p, self.views, self.ready = place, views, ready
+    def __init__(self, place, ahead, lag, views, ready, up_send, down_send, z_recv, y_send, y_recv, pair_send, pair_recv):
+        self.p, self.ahead, self.views, self.ready = place, ahead, views, ready
         self.up_send, self.down_send, self.z_recv = up_send, down_send, z_recv
         self.y_send, self.y_recv, self.pair_send, self.pair_recv = y_send, y_recv, pair_send, pair_recv
-        self.ticks = len(views) + place.nz - 1
+        self.lag = lag
+        self.ticks = len(views) + lag * (place.nz - 1)
 
     @staticmethod
     def scratch(units, nz):
@@ -434,11 +381,11 @@
 
     def tick(self, t):
         p, nz = self.p, self.p.nz
-        for u in range(AHEAD + 1) if t == 0 else (t + AHEAD,):
+        for u in range(self.ahead + 1) if t == 0 else (t + self.ahead,):
             if u < len(self.views):
                 self.own(u)
         for s in range(1, nz):
-            u = t - s
+            u = t - s * self.lag
             if not 0 <= u < len(self.views):
                 continue
 
@@ -462,7 +409,7 @@
 
                 self.unless_skipped(u, nz - s, self.over_y(u, nz - s).start)
 
-            if s == min(AHEAD, nz - 1) and self.odd(u):
+            if s == nz - 1 and self.odd(u):
                 self.wait_y(u, 0)
                 self.pair(u).start()
 
@@ -493,7 +440,7 @@
                     self.down(u, r).wait_send()
 
 
-def gather_kernel(nf, packs, shards, groups, *refs):
+def gather_kernel(nf, splits, packs, shards, groups, *refs):
     count = len(packs) + len(shards) + groups
     ins, outs = refs[:count], refs[count : 2 * count]
     to_send, to_recv, near_send, near_recv, local_sem = refs[2 * count : 2 * count + 5]
@@ -539,12 +486,14 @@
     for i, whole in enumerate(packs):
         for m in range(TP if whole else 0):
             source = p.dp(m)[0] if m else p.d
-            views.append(lambda f, i=i, d=source: pack_out[i].at[d, f])
-            ready.append(partial(wait_exchange, i, m) if m else local(i).wait)
+            for c, (start, size) in enumerate(pieces(pack_in[i].shape[-1], splits[0])):
+                views.append(lambda f, i=i, d=source, at=pl.ds(start, size): pack_out[i].at[d, f, :, at])
+                ready.append(nothing if c else partial(wait_exchange, i, m) if m else local(i).wait)
     for i in range(len(shards)):
-        views.append(lambda f, i=i: shard_out[i].at[f])
-        ready.append(local(len(packs) + i).wait)
-    gather = Gather(p, views, ready, *refs[2 * count + 5 :])
+        for c, (start, size) in enumerate(pieces(shard_in[i].shape[-1], splits[1])):
+            views.append(lambda f, i=i, at=pl.ds(start, size): shard_out[i].at[f, :, at])
+            ready.append(nothing if c else local(len(packs) + i).wait)
+    gather = Gather(p, 3, 1, views, ready, *refs[2 * count + 5 :])
     for n in range(count):
         local(n).start()
     for m in (1, 2, 3):
@@ -577,7 +526,7 @@
         local(len(packs) + len(shards) + j).wait()
 
 
-def gather_all(nf, collective_id, packs, shards, groups):
+def gather_all(nf, collective_id, splits, packs, shards, groups):
     marks = tuple(whole for _, whole in packs)
     ins = [array for array, _ in packs] + list(shards) + list(groups)
     outs = (
@@ -588,11 +537,11 @@
         + [jax.ShapeDtypeStruct((nf,) + array.shape, array.dtype) for array in shards]
         + [jax.ShapeDtypeStruct((TP,) + array.shape, array.dtype) for array in groups]
     )
-    units = TP * sum(marks) + len(shards)
+    units = TP * sum(marks) * splits[0] + len(shards) * splits[1]
     sent = sum(out.size * 2 for out in outs)
     any_space = pl.BlockSpec(memory_space=pl.ANY)
     return pl.pallas_call(
-        partial(gather_kernel, nf, marks, (True,) * len(shards), len(groups)),
+        partial(gather_kernel, nf, splits, marks, (True,) * len(shards), len(groups)),
         in_specs=[any_space] * len(ins),
         out_specs=[any_space] * len(outs),
         out_shape=outs,
@@ -629,11 +578,211 @@
     lax.fori_loop(0, lead * (rows // size), body, 0)
 
 
+PER = 2
+
+
+def forward_kernel(nf, split, *refs):
+    (x_hbm, w_hbm, out_hbm, pos_ref, conv_ref, prm_ref, gain_ref, gain_two_ref, tokens_ref), refs = refs[:9], refs[9:]
+    pack_in, shard_in, refs = refs[:2], refs[2], refs[3:]
+    (proj_hbm, mixed_hbm, inv_hbm, new_hbm, residual_ref, group_hbm), refs = refs[:6], refs[6:]
+    pack_out, shard_out, refs = refs[:2], refs[2], refs[3:]
+    (proj_ref, mixed_ref, inv_ref, new_ref, parts_ref, near_ref, stage_sem), refs = refs[:7], refs[7:]
+    (part_send, part_recv, group_send, group_recv, local_sem), refs = refs[:5], refs[5:]
+    (x_ref, w_ref, out_ref, normed_ref, load_sem), refs = refs[:5], refs[5:]
+    p = Place(nf)
+    quarter = w_hbm.shape[0] // 4
+    loads = [pltpu.make_async_copy(x_hbm, x_ref, load_sem.at[0])]
+    for k in range(4):
+        at = pl.ds(k * quarter, quarter)
+        loads.append(pltpu.make_async_copy(w_hbm.at[at], w_ref.at[at], load_sem.at[1 + k]))
+    loads.append(pltpu.make_async_copy(out_hbm, out_ref, load_sem.at[5]))
+    rows = tokens_ref.shape[0]
+    width = tokens_ref.shape[1]
+
+    local = [pltpu.make_async_copy(pack_in[i], pack_out[i].at[:, p.f], local_sem.at[i]) for i in range(2)]
+    local.append(pltpu.make_async_copy(shard_in, shard_out.at[p.f], local_sem.at[2]))
+
+    views, ready = [], []
+    for i in range(2):
+        for d in range(TP):
+            views.append(lambda f, i=i, d=d: pack_out[i].at[d, f])
+            ready.append(nothing if d else local[i].wait)
+    for c, (start, size) in enumerate(pieces(width, split)):
+        views.append(lambda f, at=pl.ds(start, size): shard_out.at[f, :, at])
+        ready.append(nothing if c else local[2].wait)
+    p.greet()
+    for copy in local:
+        copy.start()
+    gather = Gather(p, 3, 1, views, ready, *refs)
+
+    def part_copy(k):
+        src, mask = ((parts_ref.at[1], 1), (parts_ref.at[3], 1), (near_ref.at[1], 2))[k]
+        return send(src, near_ref.at[k], part_send.at[k], part_recv.at[k], p.dp(mask))
+
+    def group_copy(k):
+        src, dst, mask = ((normed_ref, 2, 2), (normed_ref, 1, 1), (group_hbm.at[2], 3, 1))[k]
+        return send(src, group_hbm.at[dst], group_send.at[k], group_recv.at[k], p.dp(mask))
+
+    own_normed = pltpu.make_async_copy(normed_ref, group_hbm.at[0], load_sem.at[6])
+
+    def stage_copies(g):
+        at = pl.ds(pl.multiple_of(g * rows, rows), rows)
+        return (
+            pltpu.make_async_copy(proj_ref, proj_hbm.at[at], stage_sem.at[0]),
+            pltpu.make_async_copy(mixed_ref, mixed_hbm.at[at], stage_sem.at[1]),
+            pltpu.make_async_copy(inv_ref, inv_hbm.at[pl.ds(pl.multiple_of(g * LH, LH), LH)], stage_sem.at[2]),
+            pltpu.make_async_copy(new_ref, new_hbm.at[at], stage_sem.at[3]),
+        )
+
+    columns = w_ref.shape[1]
+    tile = 640
+    gather.tick(0)
+    for load in loads:
+        load.start()
+    for load in loads:
+        load.wait()
+
+    def group(i, _):
+        half = i // 2
+        g = 2 * i + 1 - half * (3 + 4 * (i - 2 * half))
+
+        @pl.when(i > 0)
+        def _():
+            for copy in stage_copies(0):
+                copy.wait()
+
+        at = pl.ds(pl.multiple_of(g * rows, rows), rows)
+
+        def project(c, _):
+            where = pl.ds(pl.multiple_of(c * tile, tile), tile)
+            proj_ref[:, where] = mm(x_ref[at, :], w_ref[:, where])
+            return 0
+
+        lax.fori_loop(0, columns // tile, project, 0)
+        for step in range(TP):
+
+            @pl.when(i == step)
+            def _():
+                for t in range(PER // 2):
+                    gather.tick(1 + PER * step + t)
+
+        mixer_forward(proj_ref, pos_ref.at[at], conv_ref, prm_ref, gain_ref, mixed_ref, inv_ref, new_ref)
+        for copy in stage_copies(g):
+            copy.start()
+
+        def project_out(c, _):
+            where = pl.ds(pl.multiple_of(c * 512, 512), 512)
+            parts_ref[g, :, where] = mm(mixed_ref[...], out_ref[:, where]).astype(BF16)
+            return 0
+
+        lax.fori_loop(0, width // 512, project_out, 0)
+        for step in range(TP):
+
+            @pl.when(i == step)
+            def _():
+                if step < 2:
+                    part_copy(step).start()
+                if step == 2:
+                    part_copy(1).wait_recv()
+                    add_into(parts_ref.at[2], [parts_ref.at[2], near_ref.at[1]])
+                    send(parts_ref.at[2], near_ref.at[2], part_send.at[2], part_recv.at[2], p.dp(2)).start()
+                for t in range(PER // 2, PER):
+                    gather.tick(1 + PER * step + t)
+
+        return 0
+
+    lax.fori_loop(0, TP, group, 0)
+    part_copy(0).wait_recv()
+    far = send(parts_ref.at[2], near_ref.at[2], part_send.at[2], part_recv.at[2], p.dp(2))
+    far.wait_recv()
+
+    def norm(c, _):
+        where = pl.ds(pl.multiple_of(c * 64, 64), 64)
+        total = tokens_ref[where, :].astype(F32) + parts_ref[0, where, :].astype(F32)
+        total = total + near_ref[0, where, :].astype(F32) + near_ref[2, where, :].astype(F32)
+        residual_ref[where, :] = total
+        scale = lax.rsqrt(jnp.mean(total * total, axis=-1, keepdims=True) + EPS)
+        normed_ref[where, :] = (total * scale * gain_two_ref[0:1]).astype(BF16)
+        return 0
+
+    lax.fori_loop(0, rows // 64, norm, 0)
+    group_copy(0).start()
+    group_copy(1).start()
+    own_normed.start()
+    for t in range(1 + PER * TP, gather.ticks):
+        gather.tick(t)
+        if t == min(2 + PER * TP, gather.ticks - 1):
+            group_copy(0).wait_recv()
+            group_copy(2).start()
+    gather.finish()
+    for copy in stage_copies(0):
+        copy.wait()
+    part_copy(0).wait_send()
+    part_copy(1).wait_send()
+    far.wait_send()
+    own_normed.wait()
+    for k in (1, 2):
+        group_copy(k).wait_recv()
+    for k in range(3):
+        group_copy(k).wait_send()
+
+
+def forward(nf, x, w, out, pos, conv, prm, gain, gain_two, tokens, packs, shard):
+    total, columns = x.shape[0], w.shape[1]
+    rows, width = tokens.shape
+    split = 4 if nf <= 8 else 1
+    vmem, any_space = pl.BlockSpec(memory_space=pltpu.VMEM), pl.BlockSpec(memory_space=pl.ANY)
+    outs = [
+        jax.ShapeDtypeStruct((total, columns), F32),
+        jax.ShapeDtypeStruct((total, LH * DV), BF16),
+        jax.ShapeDtypeStruct((TP * LH, rows, rows), F32),
+        jax.ShapeDtypeStruct((total, LH * DV), F32),
+        jax.ShapeDtypeStruct((rows, width), F32),
+        jax.ShapeDtypeStruct((TP, rows, width), BF16),
+    ]
+    outs += [jax.ShapeDtypeStruct((TP, nf) + pack.shape[1:], BF16) for pack in packs]
+    outs += [jax.ShapeDtypeStruct((nf,) + shard.shape, BF16)]
+    return pl.pallas_call(
+        partial(forward_kernel, nf, split),
+        in_specs=[any_space] * 3 + [vmem] * 6 + [any_space] * 3,
+        out_specs=[any_space] * 4 + [vmem] + [any_space] * 4,
+        out_shape=outs,
+        scratch_shapes=[
+            pltpu.VMEM((rows, columns), F32),
+            pltpu.VMEM((rows, LH * DV), BF16),
+            pltpu.VMEM((LH, rows, rows), F32),
+            pltpu.VMEM((rows, LH * DV), F32),
+            pltpu.VMEM((TP, rows, width), BF16),
+            pltpu.VMEM((3, rows, width), BF16),
+            pltpu.SemaphoreType.DMA((4,)),
+            pltpu.SemaphoreType.DMA((3,)),
+            pltpu.SemaphoreType.DMA((3,)),
+            pltpu.SemaphoreType.DMA((3,)),
+            pltpu.SemaphoreType.DMA((3,)),
+            pltpu.SemaphoreType.DMA((3,)),
+            pltpu.VMEM(x.shape, BF16),
+            pltpu.VMEM(w.shape, BF16),
+            pltpu.VMEM(out.shape, BF16),
+            pltpu.VMEM((rows, width), BF16),
+            pltpu.SemaphoreType.DMA((7,)),
+        ]
+        + Gather.scratch(2 * TP + split, nf // 2),
+        compiler_params=pltpu.CompilerParams(
+            collective_id=4, has_side_effects=True, vmem_limit_bytes=VMEM_LIMIT
+        ),
+        cost_estimate=pl.CostEstimate(flops=45_000_000_000, bytes_accessed=80_000_000, transcendentals=5_000_000),
+        name="forward",
+    )(x, w, out, pos, conv, prm, gain, gain_two, tokens, *packs, shard)
+
+
+AHEAD, OLD_FIRST = 2, True
+
+
 class Reduce:
-    def __init__(self, place, part, done, y_in, z_in, pair_in, sems):
+    def __init__(self, place, part, done, own, y_in, z_in, pair_in, sems):
         self.p, self.part, self.done = place, part, done
-        self.y_in, self.z_in, self.pair_in = y_in, z_in, pair_in
-        self.y_send, self.y_recv, self.z_send, self.z_recv, self.pair_send, self.pair_recv = sems
+        self.own, self.y_in, self.z_in, self.pair_in = own, y_in, z_in, pair_in
+        self.y_send, self.y_recv, self.z_send, self.z_recv, self.pair_send, self.pair_recv, self.load_sem = sems
         self.count = len(y_in)
         self.ticks = self.count + place.nz
 
@@ -641,12 +790,14 @@
     def scratch(blocks, nz):
         units = len(blocks)
         return (
-            [pltpu.VMEM((nz,) + block, BF16) for block in blocks]
+            [pltpu.VMEM((nz + u % 2,) + block, BF16) for u, block in enumerate(blocks)]
+            + [pltpu.VMEM((nz,) + block, BF16) for block in blocks]
             + [pltpu.VMEM((nz + 1,) + block, BF16) for block in blocks]
-            + [pltpu.VMEM(block, BF16) for block in blocks]
+            + [pltpu.VMEM(block if u % 2 else (8, 128), BF16) for u, block in enumerate(blocks)]
             + [pltpu.SemaphoreType.DMA((units, nz))] * 3
             + [pltpu.SemaphoreType.DMA((units, nz + 1))]
             + [pltpu.SemaphoreType.DMA((units,))] * 2
+            + [pltpu.SemaphoreType.DMA((units, nz + 1))]
         )
 
     def odd(self, u):
@@ -673,7 +824,7 @@
         send(ref, ref, self.z_send.at[u, 0], self.z_recv.at[u, slot], self.p.beside()).wait_recv()
 
     def pass_on(self, u, z0, arrived, slot, z):
-        own = self.part(u, z0 * 2 + self.p.y)
+        own = self.own[u].at[z0]
         here = self.y_in[u].at[z0]
         if self.odd(u):
             other = self.p.flip(self.p.z, 1)
@@ -689,81 +840,110 @@
             add_into(here, [own, here] + arrived)
         self.copy_z(u, z0, slot, z).start()
 
-    def tick(self, t):
+    def loads(self, u):
         p, nz = self.p, self.p.nz
-        if t < self.count:
-            if self.odd(t):
-                self.copy_pair(t).start()
-                other = p.flip(p.z, 1)
-                for z0 in range(nz):
-
-                    @pl.when((z0 != p.z) & (z0 != other))
-                    def _():
-                        self.copy_y(t, z0).start()
-            else:
-                for z0 in range(nz):
-                    self.copy_y(t, z0).start()
-        u = t - 1
-        if 0 <= u < self.count:
-            if self.odd(u):
-                self.copy_pair(u).wait_recv()
-                add_into(self.pair_in[u], [self.pair_in[u], self.part(u, p.z * 2 + 1 - p.y)])
-                self.copy_late(u).start()
+        copies = [
+            pltpu.make_async_copy(self.part(u, z0 * 2 + p.y), self.own[u].at[z0], self.load_sem.at[u, z0])
+            for z0 in range(nz)
+        ]
+        if self.odd(u):
+            src = self.part(u, p.z * 2 + 1 - p.y)
+            copies.append(pltpu.make_async_copy(src, self.own[u].at[nz], self.load_sem.at[u, nz]))
+        return copies
+
+    def begin(self, u):
+        p, nz = self.p, self.p.nz
+        if self.odd(u):
+            self.copy_pair(u).start()
             other = p.flip(p.z, 1)
             for z0 in range(nz):
-                needed = (z0 != p.z) & (z0 != other) if self.odd(u) else z0 != p.z
-
-                @pl.when(needed)
+
+                @pl.when((z0 != p.z) & (z0 != other))
                 def _():
-                    self.copy_y(u, z0).wait_recv()
-
-            @pl.when(p.z == nz - 1)
+                    self.copy_y(u, z0).start()
+        else:
+            for z0 in range(nz):
+                self.copy_y(u, z0).start()
+        for load in self.loads(u):
+            load.start()
+
+    def set_out(self, u):
+        p, nz = self.p, self.p.nz
+        for load in self.loads(u):
+            load.wait()
+        if self.odd(u):
+            self.copy_pair(u).wait_recv()
+            add_into(self.pair_in[u], [self.pair_in[u], self.own[u].at[nz]])
+            self.copy_late(u).start()
+        other = p.flip(p.z, 1)
+        for z0 in range(nz):
+            needed = (z0 != p.z) & (z0 != other) if self.odd(u) else z0 != p.z
+
+            @pl.when(needed)
             def _():
-                for z0 in range(nz - 1):
-                    self.pass_on(u, z0, [], z0, p.z - 1)
-
-            @pl.when(p.z == 0)
-            def _():
-                for z0 in range(nz - 1, 0, -1):
-                    self.pass_on(u, z0, [], nz if z0 == 1 else z0, p.z + 1)
-
-        for hop in range(1, nz):
-            u = t - 1 - hop
-            if not 0 <= u < self.count:
-                continue
-
-            @pl.when(p.z == nz - 1 - hop)
-            def _():
-                for z0 in range(nz - hop):
-                    self.wait_z(u, z0)
-                    if z0 < nz - 1 - hop:
-                        self.pass_on(u, z0, [self.z_in[u].at[z0]], z0, p.z - 1)
-
-            @pl.when(p.z == hop)
-            def _():
-                for z0 in range(nz - 1, hop - 1, -1):
-                    slot = nz if z0 == hop else z0
-                    self.wait_z(u, slot)
-                    if z0 > hop:
-                        self.pass_on(u, z0, [self.z_in[u].at[z0]], nz if z0 == hop + 1 else z0, p.z + 1)
-
-        u = t - nz
-        if 0 <= u < self.count:
-            self.copy_y(u, p.z).wait_recv()
-            own = [self.part(u, p.f), self.y_in[u].at[p.z]]
-            above, below = self.z_in[u].at[p.z], self.z_in[u].at[nz]
-
-            @pl.when(p.z == 0)
-            def _():
-                self.done(u, own + [above])
-
-            @pl.when(p.z == nz - 1)
-            def _():
-                self.done(u, own + [below])
-
-            @pl.when(p.over & p.under)
-            def _():
-                self.done(u, own + [above, below])
+                self.copy_y(u, z0).wait_recv()
+
+        @pl.when(p.z == nz - 1)
+        def _():
+            for z0 in range(nz - 1):
+                self.pass_on(u, z0, [], z0, p.z - 1)
+
+        @pl.when(p.z == 0)
+        def _():
+            for z0 in range(nz - 1, 0, -1):
+                self.pass_on(u, z0, [], nz if z0 == 1 else z0, p.z + 1)
+
+    def relay(self, u, hop):
+        p, nz = self.p, self.p.nz
+
+        @pl.when(p.z == nz - 1 - hop)
+        def _():
+            for z0 in range(nz - hop):
+                self.wait_z(u, z0)
+                if z0 < nz - 1 - hop:
+                    self.pass_on(u, z0, [self.z_in[u].at[z0]], z0, p.z - 1)
+
+        @pl.when(p.z == hop)
+        def _():
+            for z0 in range(nz - 1, hop - 1, -1):
+                slot = nz if z0 == hop else z0
+                self.wait_z(u, slot)
+                if z0 > hop:
+                    self.pass_on(u, z0, [self.z_in[u].at[z0]], nz if z0 == hop + 1 else z0, p.z + 1)
+
+    def settle(self, u):
+        p, nz = self.p, self.p.nz
+        self.copy_y(u, p.z).wait_recv()
+        own = [self.own[u].at[p.z], self.y_in[u].at[p.z]]
+        above, below = self.z_in[u].at[p.z], self.z_in[u].at[nz]
+
+        @pl.when(p.z == 0)
+        def _():
+            self.done(u, own + [above])
+
+        @pl.when(p.z == nz - 1)
+        def _():
+            self.done(u, own + [below])
+
+        @pl.when(p.over & p.under)
+        def _():
+            self.done(u, own + [above, below])
+
+    def tick(self, t):
+        for u in range(1 + AHEAD) if t == 0 else (t + AHEAD,):
+            if u < self.count:
+                self.begin(u)
+        stages = [(t - 1 - hop, hop) for hop in range(self.p.nz - 1, -1, -1)]
+        if not OLD_FIRST:
+            stages = stages[::-1]
+        for u, hop in stages:
+            if 0 <= u < self.count:
+                if hop:
+                    self.relay(u, hop)
+                else:
+                    self.set_out(u)
+        if 0 <= t - self.p.nz < self.count:
+            self.settle(t - self.p.nz)
 
     def finish(self):
         p, nz = self.p, self.p.nz
@@ -787,103 +967,175 @@
                     self.copy_z(u, z0, z0, p.z).wait_send()
 
 
-def reduce_kernel(nf, kinds, units, groups, vecs, *refs):
-    arrays = len(kinds)
-    count = arrays + groups + vecs
-    ins, outs, rest = refs[:count], refs[count : 2 * count], refs[2 * count :]
+class Owners:
+    def __init__(self, place, kinds, units, ins, outs, final, to_send, to_recv, to_local):
+        self.p, self.kinds, self.units, self.ins, self.outs = place, kinds, units, ins, outs
+        self.packs = [u for u, (i, _, _) in enumerate(units) if kinds[i]]
+        self.final = dict(zip(self.packs, final))
+        self.to_send, self.to_recv, self.to_local = to_send, to_recv, to_local
+
+    @staticmethod
+    def scratch(kinds, units, blocks):
+        final = [pltpu.VMEM(block, BF16) for block, unit in zip(blocks, units) if kinds[unit[0]]]
+        return final, [
+            pltpu.SemaphoreType.DMA((len(units), TP)),
+            pltpu.SemaphoreType.DMA((len(units), TP)),
+            pltpu.SemaphoreType.DMA((len(units),)),
+        ]
+
+    def part(self, u, f):
+        i, start, size = self.units[u]
+        columns = pl.ds(start, size)
+        return self.ins[i].at[:, f, :, columns] if self.kinds[i] else self.ins[i].at[f, :, columns]
+
+    def place(self, u, d):
+        i, start, size = self.units[u]
+        return self.outs[i].at[d, :, pl.ds(start, size)]
+
+    def copy(self, u, m):
+        target = self.p.dp(m)
+        src = self.final[u].at[target[0]]
+        return send(src, self.place(u, self.p.d), self.to_send.at[u, m], self.to_recv.at[u, m], target)
+
+    def local(self, u):
+        return pltpu.make_async_copy(self.final[u].at[self.p.d], self.place(u, self.p.d), self.to_local.at[u])
+
+    def done(self, u, sources):
+        i, start, size = self.units[u]
+        add_into(self.final[u] if self.kinds[i] else self.outs[i].at[:, pl.ds(start, size)], sources)
+
+    def send_off(self, u):
+        if u in self.final:
+            for m in (2, 3, 1):
+                self.copy(u, m).start()
+            self.local(u).start()
+
+    def finish(self):
+        for u in self.packs:
+            self.local(u).wait()
+            for m in (1, 2, 3):
+                self.copy(u, m).wait_send()
+                source = self.p.dp(m)
+                ref = self.place(u, source[0])
+                send(ref, ref, self.to_send.at[u, m], self.to_recv.at[u, m], source).wait_recv()
+
+
+def take(refs, *counts):
+    parts = []
+    for count in counts:
+        parts.append(refs[:count])
+        refs = refs[count:]
+    return parts + [refs]
+
+
+def reduce_kernel(nf, kinds, units, groups, chain, vecs, *refs):
+    arrays, n = len(kinds), len(units)
+    ins, group, more, vec, outs, group_outs, vec_out, refs = take(
+        refs, arrays, groups, 3 if chain else 0, vecs, arrays, 3 if chain else groups, vecs
+    )
     p = Place(nf)
     nz = p.nz
-    n = len(units)
-    y_in, z_in, pair_in, rest = rest[:n], rest[n : 2 * n], rest[2 * n : 3 * n], rest[3 * n :]
-    sems, rest = rest[:6], rest[6:]
-    packs = [u for u, (i, _, _) in enumerate(units) if kinds[i]]
-    final = dict(zip(packs, rest[: len(packs)]))
-    rest = rest[len(packs) :]
-    to_send, to_recv, to_local, rest = rest[0], rest[1], rest[2], rest[3:]
-    if groups:
-        group_in, group_sems, rest = rest[0], rest[1:3], rest[3:]
+    own, y_in, z_in, pair_in, sems, refs = take(refs, n, n, n, n, 7)
+    final, to_sems, (near, kept, near_send, near_recv, keep_sem), refs = take(
+        refs, sum(kinds[i] for i, _, _ in units), 3, 5
+    )
+    owners = Owners(p, kinds, units, ins, outs, final, *to_sems)
+    red = Reduce(p, owners.part, owners.done, own, y_in, z_in, pair_in, sems)
+    if chain:
+        (residual_ref, cotangent_ref, gain_ref), (sum_ref, all_ref, gain_sum_ref) = more, group_outs
+        normed_ref, spread_send, spread_recv, spread_local = refs
+        own_spread = pltpu.make_async_copy(normed_ref, all_ref.at[0], spread_local)
     if vecs:
-        vec_in, vec_own, vec_sems = rest[0], rest[1], rest[2:4]
-
-    def part(u, f):
-        i, start, size = units[u]
-        columns = pl.ds(start, size)
-        return ins[i].at[:, f, :, columns] if kinds[i] else ins[i].at[f, :, columns]
-
-    def owner_copy(u, m):
-        i, start, size = units[u]
-        target = p.dp(m)
-        return send(
-            final[u].at[target[0]],
-            outs[i].at[p.d, :, pl.ds(start, size)],
-            to_send.at[u, m],
-            to_recv.at[u, m],
-            target,
+        vec_in, vec_own, vec_send, vec_recv = refs
+
+    def group_copy(j, k):
+        src, mask = ((group[j].at[1], 1), (group[j].at[3], 1), (near.at[j, 1], 2))[k]
+        return send(src, near.at[j, k], near_send.at[j, k], near_recv.at[j, k], p.dp(mask))
+
+    def spread(k):
+        src, dst, mask = ((normed_ref, 2, 2), (normed_ref, 1, 1), (all_ref.at[2], 3, 1))[k]
+        return send(src, all_ref.at[dst], spread_send.at[k], spread_recv.at[k], p.dp(mask))
+
+    def keep(j, k):
+        return pltpu.make_async_copy(group[j].at[2 * k], kept.at[j, k], keep_sem.at[j, k])
+
+    def norm_back(c, gain_sum):
+        where = pl.ds(pl.multiple_of(c * 32, 32), 32)
+        grad = kept[0, 0, where, :].astype(F32) + near[0, 0, where, :].astype(F32)
+        grad = grad + near[0, 2, where, :].astype(F32)
+        value = residual_ref[where, :]
+        scale = lax.rsqrt(jnp.mean(value * value, axis=-1, keepdims=True) + EPS)
+        weighted = grad * gain_ref[0:1]
+        total = (
+            cotangent_ref[where, :].astype(F32)
+            + scale * weighted
+            - value * (scale * scale * scale * jnp.mean(value * weighted, axis=-1, keepdims=True))
         )
-
-    def owner_local(u):
-        i, start, size = units[u]
-        return pltpu.make_async_copy(final[u].at[p.d], outs[i].at[p.d, :, pl.ds(start, size)], to_local.at[u])
-
-    def done(u, sources):
-        i, start, size = units[u]
-        if kinds[i]:
-            add_into(final[u], sources)
-        else:
-            add_into(outs[i].at[:, pl.ds(start, size)], sources)
-
-    def wait_owner(u, m):
-        i, start, size = units[u]
-        source = p.dp(m)
-        ref = outs[i].at[source[0], :, pl.ds(start, size)]
-        send(ref, ref, to_send.at[u, m], to_recv.at[u, m], source).wait_recv()
-
-    def group_copy(j, k):
-        src, mask = ((ins[arrays + j].at[1], 1), (ins[arrays + j].at[3], 1), (group_in.at[j, 1], 2))[k]
-        return send(src, group_in.at[j, (0, 1, 2)[k]], group_sems[0].at[j, k], group_sems[1].at[j, k], p.dp(mask))
+        sum_ref[where, :] = total
+        normed_ref[where, :] = total.astype(BF16)
+        return gain_sum + jnp.sum(grad * value * scale, axis=0, keepdims=True)
 
     def vec_copy(k):
         device = (p.dp(1), p.dp(2), p.beside())[k]
-        return send(vec_own.at[k], vec_in.at[k], vec_sems[0].at[k], vec_sems[1].at[k], device)
+        return send(vec_own.at[k], vec_in.at[k], vec_send.at[k], vec_recv.at[k], device)
 
     def vec_z(k):
         z = lax.rem(p.z + k, nz)
-        return send(vec_own.at[3], vec_in.at[3 + p.z], vec_sems[0].at[2 + k], vec_sems[1].at[2 + k], p.at_z(z))
+        return send(vec_own.at[3], vec_in.at[3 + p.z], vec_send.at[2 + k], vec_recv.at[2 + k], p.at_z(z))
 
     def vec_step(k):
         if k:
             vec_copy(k - 1).wait()
             vec_own[k] = vec_own[k - 1] + vec_in[k - 1]
         else:
-            vec_own[0] = ins[arrays + groups][...]
+            vec_own[0] = vec[0][...]
         if k < 3:
             vec_copy(k).start()
 
     p.greet()
-    red = Reduce(p, part, done, y_in, z_in, pair_in, sems)
     for j in range(groups):
         group_copy(j, 0).start()
         group_copy(j, 1).start()
+        keep(j, 0).start()
+        keep(j, 1).start()
     for t in range(red.ticks):
         red.tick(t)
-        u = t - nz
-        if u in final:
-            for m in (2, 3, 1):
-                owner_copy(u, m).start()
-            owner_local(u).start()
+        if t >= nz:
+            owners.send_off(t - nz)
         if t == 0:
             for j in range(groups):
                 group_copy(j, 0).wait_recv()
                 group_copy(j, 1).wait_recv()
-                add_into(group_in.at[j, 1], [ins[arrays + j].at[2], group_in.at[j, 1]])
+                keep(j, 0).wait()
+                keep(j, 1).wait()
+                add_into(near.at[j, 1], [kept.at[j, 1], near.at[j, 1]])
                 group_copy(j, 2).start()
+        if t == 1:
+            if chain:
+                group_copy(0, 2).wait_recv()
+                rows, width = residual_ref.shape
+                gain_sum = lax.fori_loop(0, rows // 32, norm_back, jnp.zeros((1, width), F32))
+                gain_sum_ref[...] = jnp.broadcast_to(gain_sum, gain_sum_ref.shape)
+                spread(0).start()
+                spread(1).start()
+                own_spread.start()
+        if chain and t == 3:
+            spread(0).wait_recv()
+            spread(2).start()
         if vecs and t < 4:
             vec_step(t)
     for j in range(groups):
-        group_copy(j, 2).wait_recv()
-        add_into(outs[arrays + j], [ins[arrays + j].at[0], group_in.at[j, 0], group_in.at[j, 2]])
+        if not chain:
+            group_copy(j, 2).wait_recv()
+            add_into(group_outs[j], [kept.at[j, 0], near.at[j, 0], near.at[j, 2]])
         for k in range(3):
             group_copy(j, k).wait_send()
+    if chain:
+        own_spread.wait()
+        spread(1).wait_recv()
+        spread(2).wait_recv()
+        for k in range(3):
+            spread(k).wait_send()
     if vecs:
         vec_in[3 + p.z] = vec_own[3]
         for k in range(1, nz):
@@ -891,65 +1143,70 @@
         for k in range(1, nz):
             source = lax.rem(p.z - k + nz, nz)
             ref = vec_in.at[3 + source]
-            send(ref, ref, vec_sems[0].at[2 + k], vec_sems[1].at[2 + k], p.at_z(source)).wait_recv()
+            send(ref, ref, vec_send.at[2 + k], vec_recv.at[2 + k], p.at_z(source)).wait_recv()
         total = vec_in[3]
         for k in range(1, nz):
             total = total + vec_in[3 + k]
-        outs[arrays + groups][...] = total
+        vec_out[0][...] = total
         for k in range(1, nz):
             vec_z(k).wait_send()
     red.finish()
-    for u in packs:
-        owner_local(u).wait()
-        for m in (1, 2, 3):
-            owner_copy(u, m).wait_send()
-            wait_owner(u, m)
-
-
-def reduce_all(nf, collective_id, arrays, widths, groups=(), vec=None):
+    owners.finish()
+
+
+def make_units(nf, arrays, units):
+    kinds = tuple(array.ndim == 4 for array in arrays)
+    if nf > 8:
+        units = [(i, array.shape[-1]) for i, array in enumerate(arrays)]
+    start = [0] * len(arrays)
+    full, blocks = [], []
+    for i, size in units:
+        full.append((i, start[i], size))
+        start[i] += size
+        blocks.append(((TP,) if kinds[i] else ()) + (arrays[i].shape[-2], size))
+    assert all(done == array.shape[-1] for done, array in zip(start, arrays))
+    return kinds, tuple(full), blocks
+
+
+def reduce_outs(arrays, kinds):
+    vmem, any_space = pl.BlockSpec(memory_space=pltpu.VMEM), pl.BlockSpec(memory_space=pl.ANY)
+    outs = [
+        jax.ShapeDtypeStruct((TP,) + array.shape[2:], BF16) if kind else jax.ShapeDtypeStruct(array.shape[1:], F32)
+        for array, kind in zip(arrays, kinds)
+    ]
+    return outs, [any_space if kind else vmem for kind in kinds]
+
+
+def reduce_all(nf, collective_id, arrays, units, groups, chain=None, vec=None):
     nz = nf // 2
-    kinds = tuple(array.ndim == 4 for array in arrays)
-    units, blocks = [], []
-    for i, (array, width) in enumerate(zip(arrays, widths)):
-        for start in range(0, array.shape[-1], width):
-            size = min(width, array.shape[-1] - start)
-            units.append((i, start, size))
-            blocks.append(((TP,) if kinds[i] else ()) + (array.shape[-2], size))
-    final = [pltpu.VMEM(block, BF16) for block, unit in zip(blocks, units) if kinds[unit[0]]]
-    scratch = Reduce.scratch(blocks, nz) + final
-    scratch += [
-        pltpu.SemaphoreType.DMA((len(units), TP)),
-        pltpu.SemaphoreType.DMA((len(units), TP)),
-        pltpu.SemaphoreType.DMA((len(units),)),
-    ]
-    if groups:
-        scratch += [pltpu.VMEM((len(groups), 3) + groups[0].shape[1:], BF16)]
-        scratch += [pltpu.SemaphoreType.DMA((len(groups), 3))] * 2
+    kinds, units, blocks = make_units(nf, arrays, units)
+    final, to_sems = Owners.scratch(kinds, units, blocks)
+    scratch = Reduce.scratch(blocks, nz) + final + to_sems
+    group = groups[0]
+    scratch += [pltpu.VMEM((len(groups), 3) + group.shape[1:], BF16), pltpu.VMEM((len(groups), 2) + group.shape[1:], BF16)]
+    scratch += [pltpu.SemaphoreType.DMA((len(groups), 3))] * 2 + [pltpu.SemaphoreType.DMA((len(groups), 2))]
+    vmem = pl.BlockSpec(memory_space=pltpu.VMEM)
+    outs, out_specs = reduce_outs(arrays, kinds)
+    outs += [jax.ShapeDtypeStruct(group.shape[1:], F32)] * len(groups)
+    ins = list(arrays) + list(groups)
+    held = len(ins)
+    any_space = pl.BlockSpec(memory_space=pl.ANY)
+    group_specs = [vmem] * (len(groups) + int(vec is not None))
+    if chain is not None:
+        group_specs = [vmem, any_space, vmem]
+        scratch += [pltpu.VMEM(group.shape[1:], BF16)] + [pltpu.SemaphoreType.DMA((3,))] * 2 + [pltpu.SemaphoreType.DMA]
+        outs.append(jax.ShapeDtypeStruct(group.shape, BF16))
+        outs.append(jax.ShapeDtypeStruct((8, group.shape[2]), F32))
+        ins += chain
     if vec is not None:
         scratch += [pltpu.VMEM((3 + nz, 8, TAIL), F32), pltpu.VMEM((4, 8, TAIL), F32)]
         scratch += [pltpu.SemaphoreType.DMA((2 + nz,))] * 2
-    vmem, any_space = pl.BlockSpec(memory_space=pltpu.VMEM), pl.BlockSpec(memory_space=pl.ANY)
-    outs, out_specs = [], []
-    for array, kind in zip(arrays, kinds):
-        if kind:
-            outs.append(jax.ShapeDtypeStruct((TP,) + array.shape[2:], BF16))
-            out_specs.append(any_space)
-        else:
-            outs.append(jax.ShapeDtypeStruct(array.shape[1:], F32))
-            out_specs.append(vmem)
-    for array in groups:
-        outs.append(jax.ShapeDtypeStruct(array.shape[1:], F32))
-        out_specs.append(vmem)
-    vecs = []
-    if vec is not None:
-        vecs = [vec]
         outs.append(jax.ShapeDtypeStruct(vec.shape, F32))
-        out_specs.append(vmem)
-    ins = list(arrays) + list(groups) + vecs
+        ins.append(vec)
     return pl.pallas_call(
-        partial(reduce_kernel, nf, kinds, tuple(units), len(groups), len(vecs)),
-        in_specs=[vmem] * len(ins),
-        out_specs=out_specs,
+        partial(reduce_kernel, nf, kinds, units, len(groups), chain is not None, int(vec is not None)),
+        in_specs=[any_space] * held + [vmem] * (len(ins) - held),
+        out_specs=out_specs + group_specs,
         out_shape=outs,
         scratch_shapes=scratch,
         compiler_params=pltpu.CompilerParams(
@@ -962,21 +1219,141 @@
     )(*ins)
 
 
-def dp_swap(value, mask):
-    return lax.ppermute(value, "dp", [(i, i ^ mask) for i in range(TP)])
-
-
-def dp_gather(value):
-    far = dp_swap(value, 2)
-    near = dp_swap(value, 1)
-    return jnp.stack([value, near, far, dp_swap(far, 1)])
-
-
-def dp_reduce(parts):
-    got = dp_swap(jnp.stack([parts[1], parts[3]]), 1)
-    mine = parts[0].astype(F32) + got[0].astype(F32)
-    far = (parts[2].astype(F32) + got[1].astype(F32)).astype(BF16)
-    return mine + dp_swap(far, 2).astype(F32)
+def mixer_back_kernel(nf, kinds, units, *refs):
+    arrays, n = len(kinds), len(units)
+    ins, (grad_hbm, out_hbm, pos_ref, conv_ref, prm_ref, gain_ref), (proj_hbm, inv_hbm, new_hbm), refs = take(
+        refs, arrays, 6, 3
+    )
+    outs, (gproj_hbm, gconv_ref, misc_ref), refs = take(refs, arrays, 3)
+    p = Place(nf)
+    own, y_in, z_in, pair_in, sems, refs = take(refs, n, n, n, n, 7)
+    final, to_sems, refs = take(refs, sum(kinds[i] for i, _, _ in units), 3)
+    proj_ref, inv_ref, new_ref, gmix_ref, gproj_ref, grad_ref, out_ref, load_sem, store_sem = refs
+    owners = Owners(p, kinds, units, ins, outs, final, *to_sems)
+    red = Reduce(p, owners.part, owners.done, own, y_in, z_in, pair_in, sems)
+    rows = proj_ref.shape[0]
+
+    def loads(g):
+        at = pl.ds(pl.multiple_of(g * rows, rows), rows)
+        return (
+            pltpu.make_async_copy(proj_hbm.at[at], proj_ref, load_sem.at[0]),
+            pltpu.make_async_copy(inv_hbm.at[pl.ds(pl.multiple_of(g * LH, LH), LH)], inv_ref, load_sem.at[1]),
+            pltpu.make_async_copy(new_hbm.at[at], new_ref, load_sem.at[2]),
+        )
+
+    whole = (
+        pltpu.make_async_copy(grad_hbm, grad_ref, load_sem.at[3]),
+        pltpu.make_async_copy(out_hbm, out_ref, load_sem.at[4]),
+    )
+
+    def store(g):
+        at = pl.ds(pl.multiple_of(g * rows, rows), rows)
+        return pltpu.make_async_copy(gproj_ref, gproj_hbm.at[at], store_sem)
+
+    def tick(t):
+        if t < red.ticks:
+            red.tick(t)
+            if t >= p.nz:
+                owners.send_off(t - p.nz)
+
+    p.greet()
+    for copy in loads(0):
+        copy.start()
+    gconv_ref[...] = jnp.zeros_like(gconv_ref)
+    misc_ref[...] = jnp.zeros_like(misc_ref)
+    tick(0)
+    for copy in whole:
+        copy.start()
+    for copy in whole:
+        copy.wait()
+    every = 2
+
+    def group(g, _):
+        at = pl.ds(pl.multiple_of(g * rows, rows), rows)
+
+        def back(c, _):
+            where = pl.ds(pl.multiple_of(c * 256, 256), 256)
+            gmix_ref[:, where] = mm(grad_ref[at, :], out_ref[where, :], ((1,), (1,)))
+            return 0
+
+        lax.fori_loop(0, LH * DV // 256, back, 0)
+        for copy in loads(g):
+            copy.wait()
+
+        @pl.when(g > 0)
+        def _():
+            store(0).wait()
+
+        for step in range(TP):
+
+            @pl.when(g == step)
+            def _():
+                tick(1 + every * step)
+
+        mixer_back(
+            proj_ref, pos_ref.at[at], conv_ref, prm_ref, gain_ref, inv_ref, new_ref, gmix_ref, gproj_ref, gconv_ref, misc_ref
+        )
+        store(g).start()
+
+        @pl.when(g < TP - 1)
+        def _():
+            for copy in loads(g + 1):
+                copy.start()
+
+        for step in range(TP):
+
+            @pl.when(g == step)
+            def _():
+                tick(2 + every * step)
+
+        return 0
+
+    lax.fori_loop(0, TP, group, 0)
+    for t in range(1 + every * TP, red.ticks):
+        tick(t)
+    store(0).wait()
+    red.finish()
+    owners.finish()
+
+
+def mixer_back_all(nf, collective_id, arrays, units, grad, out, pos, conv, prm, gain, proj, inv, new):
+    nz = nf // 2
+    kinds, units, blocks = make_units(nf, arrays, units)
+    final, to_sems = Owners.scratch(kinds, units, blocks)
+    total, columns = proj.shape
+    rows = total // TP
+    vmem, any_space = pl.BlockSpec(memory_space=pltpu.VMEM), pl.BlockSpec(memory_space=pl.ANY)
+    outs, out_specs = reduce_outs(arrays, kinds)
+    outs += [
+        jax.ShapeDtypeStruct((total, columns), BF16),
+        jax.ShapeDtypeStruct(conv.shape, F32),
+        jax.ShapeDtypeStruct((8, DV), F32),
+    ]
+    return pl.pallas_call(
+        partial(mixer_back_kernel, nf, kinds, units),
+        in_specs=[any_space] * (len(arrays) + 2) + [vmem] * 4 + [any_space] * 3,
+        out_specs=out_specs + [any_space, vmem, vmem],
+        out_shape=outs,
+        scratch_shapes=Reduce.scratch(blocks, nz)
+        + final
+        + to_sems
+        + [
+            pltpu.VMEM((rows, columns), F32),
+            pltpu.VMEM((LH, rows, rows), F32),
+            pltpu.VMEM((rows, LH * DV), F32),
+            pltpu.VMEM((rows, LH * DV), F32),
+            pltpu.VMEM((rows, columns), BF16),
+            pltpu.VMEM(grad.shape, BF16),
+            pltpu.VMEM(out.shape, BF16),
+            pltpu.SemaphoreType.DMA((5,)),
+            pltpu.SemaphoreType.DMA,
+        ],
+        compiler_params=pltpu.CompilerParams(
+            collective_id=collective_id, has_side_effects=True, vmem_limit_bytes=VMEM_LIMIT
+        ),
+        cost_estimate=pl.CostEstimate(flops=60_000_000_000, bytes_accessed=80_000_000, transcendentals=5_000_000),
+        name="mixer_back",
+    )(*arrays, grad, out, pos, conv, prm, gain, proj, inv, new)
 
 
 def local(
@@ -1043,18 +1420,16 @@
     pack_up = by_target(w_gate_up[:, ff * TP :])
     extra = jnp.broadcast_to(position.astype(BF16)[:, None], (rows, TAIL))
     cotangent = live * out_grad.astype(F32)
-    proj_full, gate_full, up_full, out_full, down_full, group, grad_down = gather_all(
+    proj_full, pack_gate, pack_up, out_full, group, grad_down = gather_all(
         nf,
         1,
-        ((pack_one, True), (pack_gate, True), (pack_up, True)),
-        (w_out, w_down),
+        (1, 2) if nf <= 8 else (1, 1),
+        ((pack_one, True), (pack_gate, False), (pack_up, False)),
+        (w_out,),
         (jnp.concatenate([tokens, extra], axis=1), cotangent.astype(BF16)),
     )
     proj_full = proj_full.reshape(width, -1)
-    gate_full = gate_full.reshape(width, ff)
-    up_full = up_full.reshape(width, ff)
     out_full = out_full.reshape(-1, width)
-    down_full = down_full.reshape(ff, width)
     group = group.reshape(TP * rows, width + TAIL)
     grad_down = grad_down.reshape(TP * rows, width)
     group_pos = group[:, width:].astype(F32)
@@ -1087,19 +1462,31 @@
 
     scale_one = lax.rsqrt(jnp.mean(group_tokens * group_tokens, axis=-1, keepdims=True) + EPS)
     normed_one = (group_tokens * scale_one * gain_one).astype(BF16)
-    proj = mm(normed_one, proj_full)
-    mixed, inv, new = mixer_fwd(proj, group_pos, conv_mine, prm, gain_head)
-    mixed_out = mm(mixed, out_full).astype(BF16).reshape(TP, rows, width)
-    residual = tokens.astype(F32) + dp_reduce(mixed_out)
-    scale_two = lax.rsqrt(jnp.mean(residual * residual, axis=-1, keepdims=True) + EPS)
-    normed_two = dp_gather((residual * scale_two * gain_two).astype(BF16)).reshape(TP * rows, width)
+    gain_two_rows = jnp.broadcast_to(gain_two[None], (8, width))
+    proj, mixed, inv, new, residual, normed_two, gate_full, up_full, down_full = forward(
+        nf,
+        normed_one,
+        proj_full,
+        out_full,
+        group_pos,
+        conv_mine,
+        prm,
+        gain_head,
+        gain_two_rows,
+        tokens,
+        (pack_gate, pack_up),
+        w_down,
+    )
+    gate_full = gate_full.reshape(width, ff)
+    up_full = up_full.reshape(width, ff)
+    down_full = down_full.reshape(ff, width)
+    normed_two = normed_two.reshape(TP * rows, width)
     gate = mm(normed_two, gate_full)
     up = mm(normed_two, up_full)
     gate_sig = jax.nn.sigmoid(gate)
     gate_act = gate * gate_sig
     hidden = (gate_act * up).astype(BF16)
     down_out = mm(hidden, down_full).astype(BF16).reshape(TP, rows, width)
-    layer_out = (live * (residual + dp_reduce(down_out))).astype(BF16)
 
     grad_wdown = mm(hidden, grad_down, ((0,), (0,))).astype(BF16).reshape(nf, -1, width)
     grad_hidden = mm(grad_down, down_full, ((1,), (1,)))
@@ -1108,27 +1495,38 @@
     gate_grad, up_grad = (
         mm(normed_two, grad, ((0,), (0,))).astype(BF16).reshape(TP, nf, own, ff) for grad in (grad_gate, grad_up)
     )
-    gate_grad, up_grad, wdown_grad = reduce_all(nf, 2, (gate_grad, up_grad, grad_wdown), (768, 768, 1024))
     grad_two = mm(grad_gate, gate_full, ((1,), (1,))) + mm(grad_up, up_full, ((1,), (1,)))
-    grad_two = dp_reduce(grad_two.astype(BF16).reshape(TP, rows, width))
-    weighted = grad_two * gain_two
-    gain_two_part = jnp.sum(grad_two * residual * scale_two, axis=0)
-    grad_residual = (
-        cotangent
-        + scale_two * weighted
-        - residual * (scale_two**3 * jnp.mean(residual * weighted, axis=-1, keepdims=True))
-    )
-
-    grad_mixed_in = dp_gather(grad_residual.astype(BF16)).reshape(TP * rows, width)
+    gate_grad, up_grad, grad_residual, grad_mixed_in, gain_two_part = reduce_all(
+        nf,
+        2,
+        (gate_grad, up_grad),
+        ((0, 128), (0, 256), (0, 512), (0, 512), (1, 640), (1, 512), (1, 128), (1, 128)),
+        (grad_two.astype(BF16).reshape(TP, rows, width),),
+        chain=[residual, cotangent.astype(BF16), gain_two_rows],
+    )
+    gain_two_part = gain_two_part[0]
+    grad_mixed_in = grad_mixed_in.reshape(TP * rows, width)
+
     wout_grad = mm(mixed, grad_mixed_in, ((0,), (0,))).astype(BF16).reshape(nf, -1, width)
-    grad_mixed = mm(grad_mixed_in, out_full, ((1,), (1,)))
-    grad_proj, grad_taps, misc = mixer_bwd(
-        proj, group_pos, conv_mine, prm, gain_head, inv, new, grad_mixed
+    wdown_grad, wout_grad, grad_proj, grad_taps, misc = mixer_back_all(
+        nf,
+        5,
+        (grad_wdown, wout_grad),
+        ((0, 128), (0, 384), (0, 768), (0, 768), (1, 768), (1, 768), (1, 256), (1, 256)),
+        grad_mixed_in,
+        out_full,
+        group_pos,
+        conv_mine,
+        prm,
+        gain_head,
+        proj,
+        inv,
+        new,
     )
     grad_one_part = mm(grad_proj, proj_full, ((1,), (1,)))
     gain_one_part = jnp.sum(grad_one_part * group_tokens * scale_one, axis=0)
 
-    grad_taps = jnp.sum(grad_taps[:, :CONV], axis=0)
+    grad_taps = grad_taps[:CONV]
     k, v = LH * DK, LH * DV
     taps_all = jnp.zeros((CONV, 2 * key_width + value_width), F32)
     taps_all = lax.dynamic_update_slice(taps_all, grad_taps[:, :k], (0, me * k))
@@ -1140,7 +1538,6 @@
     small = jnp.pad(small, ((0, 0), (columns - TAIL + 2 * LH, TAIL - 2 * LH - small.shape[1])))
     one_grad = (mm(normed_one, grad_proj, ((0,), (0,))) + small).astype(BF16).reshape(TP, nf, own, columns)
 
-    misc = jnp.sum(misc, axis=0)
     heads_zero = jnp.zeros((HEADS,), F32)
     head_vec = jnp.concatenate(
         [
@@ -1150,13 +1547,13 @@
         ]
     )
     head_vec = jnp.pad(head_vec, (0, 8 * TAIL - head_vec.shape[0])).reshape(8, TAIL)
-    one_own, wout_grad, grad_one, head_vec = reduce_all(
+    one_own, grad_one, down_sum, head_vec = reduce_all(
         nf,
         3,
-        (one_grad, wout_grad),
-        (640, 2048),
-        (grad_one_part.astype(BF16).reshape(TP, rows, width),),
-        head_vec,
+        (one_grad,),
+        ((0, 128), (0, 384), (0, 640), (0, 640), (0, 640), (0, 512), (0, 128), (0, 128)),
+        (grad_one_part.astype(BF16).reshape(TP, rows, width), down_out),
+        vec=head_vec,
     )
     head_vec = head_vec.reshape(-1)
     one_own = one_own.astype(F32)
@@ -1185,6 +1582,7 @@
     norm2_gain_grad = own_small[:, 1]
     conv_grad = own_small[:, 2:].reshape(CONV, -1)
 
+    layer_out = (live * (residual + down_sum)).astype(BF16)
     tokens_f = tokens.astype(F32)
     scale_own = scale_one[:rows]
     weighted_one = grad_one * gain_one

time: 1250 us -> 1040 us (0.83)
  waiting for transfers between devices: 84.1 us -> 0 us
  Pallas kernels: 880 us -> 834 us
  matrix products: 169 us -> 140 us
  local copies, waits for them, and re-layouts: 59.8 us -> 34.3 us
    ppermute x12 -> x0, waiting for transfers between devices: 84.1 us -> none  [dp_swap(): return lax.ppermute(value, 'dp', [(i, i ^ mask) for i in range(TP)])]
    pallas_call x5, Pallas kernels: 880 us -> 834 us  [the longest x2 325 us: reduce_all(): pl.pallas_call(partial(reduce_kernel, nf, kinds, units, len(groups), chai...]
    dot_general x15 -> x12, matrix products: 169 us -> 140 us  [mm(): lax.dot_general(left, right, (dims, ((), ())), preferred_element_type=F32)]
    unnamed x121 -> x98, local copies, waits for them, and re-layouts: 30.2 us -> 18.3 us
  transfers between devices with their start and end apart: 12 -> 0, of which waited for: 7 -> 0; matrix products, arithmetic and copies ran while one was open for 4% -> 0% of each run, Pallas kernels for 17% -> 0%
where the time goes in v3:
time: 1040 us
  Pallas kernels  834 us (80%)
  matrix products  140 us (13%)
  local copies, waits for them, and re-layouts  34.3 us (3%)
  other arithmetic  28.9 us (3%)
    pallas_call x2, Pallas kernels, reduce_all(): pl.pallas_call(partial(reduce_kernel, nf, kinds, units, len(groups), chai...  325 us
    pallas_call x1, Pallas kernels, forward(): pl.pallas_call(partial(forward_kernel, nf, split), in_specs=[any_space] *...  206 us
    pallas_call x1, Pallas kernels, gather_all(): pl.pallas_call(partial(gather_kernel, nf, splits, marks, (True,) * len(sh...  172 us
    dot_general x12, matrix products, mm(): lax.dot_general(left, right, (dims, ((), ())), preferred_element_type=F32)  140 us
    pallas_call x1, Pallas kernels, mixer_back_all(): pl.pallas_call(partial(mixer_back_kernel, nf, kinds, units), in_specs=[an...  131 us

profile of v3, /device:TPU:0, one launch (start us, length us, event | category | flops | bytes accessed | tf_op | source)
XLA Modules:
  0.0 1038.8 jit_solution(3110788290394997051)
XLA Ops:
  10.4 172.3 %gather_1.1 = (bf16[4,8,64,3200]{3,2,1,0:T(8,128)(2,1)S(1)}, bf16[4,64,1408]{2,1,0:T(8,128)(2,1)S(1)}, bf16[4,64,1408]{2,1,0:T(8,128)(2,1)S(1)}, bf16[8,128,2048...) custom-call(bf16[4,64,3200]{2,1,0:T(8,128)(2,1)S(1)} %copy-done.4, ...), custom_call_target="tpu_custom_call" | custom-call | bytes 54788096 | tf_op jit(solution)/shard_map/gather_1/pallas_call | solution.py:543
  182.7 2.1 copy-done
  190.5 4.7 copy-done.6
  196.6 2.3 convert_reduce_fusion
  198.9 3.1 fusion.3
  202.6 2.8 fusion.5.refs_0_
  209.1 206.1 %forward.1 = (f32[1024,3200]{1,0:T(8,128)}, bf16[1024,1024]{1,0:T(8,128)(2,1)}, f32[16,256,256]{2,1,0:T(8,128)}, f32[1024,1024]{1,0:T(8,128)}, f32[256,2048]{1,0...) custom-call(bf16[1024,2048]{1,0:T(8,128)(2,1)} %fusion.5.refs_0_, ...), custom_call_target="tpu_custom_call" | custom-call | flops 44999999488 | bytes 80000000 | tf_op jit(solution)/shard_map/forward/pallas_call | solution.py:745
  415.2 11.8 %fusion.33 = f32[1024,1408]{1,0:T(8,128)} fusion(bf16[1024,2048]{1,0:T(8,128)(2,1)} %bitcast.206, bf16[2048,1408]{1,0:T(8,128)(2,1)} %bitcast.201), kind=kOutput, calls=%fused_computation.109 | convolution fusion | flops 5905580032 | bytes 15728640 | tf_op jit(solution)/shard_map/dot_general | solution.py:25
  427.0 8.4 fusion.32
  435.4 13.6 %multiply_convert_fusion = (bf16[1024,1408]{1,0:T(8,128)(2,1)}, bf16[1024,1408]{1,0:T(8,128)(2,1)}, bf16[1024,1408]{1,0:T(8,128)(2,1)}) fusion(f32[1024,1408]{1,0:T(8,128)} %fusion.32, f32[1024,1408]{1,0:T(8,128)} %fusion.33, bf16[1024,2048]{1,0:T(8,128)(2,1)S(1)} %bitcast.155, bf16[1408,2048]{1,0:T(8,128)(2,1)S(1)} %bitcast.200), kind=kOutput, calls=%fused_computation.19 | convolution fusion | flops 5927206912 | bytes 30146560 | tf_op jit(solution)/shard_map/dot_general | solution.py:25
  449.0 9.7 fusion.34
  458.8 11.1 %add_convert_fusion = bf16[1024,2048]{1,0:T(8,128)(2,1)} fusion(f32[1024,2048]{1,0:T(8,128)S(1)} %fusion.34, bf16[1024,1408]{1,0:T(8,128)(2,1)S(1)} %copy-done.42, bf16[2048,1408]{1,0:T(8,128)(2,1)} %bitcast.202), kind=kOutput, calls=%fused_computation.15 | convolution fusion | flops 5909774336 | bytes 21233664 | tf_op jit(solution)/shard_map/dot_general | solution.py:25
  469.9 8.8 convolution_convert_fusion
  478.7 8.6 convolution_convert_fusion.1
  487.4 144.6 %reduce_2.1 = (bf16[4,64,1408]{2,1,0:T(8,128)(2,1)}, bf16[4,64,1408]{2,1,0:T(8,128)(2,1)}, f32[256,2048]{1,0:T(8,128)}, bf16[4,256,2048]{2,1,0:T(8,128)(2,1)}, f32[8,2048]{1,0:T(8,128)}) custom-call(bf16[4,8,64,1408]{3,2,1,0:T(8,128)(2,1)} %bitcast.159, bf16[4,8,64,1408]{3,2,1,0:T(8,128)(2,1)} %bitcast.158, bf16[4,256,2048]{2,1,0:T(8,128)(2,1)} %bitcast.164, ...), custom_call_target="tpu_custom_call" | custom-call | bytes 37879808 | tf_op jit(solution)/shard_map/reduce_2/pallas_call | solution.py:1206
  636.9 6.3 convolution_convert_fusion.4
  643.2 8.1 convolution_convert_fusion.2
  651.3 131.4 %mixer_back.1 = (f32[176,2048]{1,0:T(8,128)}, f32[128,2048]{1,0:T(8,128)}, bf16[1024,3200]{1,0:T(8,128)(2,1)}, f32[8,2048]{1,0:T(8,128)}, f32[8,256]{1,0:T(8,128)}) custom-call(bf16[8,176,2048]{2,1,0:T(8,128)(2,1)} %bitcast.205, bf16[8,128,2048]{2,1,0:T(8,128)(2,1)} %bitcast.210, bf16[1024,2048]{1,0:T(8,128)(2,1)} %bitcast.195, ...), custom_call_target="tpu_custom_call" | custom-call | flops 60000002048 | bytes 80000000 | tf_op jit(solution)/shard_map/mixer_back/pallas_call | solution.py:1332
  785.6 10.8 %convolution_convert_fusion.3 = bf16[1024,2048]{1,0:T(8,128)(2,1)} fusion(bf16[1024,1408]{1,0:T(8,128)(2,1)S(1)} %copy-done.40, bf16[1408,2048]{1,0:T(8,128)(2,1)} %bitcast.197), kind=kOutput, calls=%fused_computation.24 | convolution fusion | flops 5907677184 | bytes 12845056 | tf_op jit(solution)/shard_map/dot_general | solution.py:25
  796.4 21.3 %fusion.26 = (bf16[1024,2048]{1,0:T(8,128)(2,1)}, f32[2048]{0:T(1024)S(1)}) fusion(f32[1024]{0:T(1024)S(1)} %copy-done.21, bf16[1024,2176]{1,0:T(8,128)(2,1)} %bitcast.147, bf16[1024,3200]{1,0:T(8,128)(2,1)} %get-tuple-element.58, bf16[2048,3200]{1,0:T(8,128)(2,1)} %bitcast.152), kind=kOutput, calls=%fused_computation.102 | convolution fusion | flops 13432256512 | bytes 28061696 | tf_op jit(solution)/shard_map/dot_general | solution.py:25
  819.7 21.1 %fusion.1 = bf16[2048,3200]{1,0:T(8,128)(2,1)} fusion(f32[2048,16]{1,0:T(8,128)S(1)} %reshape.263, f32[2048,1]{1,0:T(8,128)S(1)} %copy.124, f32[2048,1]{1,0:T(8,128)S(1)} %copy.123, bf16[1024,2048]{1,0:T(8,128)(2,1)} %fusion.5.refs_0_, bf16[1024,3200]{1,0:T(8,128)(2,1)} %get-tuple-element.58), kind=kOutput, calls=%fused_computation.4 | convolution fusion | flops 13487308800 | bytes 24002560 | tf_op jit(solution)/shard_map/dot_general | solution.py:25
  840.9 179.9 %reduce_3.1 = (bf16[4,64,3200]{2,1,0:T(8,128)(2,1)}, f32[256,2048]{1,0:T(8,128)}, f32[256,2048]{1,0:T(8,128)}, f32[8,128]{1,0:T(8,128)}) custom-call(bf16[4,8,64,3200]{3,2,1,0:T(8,128)(2,1)} %bitcast.157, bf16[4,256,2048]{2,1,0:T(8,128)(2,1)} %bitcast.163, bf16[4,256,2048]{2,1,0:T(8,128)(2,1)} %bitcast.162, f32[8,128]{1,0:T(8,128)} %fusion.23.refs_3_), custom_call_target="tpu_custom_call" | custom-call | bytes 42999808 | tf_op jit(solution)/shard_map/reduce_3/pallas_call | solution.py:1206
  1027.5 2.4 fusion.9
  1030.0 4.0 fusion.12
  (170 shorter events, 41.9 us)
Async XLA Ops:
  3.5 3.7 copy-start.35
  4.3 4.6 copy-start.5
  7.2 188.3 %copy-start.2 = (bf16[256,2048]{1,0:T(8,128)(2,1)}, bf16[256,2048]{1,0:T(8,128)(2,1)S(1)}, u32[]{:S(2)}) copy-start(bf16[256,2048]{1,0:T(8,128)(2,1)S(1)} %multiply_convert_fusion.4.refs_5_.refs_4_) | copy-start | bytes 3145732
  190.5 4.7 copy-start.6
  195.9 6.7 copy-start.1
  202.6 5.9 copy-start.27
  415.2 11.8 %copy-start.36 = (bf16[4,8,64,1408]{3,2,1,0:T(8,128)(2,1)S(1)}, bf16[4,8,64,1408]{3,2,1,0:T(8,128)(2,1)}, u32[]{:S(2)}) copy-start(bf16[4,8,64,1408]{3,2,1,0:T(8,128)(2,1)} %get-tuple-element.49) | copy-start | bytes 17301508
  415.2 11.8 %copy-start.37 = (bf16[4,256,2048]{2,1,0:T(8,128)(2,1)S(1)}, bf16[4,256,2048]{2,1,0:T(8,128)(2,1)}, u32[]{:S(2)}) copy-start(bf16[4,256,2048]{2,1,0:T(8,128)(2,1)} %get-tuple-element.48) | copy-start | bytes 12582916
  415.2 20.2 %slice-start = ((s8[5767168]{0:T(1024)(128)(4,1)}), s8[4194304]{0:T(1024)(128)(4,1)S(1)}, s32[]{:S(2)}) async-start(s8[5767168]{0:T(1024)(128)(4,1)} %bitcast.198), calls=%async_computation | async-start | bytes 8388608
  427.0 8.4 copy-start.9
  427.0 8.4 slice-start.1
  449.0 9.8 copy-start.42
  458.8 11.1 %copy-start.38 = (bf16[4,256,2048]{2,1,0:T(8,128)(2,1)S(1)}, bf16[4,256,2048]{2,1,0:T(8,128)(2,1)}, u32[]{:S(2)}) copy-start(bf16[4,256,2048]{2,1,0:T(8,128)(2,1)} %get-tuple-element.48) | copy-start | bytes 12582916
  469.9 8.8 copy-start.41
  632.0 4.9 copy-start.34
  632.0 4.9 copy-start.39
  636.9 6.3 copy-start.10
  636.9 6.3 copy-start.40
  785.6 10.8 %copy-start.21 = (f32[1024]{0:T(1024)S(1)}, f32[1024]{0:T(1024)}, u32[]{:S(2)}) copy-start(f32[1024]{0:T(1024)} %copy-done.20) | copy-start | bytes 12292
  796.3 21.7 %copy-start.22 = (f32[8,2048]{1,0:T(8,128)S(1)}, f32[8,2048]{1,0:T(8,128)}, u32[]{:S(2)}) copy-start(f32[8,2048]{1,0:T(8,128)} %get-tuple-element.60) | copy-start | bytes 196612
  1024.0 3.5 copy-start.19
  1027.5 6.5 copy-start.13
  1027.5 6.5 copy-start.14
  1027.5 6.5 copy-start.24
  (21 other events, 46.3 us)

commit v4 on v3

--- a/solution.py
+++ b/solution.py
@@ -711,7 +711,7 @@
     own_normed.start()
     for t in range(1 + PER * TP, gather.ticks):
         gather.tick(t)
-        if t == min(2 + PER * TP, gather.ticks - 1):
+        if t == min(3 + PER * TP, gather.ticks - 1):
             group_copy(0).wait_recv()
             group_copy(2).start()
     gather.finish()
@@ -1098,6 +1098,8 @@
         group_copy(j, 1).start()
         keep(j, 0).start()
         keep(j, 1).start()
+    vec_ticks = (0, 3, 6, 9) if red.ticks >= 12 else (0, 1, 2, 3)
+    late = min(7, red.ticks - 1)
     for t in range(red.ticks):
         red.tick(t)
         if t >= nz:
@@ -1110,7 +1112,7 @@
                 keep(j, 1).wait()
                 add_into(near.at[j, 1], [kept.at[j, 1], near.at[j, 1]])
                 group_copy(j, 2).start()
-        if t == 1:
+        if t == min(3, red.ticks - 2):
             if chain:
                 group_copy(0, 2).wait_recv()
                 rows, width = residual_ref.shape
@@ -1119,15 +1121,20 @@
                 spread(0).start()
                 spread(1).start()
                 own_spread.start()
-        if chain and t == 3:
+        if chain and t == min(7, red.ticks - 1):
             spread(0).wait_recv()
             spread(2).start()
-        if vecs and t < 4:
-            vec_step(t)
+        if vecs and t in vec_ticks:
+            vec_step(vec_ticks.index(t))
+        if vecs and t == vec_ticks[3]:
+            vec_in[3 + p.z] = vec_own[3]
+            for k in range(1, nz):
+                vec_z(k).start()
+        if t == late and not chain:
+            for j in range(groups):
+                group_copy(j, 2).wait_recv()
+                add_into(group_outs[j], [kept.at[j, 0], near.at[j, 0], near.at[j, 2]])
     for j in range(groups):
-        if not chain:
-            group_copy(j, 2).wait_recv()
-            add_into(group_outs[j], [kept.at[j, 0], near.at[j, 0], near.at[j, 2]])
         for k in range(3):
             group_copy(j, k).wait_send()
     if chain:
@@ -1137,9 +1144,6 @@
         for k in range(3):
             spread(k).wait_send()
     if vecs:
-        vec_in[3 + p.z] = vec_own[3]
-        for k in range(1, nz):
-            vec_z(k).start()
         for k in range(1, nz):
             source = lax.rem(p.z - k + nz, nz)
             ref = vec_in.at[3 + source]

time: 1040 us -> 1010 us (0.971)
  Pallas kernels: 834 us -> 801 us
    pallas_call x2, Pallas kernels: 325 us -> 292 us  [reduce_all(): pl.pallas_call(partial(reduce_kernel, nf, kinds, units, len(groups), chai...]
where the time goes in v4:
time: 1010 us
  Pallas kernels  801 us (79%)
  matrix products  140 us (14%)
  local copies, waits for them, and re-layouts  34.3 us (3%)
  other arithmetic  28.9 us (3%)
    pallas_call x2, Pallas kernels, reduce_all(): pl.pallas_call(partial(reduce_kernel, nf, kinds, units, len(groups), chai...  292 us
    pallas_call x1, Pallas kernels, forward(): pl.pallas_call(partial(forward_kernel, nf, split), in_specs=[any_space] *...  206 us
    pallas_call x1, Pallas kernels, gather_all(): pl.pallas_call(partial(gather_kernel, nf, splits, marks, (True,) * len(sh...  172 us
    dot_general x12, matrix products, mm(): lax.dot_general(left, right, (dims, ((), ())), preferred_element_type=F32)  140 us
    pallas_call x1, Pallas kernels, mixer_back_all(): pl.pallas_call(partial(mixer_back_kernel, nf, kinds, units), in_specs=[an...  131 us

profile of v4, /device:TPU:0, one launch (start us, length us, event | category | flops | bytes accessed | tf_op | source)
XLA Modules:
  0.0 1005.4 jit_solution(1310309678430759431)
XLA Ops:
  10.4 172.3 %gather_1.1 = (bf16[4,8,64,3200]{3,2,1,0:T(8,128)(2,1)S(1)}, bf16[4,64,1408]{2,1,0:T(8,128)(2,1)S(1)}, bf16[4,64,1408]{2,1,0:T(8,128)(2,1)S(1)}, bf16[8,128,2048...) custom-call(bf16[4,64,3200]{2,1,0:T(8,128)(2,1)S(1)} %copy-done.4, ...), custom_call_target="tpu_custom_call" | custom-call | bytes 54788096 | tf_op jit(solution)/shard_map/gather_1/pallas_call | solution.py:543
  182.7 2.1 copy-done
  190.5 4.7 copy-done.6
  196.6 2.3 convert_reduce_fusion
  198.9 3.1 fusion.3
  202.6 2.8 fusion.5.refs_0_
  209.1 206.1 %forward.1 = (f32[1024,3200]{1,0:T(8,128)}, bf16[1024,1024]{1,0:T(8,128)(2,1)}, f32[16,256,256]{2,1,0:T(8,128)}, f32[1024,1024]{1,0:T(8,128)}, f32[256,2048]{1,0...) custom-call(bf16[1024,2048]{1,0:T(8,128)(2,1)} %fusion.5.refs_0_, ...), custom_call_target="tpu_custom_call" | custom-call | flops 44999999488 | bytes 80000000 | tf_op jit(solution)/shard_map/forward/pallas_call | solution.py:745
  415.2 11.8 %fusion.33 = f32[1024,1408]{1,0:T(8,128)} fusion(bf16[1024,2048]{1,0:T(8,128)(2,1)} %bitcast.206, bf16[2048,1408]{1,0:T(8,128)(2,1)} %bitcast.201), kind=kOutput, calls=%fused_computation.109 | convolution fusion | flops 5905580032 | bytes 15728640 | tf_op jit(solution)/shard_map/dot_general | solution.py:25
  427.0 8.4 fusion.32
  435.4 13.6 %multiply_convert_fusion = (bf16[1024,1408]{1,0:T(8,128)(2,1)}, bf16[1024,1408]{1,0:T(8,128)(2,1)}, bf16[1024,1408]{1,0:T(8,128)(2,1)}) fusion(f32[1024,1408]{1,0:T(8,128)} %fusion.32, f32[1024,1408]{1,0:T(8,128)} %fusion.33, bf16[1024,2048]{1,0:T(8,128)(2,1)S(1)} %bitcast.155, bf16[1408,2048]{1,0:T(8,128)(2,1)S(1)} %bitcast.200), kind=kOutput, calls=%fused_computation.19 | convolution fusion | flops 5927206912 | bytes 30146560 | tf_op jit(solution)/shard_map/dot_general | solution.py:25
  449.0 9.7 fusion.34
  458.8 11.1 %add_convert_fusion = bf16[1024,2048]{1,0:T(8,128)(2,1)} fusion(f32[1024,2048]{1,0:T(8,128)S(1)} %fusion.34, bf16[1024,1408]{1,0:T(8,128)(2,1)S(1)} %copy-done.42, bf16[2048,1408]{1,0:T(8,128)(2,1)} %bitcast.202), kind=kOutput, calls=%fused_computation.15 | convolution fusion | flops 5909774336 | bytes 21233664 | tf_op jit(solution)/shard_map/dot_general | solution.py:25
  469.9 8.8 convolution_convert_fusion
  478.7 8.6 convolution_convert_fusion.1
  487.4 140.2 %reduce_2.1 = (bf16[4,64,1408]{2,1,0:T(8,128)(2,1)}, bf16[4,64,1408]{2,1,0:T(8,128)(2,1)}, f32[256,2048]{1,0:T(8,128)}, bf16[4,256,2048]{2,1,0:T(8,128)(2,1)}, f32[8,2048]{1,0:T(8,128)}) custom-call(bf16[4,8,64,1408]{3,2,1,0:T(8,128)(2,1)} %bitcast.159, bf16[4,8,64,1408]{3,2,1,0:T(8,128)(2,1)} %bitcast.158, bf16[4,256,2048]{2,1,0:T(8,128)(2,1)} %bitcast.164, ...), custom_call_target="tpu_custom_call" | custom-call | bytes 37879808 | tf_op jit(solution)/shard_map/reduce_2/pallas_call | solution.py:1210
  632.5 6.3 convolution_convert_fusion.4
  638.8 8.1 convolution_convert_fusion.2
  646.8 130.9 %mixer_back.1 = (f32[176,2048]{1,0:T(8,128)}, f32[128,2048]{1,0:T(8,128)}, bf16[1024,3200]{1,0:T(8,128)(2,1)}, f32[8,2048]{1,0:T(8,128)}, f32[8,256]{1,0:T(8,128)}) custom-call(bf16[8,176,2048]{2,1,0:T(8,128)(2,1)} %bitcast.205, bf16[8,128,2048]{2,1,0:T(8,128)(2,1)} %bitcast.210, bf16[1024,2048]{1,0:T(8,128)(2,1)} %bitcast.195, ...), custom_call_target="tpu_custom_call" | custom-call | flops 60000002048 | bytes 80000000 | tf_op jit(solution)/shard_map/mixer_back/pallas_call | solution.py:1336
  780.6 10.8 %convolution_convert_fusion.3 = bf16[1024,2048]{1,0:T(8,128)(2,1)} fusion(bf16[1024,1408]{1,0:T(8,128)(2,1)S(1)} %copy-done.40, bf16[1408,2048]{1,0:T(8,128)(2,1)} %bitcast.197), kind=kOutput, calls=%fused_computation.24 | convolution fusion | flops 5907677184 | bytes 12845056 | tf_op jit(solution)/shard_map/dot_general | solution.py:25
  791.4 21.3 %fusion.26 = (bf16[1024,2048]{1,0:T(8,128)(2,1)}, f32[2048]{0:T(1024)S(1)}) fusion(f32[1024]{0:T(1024)S(1)} %copy-done.21, bf16[1024,2176]{1,0:T(8,128)(2,1)} %bitcast.147, bf16[1024,3200]{1,0:T(8,128)(2,1)} %get-tuple-element.58, bf16[2048,3200]{1,0:T(8,128)(2,1)} %bitcast.152), kind=kOutput, calls=%fused_computation.102 | convolution fusion | flops 13432256512 | bytes 28061696 | tf_op jit(solution)/shard_map/dot_general | solution.py:25
  814.8 21.1 %fusion.1 = bf16[2048,3200]{1,0:T(8,128)(2,1)} fusion(f32[2048,16]{1,0:T(8,128)S(1)} %reshape.263, f32[2048,1]{1,0:T(8,128)S(1)} %copy.124, f32[2048,1]{1,0:T(8,128)S(1)} %copy.123, bf16[1024,2048]{1,0:T(8,128)(2,1)} %fusion.5.refs_0_, bf16[1024,3200]{1,0:T(8,128)(2,1)} %get-tuple-element.58), kind=kOutput, calls=%fused_computation.4 | convolution fusion | flops 13487308800 | bytes 24002560 | tf_op jit(solution)/shard_map/dot_general | solution.py:25
  835.9 151.5 %reduce_3.1 = (bf16[4,64,3200]{2,1,0:T(8,128)(2,1)}, f32[256,2048]{1,0:T(8,128)}, f32[256,2048]{1,0:T(8,128)}, f32[8,128]{1,0:T(8,128)}) custom-call(bf16[4,8,64,3200]{3,2,1,0:T(8,128)(2,1)} %bitcast.157, bf16[4,256,2048]{2,1,0:T(8,128)(2,1)} %bitcast.163, bf16[4,256,2048]{2,1,0:T(8,128)(2,1)} %bitcast.162, f32[8,128]{1,0:T(8,128)} %fusion.23.refs_3_), custom_call_target="tpu_custom_call" | custom-call | bytes 42999808 | tf_op jit(solution)/shard_map/reduce_3/pallas_call | solution.py:1210
  994.2 2.4 fusion.9
  996.6 4.0 fusion.12
  (170 shorter events, 41.9 us)
Async XLA Ops:
  3.5 3.7 copy-start.35
  4.3 4.6 copy-start.5
  7.2 188.3 %copy-start.2 = (bf16[256,2048]{1,0:T(8,128)(2,1)}, bf16[256,2048]{1,0:T(8,128)(2,1)S(1)}, u32[]{:S(2)}) copy-start(bf16[256,2048]{1,0:T(8,128)(2,1)S(1)} %multiply_convert_fusion.4.refs_5_.refs_4_) | copy-start | bytes 3145732
  190.5 4.7 copy-start.6
  195.9 6.7 copy-start.1
  202.6 5.9 copy-start.27
  415.2 11.8 %copy-start.36 = (bf16[4,8,64,1408]{3,2,1,0:T(8,128)(2,1)S(1)}, bf16[4,8,64,1408]{3,2,1,0:T(8,128)(2,1)}, u32[]{:S(2)}) copy-start(bf16[4,8,64,1408]{3,2,1,0:T(8,128)(2,1)} %get-tuple-element.49) | copy-start | bytes 17301508
  415.2 11.8 %copy-start.37 = (bf16[4,256,2048]{2,1,0:T(8,128)(2,1)S(1)}, bf16[4,256,2048]{2,1,0:T(8,128)(2,1)}, u32[]{:S(2)}) copy-start(bf16[4,256,2048]{2,1,0:T(8,128)(2,1)} %get-tuple-element.48) | copy-start | bytes 12582916
  415.2 20.2 %slice-start = ((s8[5767168]{0:T(1024)(128)(4,1)}), s8[4194304]{0:T(1024)(128)(4,1)S(1)}, s32[]{:S(2)}) async-start(s8[5767168]{0:T(1024)(128)(4,1)} %bitcast.198), calls=%async_computation | async-start | bytes 8388608
  427.0 8.4 copy-start.9
  427.0 8.4 slice-start.1
  449.0 9.8 copy-start.42
  458.8 11.1 %copy-start.38 = (bf16[4,256,2048]{2,1,0:T(8,128)(2,1)S(1)}, bf16[4,256,2048]{2,1,0:T(8,128)(2,1)}, u32[]{:S(2)}) copy-start(bf16[4,256,2048]{2,1,0:T(8,128)(2,1)} %get-tuple-element.48) | copy-start | bytes 12582916
  469.9 8.8 copy-start.41
  627.6 4.9 copy-start.34
  627.6 4.9 copy-start.39
  632.5 6.3 copy-start.10
  632.5 6.3 copy-start.40
  780.6 10.8 %copy-start.21 = (f32[1024]{0:T(1024)S(1)}, f32[1024]{0:T(1024)}, u32[]{:S(2)}) copy-start(f32[1024]{0:T(1024)} %copy-done.20) | copy-start | bytes 12292
  791.4 21.7 %copy-start.22 = (f32[8,2048]{1,0:T(8,128)S(1)}, f32[8,2048]{1,0:T(8,128)}, u32[]{:S(2)}) copy-start(f32[8,2048]{1,0:T(8,128)} %get-tuple-element.60) | copy-start | bytes 196612
  990.6 3.5 copy-start.19
  994.2 6.5 copy-start.13
  994.2 6.5 copy-start.14
  994.2 6.5 copy-start.24
  (21 other events, 46.3 us)

commit v5 on v4

--- a/solution.py
+++ b/solution.py
@@ -1098,7 +1098,7 @@
         group_copy(j, 1).start()
         keep(j, 0).start()
         keep(j, 1).start()
-    vec_ticks = (0, 3, 6, 9) if red.ticks >= 12 else (0, 1, 2, 3)
+    vec_ticks = (0, 3, 6, 8) if red.ticks >= 11 else (0, 1, 2, 3)
     late = min(7, red.ticks - 1)
     for t in range(red.ticks):
         red.tick(t)
@@ -1504,7 +1504,7 @@
         nf,
         2,
         (gate_grad, up_grad),
-        ((0, 128), (0, 256), (0, 512), (0, 512), (1, 640), (1, 512), (1, 128), (1, 128)),
+        ((0, 128), (0, 512), (0, 768), (1, 768), (1, 512), (1, 128)),
         (grad_two.astype(BF16).reshape(TP, rows, width),),
         chain=[residual, cotangent.astype(BF16), gain_two_rows],
     )
@@ -1516,7 +1516,7 @@
         nf,
         5,
         (grad_wdown, wout_grad),
-        ((0, 128), (0, 384), (0, 768), (0, 768), (1, 768), (1, 768), (1, 256), (1, 256)),
+        ((0, 128), (0, 640), (0, 1280), (1, 1024), (1, 768), (1, 256)),
         grad_mixed_in,
         out_full,
         group_pos,
@@ -1555,7 +1555,7 @@
         nf,
         3,
         (one_grad,),
-        ((0, 128), (0, 384), (0, 640), (0, 640), (0, 640), (0, 512), (0, 128), (0, 128)),
+        ((0, 128), (0, 512), (0, 768), (0, 768), (0, 640), (0, 256), (0, 128)),
         (grad_one_part.astype(BF16).reshape(TP, rows, width), down_out),
         vec=head_vec,
     )

time: 1010 us -> 1030 us (1.020)
  Pallas kernels: 801 us -> 818 us
    pallas_call x1, Pallas kernels: 131 us -> 143 us  [mixer_back_all(): pl.pallas_call(partial(mixer_back_kernel, nf, kinds, units), in_specs=[an...]
where the time goes in v5:
time: 1030 us; the launch traced here: 1020 us
  Pallas kernels  818 us (79%)
  matrix products  139 us (13%)
  local copies, waits for them, and re-layouts  34.3 us (3%)
  other arithmetic  28.9 us (3%)
    pallas_call x2, Pallas kernels, reduce_all(): pl.pallas_call(partial(reduce_kernel, nf, kinds, units, len(groups), chai...  297 us
    pallas_call x1, Pallas kernels, forward(): pl.pallas_call(partial(forward_kernel, nf, split), in_specs=[any_space] *...  206 us
    pallas_call x1, Pallas kernels, gather_all(): pl.pallas_call(partial(gather_kernel, nf, splits, marks, (True,) * len(sh...  172 us
    pallas_call x1, Pallas kernels, mixer_back_all(): pl.pallas_call(partial(mixer_back_kernel, nf, kinds, units), in_specs=[an...  143 us
    dot_general x12, matrix products, mm(): lax.dot_general(left, right, (dims, ((), ())), preferred_element_type=F32)  139 us

profile of v5, /device:TPU:0, one launch (start us, length us, event | category | flops | bytes accessed | tf_op | source)
XLA Modules:
  0.0 1022.5 jit_solution(2365465274594773465)
XLA Ops:
  10.4 172.3 %gather_1.1 = (bf16[4,8,64,3200]{3,2,1,0:T(8,128)(2,1)S(1)}, bf16[4,64,1408]{2,1,0:T(8,128)(2,1)S(1)}, bf16[4,64,1408]{2,1,0:T(8,128)(2,1)S(1)}, bf16[8,128,2048...) custom-call(bf16[4,64,3200]{2,1,0:T(8,128)(2,1)S(1)} %copy-done.4, ...), custom_call_target="tpu_custom_call" | custom-call | bytes 54788096 | tf_op jit(solution)/shard_map/gather_1/pallas_call | solution.py:543
  182.7 2.1 copy-done
  190.5 4.7 copy-done.6
  196.6 2.3 convert_reduce_fusion
  198.9 3.1 fusion.3
  202.6 2.8 fusion.5.refs_0_
  209.1 206.1 %forward.1 = (f32[1024,3200]{1,0:T(8,128)}, bf16[1024,1024]{1,0:T(8,128)(2,1)}, f32[16,256,256]{2,1,0:T(8,128)}, f32[1024,1024]{1,0:T(8,128)}, f32[256,2048]{1,0...) custom-call(bf16[1024,2048]{1,0:T(8,128)(2,1)} %fusion.5.refs_0_, ...), custom_call_target="tpu_custom_call" | custom-call | flops 44999999488 | bytes 80000000 | tf_op jit(solution)/shard_map/forward/pallas_call | solution.py:745
  415.2 11.8 %fusion.33 = f32[1024,1408]{1,0:T(8,128)} fusion(bf16[1024,2048]{1,0:T(8,128)(2,1)} %bitcast.206, bf16[2048,1408]{1,0:T(8,128)(2,1)} %bitcast.201), kind=kOutput, calls=%fused_computation.109 | convolution fusion | flops 5905580032 | bytes 15728640 | tf_op jit(solution)/shard_map/dot_general | solution.py:25
  427.0 8.4 fusion.32
  435.4 13.6 %multiply_convert_fusion = (bf16[1024,1408]{1,0:T(8,128)(2,1)}, bf16[1024,1408]{1,0:T(8,128)(2,1)}, bf16[1024,1408]{1,0:T(8,128)(2,1)}) fusion(f32[1024,1408]{1,0:T(8,128)} %fusion.32, f32[1024,1408]{1,0:T(8,128)} %fusion.33, bf16[1024,2048]{1,0:T(8,128)(2,1)S(1)} %bitcast.155, bf16[1408,2048]{1,0:T(8,128)(2,1)S(1)} %bitcast.200), kind=kOutput, calls=%fused_computation.19 | convolution fusion | flops 5927206912 | bytes 30146560 | tf_op jit(solution)/shard_map/dot_general | solution.py:25
  449.0 9.7 fusion.34
  458.8 11.1 %add_convert_fusion = bf16[1024,2048]{1,0:T(8,128)(2,1)} fusion(f32[1024,2048]{1,0:T(8,128)S(1)} %fusion.34, bf16[1024,1408]{1,0:T(8,128)(2,1)S(1)} %copy-done.42, bf16[2048,1408]{1,0:T(8,128)(2,1)} %bitcast.202), kind=kOutput, calls=%fused_computation.15 | convolution fusion | flops 5909774336 | bytes 21233664 | tf_op jit(solution)/shard_map/dot_general | solution.py:25
  469.9 8.8 convolution_convert_fusion
  478.7 8.6 convolution_convert_fusion.1
  487.4 141.8 %reduce_2.1 = (bf16[4,64,1408]{2,1,0:T(8,128)(2,1)}, bf16[4,64,1408]{2,1,0:T(8,128)(2,1)}, f32[256,2048]{1,0:T(8,128)}, bf16[4,256,2048]{2,1,0:T(8,128)(2,1)}, f32[8,2048]{1,0:T(8,128)}) custom-call(bf16[4,8,64,1408]{3,2,1,0:T(8,128)(2,1)} %bitcast.159, bf16[4,8,64,1408]{3,2,1,0:T(8,128)(2,1)} %bitcast.158, bf16[4,256,2048]{2,1,0:T(8,128)(2,1)} %bitcast.164, ...), custom_call_target="tpu_custom_call" | custom-call | bytes 37879808 | tf_op jit(solution)/shard_map/reduce_2/pallas_call | solution.py:1210
  634.1 6.3 convolution_convert_fusion.4
  640.4 8.1 convolution_convert_fusion.2
  648.4 143.1 %mixer_back.1 = (f32[176,2048]{1,0:T(8,128)}, f32[128,2048]{1,0:T(8,128)}, bf16[1024,3200]{1,0:T(8,128)(2,1)}, f32[8,2048]{1,0:T(8,128)}, f32[8,256]{1,0:T(8,128)}) custom-call(bf16[8,176,2048]{2,1,0:T(8,128)(2,1)} %bitcast.205, bf16[8,128,2048]{2,1,0:T(8,128)(2,1)} %bitcast.210, bf16[1024,2048]{1,0:T(8,128)(2,1)} %bitcast.195, ...), custom_call_target="tpu_custom_call" | custom-call | flops 60000002048 | bytes 80000000 | tf_op jit(solution)/shard_map/mixer_back/pallas_call | solution.py:1336
  794.4 10.8 %convolution_convert_fusion.3 = bf16[1024,2048]{1,0:T(8,128)(2,1)} fusion(bf16[1024,1408]{1,0:T(8,128)(2,1)S(1)} %copy-done.40, bf16[1408,2048]{1,0:T(8,128)(2,1)} %bitcast.197), kind=kOutput, calls=%fused_computation.24 | convolution fusion | flops 5907677184 | bytes 12845056 | tf_op jit(solution)/shard_map/dot_general | solution.py:25
  805.2 21.3 %fusion.26 = (bf16[1024,2048]{1,0:T(8,128)(2,1)}, f32[2048]{0:T(1024)S(1)}) fusion(f32[1024]{0:T(1024)S(1)} %copy-done.21, bf16[1024,2176]{1,0:T(8,128)(2,1)} %bitcast.147, bf16[1024,3200]{1,0:T(8,128)(2,1)} %get-tuple-element.58, bf16[2048,3200]{1,0:T(8,128)(2,1)} %bitcast.152), kind=kOutput, calls=%fused_computation.102 | convolution fusion | flops 13432256512 | bytes 28061696 | tf_op jit(solution)/shard_map/dot_general | solution.py:25
  828.6 20.9 %fusion.1 = bf16[2048,3200]{1,0:T(8,128)(2,1)} fusion(f32[2048,16]{1,0:T(8,128)S(1)} %reshape.263, f32[2048,1]{1,0:T(8,128)S(1)} %copy.124, f32[2048,1]{1,0:T(8,128)S(1)} %copy.123, bf16[1024,2048]{1,0:T(8,128)(2,1)} %fusion.5.refs_0_, bf16[1024,3200]{1,0:T(8,128)(2,1)} %get-tuple-element.58), kind=kOutput, calls=%fused_computation.4 | convolution fusion | flops 13487308800 | bytes 24002560 | tf_op jit(solution)/shard_map/dot_general | solution.py:25
  849.5 155.0 %reduce_3.1 = (bf16[4,64,3200]{2,1,0:T(8,128)(2,1)}, f32[256,2048]{1,0:T(8,128)}, f32[256,2048]{1,0:T(8,128)}, f32[8,128]{1,0:T(8,128)}) custom-call(bf16[4,8,64,3200]{3,2,1,0:T(8,128)(2,1)} %bitcast.157, bf16[4,256,2048]{2,1,0:T(8,128)(2,1)} %bitcast.163, bf16[4,256,2048]{2,1,0:T(8,128)(2,1)} %bitcast.162, f32[8,128]{1,0:T(8,128)} %fusion.23.refs_3_), custom_call_target="tpu_custom_call" | custom-call | bytes 42999808 | tf_op jit(solution)/shard_map/reduce_3/pallas_call | solution.py:1210
  1011.3 2.4 fusion.9
  1013.7 4.0 fusion.12
  (170 shorter events, 41.9 us)
Async XLA Ops:
  3.5 3.7 copy-start.35
  4.3 4.6 copy-start.5
  7.2 188.3 %copy-start.2 = (bf16[256,2048]{1,0:T(8,128)(2,1)}, bf16[256,2048]{1,0:T(8,128)(2,1)S(1)}, u32[]{:S(2)}) copy-start(bf16[256,2048]{1,0:T(8,128)(2,1)S(1)} %multiply_convert_fusion.4.refs_5_.refs_4_) | copy-start | bytes 3145732
  190.5 4.7 copy-start.6
  195.9 6.7 copy-start.1
  202.6 5.9 copy-start.27
  415.2 11.8 %copy-start.36 = (bf16[4,8,64,1408]{3,2,1,0:T(8,128)(2,1)S(1)}, bf16[4,8,64,1408]{3,2,1,0:T(8,128)(2,1)}, u32[]{:S(2)}) copy-start(bf16[4,8,64,1408]{3,2,1,0:T(8,128)(2,1)} %get-tuple-element.49) | copy-start | bytes 17301508
  415.2 11.8 %copy-start.37 = (bf16[4,256,2048]{2,1,0:T(8,128)(2,1)S(1)}, bf16[4,256,2048]{2,1,0:T(8,128)(2,1)}, u32[]{:S(2)}) copy-start(bf16[4,256,2048]{2,1,0:T(8,128)(2,1)} %get-tuple-element.48) | copy-start | bytes 12582916
  415.2 20.2 %slice-start = ((s8[5767168]{0:T(1024)(128)(4,1)}), s8[4194304]{0:T(1024)(128)(4,1)S(1)}, s32[]{:S(2)}) async-start(s8[5767168]{0:T(1024)(128)(4,1)} %bitcast.198), calls=%async_computation | async-start | bytes 8388608
  427.0 8.4 copy-start.9
  427.0 8.4 slice-start.1
  449.0 9.8 copy-start.42
  458.8 11.1 %copy-start.38 = (bf16[4,256,2048]{2,1,0:T(8,128)(2,1)S(1)}, bf16[4,256,2048]{2,1,0:T(8,128)(2,1)}, u32[]{:S(2)}) copy-start(bf16[4,256,2048]{2,1,0:T(8,128)(2,1)} %get-tuple-element.48) | copy-start | bytes 12582916
  469.9 8.8 copy-start.41
  629.2 4.9 copy-start.34
  629.2 4.9 copy-start.39
  634.1 6.3 copy-start.10
  634.1 6.3 copy-start.40
  794.4 10.8 %copy-start.21 = (f32[1024]{0:T(1024)S(1)}, f32[1024]{0:T(1024)}, u32[]{:S(2)}) copy-start(f32[1024]{0:T(1024)} %copy-done.20) | copy-start | bytes 12292
  805.2 21.7 %copy-start.22 = (f32[8,2048]{1,0:T(8,128)S(1)}, f32[8,2048]{1,0:T(8,128)}, u32[]{:S(2)}) copy-start(f32[8,2048]{1,0:T(8,128)} %get-tuple-element.60) | copy-start | bytes 196612
  1007.8 3.5 copy-start.19
  1011.3 6.5 copy-start.13
  1011.3 6.5 copy-start.14
  1011.3 6.5 copy-start.24
  (21 other events, 46.3 us)
